TPU v7x, 256 devices: a whole 4x4x8 slice. The times are simulated.
256 devices in a mesh: narrow: 4 (over x), wide: 64 (over y, z, core).
Axes of the slice: x: 4, y: 4, z: 8, core: 2. Of those that a mesh axis runs over, the one named last changes fastest.
Arguments:
- deflation: bfloat16 [8, 3, 16, 512, 256], P(None, None, 'narrow', 'wide'), may hold values from 0.25 to 1
- residual: float32 [3, 16, 512, 256], P(None, 'narrow', 'wide'), may hold values from -1 to 2
- stiffness: float32 [16, 512, 256], P('narrow', 'wide'), may hold values from 0.25 to 2.5
- mass: float32 [16, 512, 256], P('narrow', 'wide'), may hold values from 1 to 4
- stencil: float32 [27, 3, 3], replicated, may hold values from -0.625 to 0.625
- local_inverse: bfloat16 [12, 12, 12, 320, 256], P(None, None, 'narrow', 'wide'), may hold values from -1.75 to 1.75
- inverse_factor: float32 [2048, 2048], P(('narrow', 'wide')), as said below
- margin_range: int32 [4, 64, 2, 2], P('narrow', 'wide'), may hold values from 0 to 10, as said below
- neighbor_blocks: int32 [4, 64, 9], P('narrow', 'wide'), may hold values from -1 to 255, as said below
Outputs:
- preconditioned: float32 [3, 16, 512, 256], P(None, 'narrow', 'wide')
- coarse_blocks: float32 [4, 64, 9, 8, 8], P('narrow', 'wide')
- coarse_solution: float32 [2048], replicated
Inputs may be any that keep to these rules, and one draw needn't show every extreme that they name: `margin_range`: starts are 0 or 1, stops are 5 or 6 along the first dimension and 9 or 10 along the second. `neighbor_blocks`: entry (i, j, (dx + 1) * 3 + dy + 1) is the coarse block number of subdomain (i + dx, j + dy), or -1 if that lies outside the subdomain grid; the numbers of the subdomains are a permutation of 0 to 4 * 64 - 1. `inverse_factor`: zero above the diagonal.
All inputs are finite; a program needn't handle non-finite values.
Results may differ from a plain program's by a relative error of at most 0.0025.
Values may be sent and summed in bfloat16 or wider, within the bound.
No kernel may reach another device: no remote copies, remote signals or barrier semaphores. Data moves between devices by JAX's collectives and lax.ppermute only.
A program may use at most 128 MiB of HBM per device.

v0:
```python
import jax
import jax.numpy as jnp
from jax import lax
from jax.sharding import PartitionSpec as P


def extended_2(block, sides, width):
    for axis, dim in sides:
        count = lax.axis_size(axis)
        forward = [(i, i + 1) for i in range(count - 1)]
        backward = [(target, source) for source, target in forward]
        low = lax.ppermute(
            lax.slice_in_dim(block, block.shape[dim] - width, None, axis=dim), axis, forward
        )
        high = lax.ppermute(lax.slice_in_dim(block, 0, width, axis=dim), axis, backward)
        block = jnp.concatenate([low, block, high], axis=dim)
    return block


def side_table(shift, cells):
    where_to = jnp.arange(cells) + shift
    classes = jnp.where(where_to < 0, 0, jnp.where(where_to >= cells, 2, 1))
    return (classes[:, None] == jnp.arange(3)[None, :]).astype(jnp.float32)


def coarse_blocks_of(padded, stencil, stiffness, mass):
    vectors, components, ext_x, ext_y, depth = padded.shape
    cells_x = ext_x - 2
    cells_y = ext_y - 2
    deep = jnp.pad(padded, ((0, 0), (0, 0), (0, 0), (0, 0), (1, 1)))
    own = padded[:, :, 1 : cells_x + 1, 1 : cells_y + 1, :].astype(jnp.float32)
    weighted = own * stiffness
    mass_gram = jnp.einsum("acxyz,bcxyz->abxy", own * mass, own, precision=lax.Precision.HIGHEST)
    blocks = jnp.zeros((3, 3, vectors, vectors), jnp.float32)
    for shift_x in (-1, 0, 1):
        for shift_y in (-1, 0, 1):
            products = jnp.zeros((vectors, vectors, cells_x, cells_y), jnp.float32)
            for shift_z in (-1, 0, 1):
                piece = deep[
                    :,
                    :,
                    1 + shift_x : 1 + shift_x + cells_x,
                    1 + shift_y : 1 + shift_y + cells_y,
                    1 + shift_z : 1 + shift_z + depth,
                ]
                offset = ((shift_x + 1) * 3 + shift_y + 1) * 3 + shift_z + 1
                gram = jnp.einsum(
                    "aixyz,bjxyz->aibjxy",
                    weighted,
                    piece.astype(jnp.float32),
                    precision=lax.Precision.HIGHEST,
                )
                products = products + jnp.einsum(
                    "aibjxy,ij->abxy", gram, stencil[offset], precision=lax.Precision.HIGHEST
                )
            if shift_x == 0 and shift_y == 0:
                products = products + mass_gram
            blocks = blocks + jnp.einsum(
                "abxy,xs,yt->stab",
                products,
                side_table(shift_x, cells_x),
                side_table(shift_y, cells_y),
                precision=lax.Precision.HIGHEST,
            )
    return blocks.reshape(9, vectors, vectors)


def margin_mask(extended, ranges):
    along_x = jnp.arange(extended.shape[1])
    along_y = jnp.arange(extended.shape[2])
    keep_x = (along_x >= ranges[0, 0]) & (along_x < ranges[0, 1])
    keep_y = (along_y >= ranges[1, 0]) & (along_y < ranges[1, 1])
    keep = keep_x[:, None] & keep_y[None, :]
    return jnp.where(keep[None, :, :, None], extended, jnp.zeros_like(extended))


def local_solve(inverse, extended):
    components, ext_x, ext_y, depth = extended.shape
    half_x = ext_x // 2
    half_y = ext_y // 2
    grouped = (
        extended.reshape(components, half_x, 2, half_y, 2, depth)
        .transpose(0, 2, 4, 1, 3, 5)
        .reshape(components * 4, half_x, half_y, depth)
    )
    solved = jnp.einsum("ijxyz,jxyz->ixyz", inverse, grouped, preferred_element_type=jnp.float32)
    solved = (
        solved.reshape(components, 2, 2, half_x, half_y, depth)
        .transpose(0, 3, 1, 4, 2, 5)
        .reshape(components, ext_x, ext_y, depth)
    )
    return solved[:, 1 : ext_x - 1, 1 : ext_y - 1, :]


def body(
    deflation,
    residual,
    stiffness,
    mass,
    stencil,
    local_inverse,
    inverse_factor,
    margin_range,
    neighbor_blocks,
):
    vectors = deflation.shape[0]
    rounded = residual.astype(jnp.bfloat16)
    padded_vectors = extended_2(deflation, (("narrow", 2), ("wide", 3)), 1)
    extended = extended_2(rounded, (("narrow", 1), ("wide", 2)), 1)
    blocks = coarse_blocks_of(padded_vectors, stencil, stiffness, mass)
    rhs_own = jnp.einsum("acxyz,cxyz->a", deflation, rounded, preferred_element_type=jnp.float32)
    extended = margin_mask(extended, margin_range[0, 0])
    local = local_solve(local_inverse, extended)
    listing = neighbor_blocks[0, 0]
    own_block = listing[4]
    total = inverse_factor.shape[1] // vectors
    slots = jnp.arange(total, dtype=jnp.int32)
    own_slot = (slots == own_block).astype(jnp.float32)

    def place(values):
        return lax.psum((own_slot[:, None] * values[None, :]).reshape(-1), ("narrow", "wide"))

    def solve(vector):
        inner = jnp.dot(inverse_factor, vector, precision=lax.Precision.HIGHEST)
        share = jnp.dot(inner, inverse_factor, precision=lax.Precision.HIGHEST)
        return lax.psum(share, ("narrow", "wide"))

    coarse_rhs = place(rhs_own)
    first = solve(coarse_rhs)
    picker = (listing[:, None] == slots[None, :]).astype(jnp.float32)
    near = jnp.dot(picker, first.reshape(total, vectors), precision=lax.Precision.HIGHEST)
    image_own = jnp.einsum("nab,nb->a", blocks, near, precision=lax.Precision.HIGHEST)
    coarse_image = place(image_own)
    coarse_solution = first + solve(coarse_rhs - coarse_image)
    weights = jnp.dot(
        own_slot, coarse_solution.reshape(total, vectors), precision=lax.Precision.HIGHEST
    )
    correction = jnp.sum(weights[:, None, None, None, None] * deflation, axis=0, dtype=jnp.float32)
    preconditioned = local + correction
    return (preconditioned, blocks.reshape(1, 1, 9, vectors, vectors), coarse_solution)


def solution(mesh):
    placed = (
        P(None, None, "narrow", "wide", None),
        P(None, "narrow", "wide", None),
        P("narrow", "wide", None),
        P("narrow", "wide", None),
        P(),
        P(None, None, "narrow", "wide", None),
        P(("narrow", "wide"), None),
        P("narrow", "wide", None, None),
        P("narrow", "wide", None),
    )
    return jax.shard_map(
        body,
        mesh=mesh,
        in_specs=placed,
        out_specs=(P(None, "narrow", "wide", None), P("narrow", "wide", None, None, None), P()),
        check_vma=False,
    )
```

profile of v0, /device:TPU:2, one launch (start us, length us, event | category | flops | bytes accessed | tf_op | source)
XLA Modules:
  0.0 579.2 jit_solution(9469179757668019823)
XLA Ops:
  1.7 3.4 collective-permute-start
  5.1 2.4 collective-permute-start.1
  10.8 3.9 collective-permute-start.4
  22.9 77.6 %psum.28 = f32[2048]{0:T(1024)S(1)} all-reduce(f32[2048]{0:T(1024)S(1)} %mul.59), channel_id=1, replica_groups=mesh['narrow'=4,'wide'=64] {'narrow','wide'}, use_global_device_ids=true, to_apply=%region_0.1 | all-reduce | flops 2048 | bytes 16384 | tf_op jit(solution)/shard_map/psum | solution.py:121
  101.1 73.4 %psum.29 = f32[2048]{0:T(1024)S(1)} all-reduce(f32[2048]{0:T(1024)S(1)} %bitcast.503), channel_id=1, replica_groups=mesh['narrow'=4,'wide'=64] {'narrow','wide'}, use_global_device_ids=true, to_apply=%region_1.2 | all-reduce | flops 2048 | bytes 16384 | tf_op jit(solution)/shard_map/psum | solution.py:126
  178.6 2.9 fusion.8
  202.5 2.2 multiply_reduce_fusion
  208.7 6.0 %collective-permute-start.6 = (bf16[8,3,6,1,256]{4,0,3,2,1:T(8,128)(2,1)}, bf16[8,3,6,1,256]{4,0,3,2,1:T(8,128)(2,1)S(1)}, u32[]{:S(2)}, u32[]{:S(2)}) collective-permute-start(bf16[8,3,6,1,256]{4,0,3,2,1:T(8,128)(2,1)} %copy.26), channel_id=1, source_target_pairs={{0,1},{1,2},{2,3},{3,4},{4,5},{5,6},{6,7},{7,8},{8,9},{9,10},{10,1... | collective-permute-start | bytes 221192 | tf_op jit(solution)/shard_map/ppermute | solution.py:12
  214.7 3.6 convolution_bitcast_fusion.22
  218.2 2.8 copy.112
  221.0 4.6 convolution_bitcast_fusion.4
  225.6 3.0 copy.218
  228.7 3.4 fusion.174
  232.1 2.7 fusion.189
  235.4 3.2 convolution_bitcast_fusion.24
  238.6 3.6 convolution_bitcast_fusion.23
  242.2 3.3 convolution_bitcast_fusion.21
  245.5 3.7 convolution_bitcast_fusion.20
  249.2 3.3 convolution_bitcast_fusion.18
  252.5 3.6 convolution_bitcast_fusion.17
  256.1 3.3 convolution_bitcast_fusion.15
  259.4 3.6 convolution_bitcast_fusion.11
  263.0 3.3 convolution_bitcast_fusion.9
  266.3 3.9 convolution_bitcast_fusion.8
  270.1 3.2 convolution_bitcast_fusion.6
  273.3 3.6 convolution_bitcast_fusion.5
  276.9 3.3 convolution_bitcast_fusion.3
  280.2 3.6 convolution_bitcast_fusion.2
  283.8 3.3 convolution_bitcast_fusion
  287.1 4.0 convolution_bitcast_fusion.26
  291.1 2.6 fusion.9
  296.7 2.5 convolution_bitcast_fusion.25
  301.3 3.2 copy.100
  306.6 3.1 copy.117
  311.7 2.6 convolution_bitcast_fusion.19
  316.4 3.3 copy.133
  321.8 2.5 convolution_bitcast_fusion.16
  326.5 2.5 convolution_bitcast_fusion.7
  331.1 3.1 copy.149
  336.3 2.6 convolution_bitcast_fusion.10
  341.0 3.6 convolution_bitcast_fusion.1
  344.5 3.2 copy.233
  360.2 3.1 copy.90
  365.6 2.6 fusion.10
  391.7 2.3 fusion.182
  404.5 2.5 fusion.188
  426.3 76.7 %psum.30 = f32[2048]{0:T(1024)S(1)} all-reduce(f32[2048]{0:T(1024)S(1)} %mul.66), channel_id=1, replica_groups=mesh['narrow'=4,'wide'=64] {'narrow','wide'}, use_global_device_ids=true, to_apply=%region_2.3 | all-reduce | flops 2048 | bytes 16384 | tf_op jit(solution)/shard_map/psum | solution.py:121
  503.5 73.5 %psum.31 = f32[2048]{0:T(1024)S(1)} all-reduce(f32[2048]{0:T(1024)S(1)} %bitcast.504), channel_id=1, replica_groups=mesh['narrow'=4,'wide'=64] {'narrow','wide'}, use_global_device_ids=true, to_apply=%region_3.4 | all-reduce | flops 2048 | bytes 16384 | tf_op jit(solution)/shard_map/psum | solution.py:126
  (328 shorter events, 134.0 us)
Async XLA Ops:
  0.6 99.9 %copy-start = (f32[8,2048]{1,0:T(8,128)S(1)}, f32[8,2048]{1,0:T(8,128)}, u32[]{:S(2)}) copy-start(f32[8,2048]{1,0:T(8,128)} %param.15) | copy-start | bytes 196612
  0.6 19.5 %copy-start.40 = (f32[3,4,8,256]{3,2,1,0:T(8,128)S(1)}, f32[3,4,8,256]{3,2,1,0:T(8,128)}, u32[]{:S(2)}) copy-start(f32[3,4,8,256]{3,2,1,0:T(8,128)} %param.10) | copy-start | bytes 294916
  0.7 21.5 %copy-start.1 = (bf16[8,3,4,8,256]{4,3,2,1,0:T(8,128)(2,1)S(1)}, bf16[8,3,4,8,256]{4,3,2,1,0:T(8,128)(2,1)}, u32[]{:S(2)}) copy-start(bf16[8,3,4,8,256]{4,3,2,1,0:T(8,128)(2,1)} %param.9) | copy-start | bytes 1179652
  0.7 19.5 %copy-start.84 = (s32[1,1,9]{2,1,0:T(1,128)S(1)}, s32[1,1,9]{2,1,0:T(1,128)}, u32[]{:S(2)}) copy-start(s32[1,1,9]{2,1,0:T(1,128)} %param.17) | copy-start | bytes 112
  0.7 20.7 %copy-start.80 = (s32[1,1,2,2]{3,2,1,0:T(2,128)S(1)}, s32[1,1,2,2]{3,2,1,0:T(2,128)}, u32[]{:S(2)}) copy-start(s32[1,1,2,2]{3,2,1,0:T(2,128)} %param.16) | copy-start | bytes 52
  1.7 180.4 %collective-permute-start = (bf16[3,1,8,256]{3,2,1,0:T(8,128)(2,1)S(1)}, bf16[3,1,8,256]{3,2,1,0:T(8,128)(2,1)S(1)}, u32[]{:S(2)}, u32[]{:S(2)}) collective-permute-start(bf16[3,1,8,256]{3,2,1,0:T(8,128)(2,1)S(1)} %get-tuple-element.41), channel_id=1, source_target_pairs={{0,64},{64,128},{128,192},{1,65},{65,129},{129,193},{2,66},{66,130... | collective-permute-start | bytes 36872 | tf_op jit(solution)/shard_map/ppermute | solution.py:12
  5.1 172.3 %copy-start.45 = (f32[4,8,256]{2,1,0:T(8,128)S(1)}, f32[4,8,256]{2,1,0:T(8,128)}, u32[]{:S(2)}) copy-start(f32[4,8,256]{2,1,0:T(8,128)} %param.12) | copy-start | bytes 98308
  5.1 172.3 %copy-start.46 = (f32[4,8,256]{2,1,0:T(8,128)S(1)}, f32[4,8,256]{2,1,0:T(8,128)}, u32[]{:S(2)}) copy-start(f32[4,8,256]{2,1,0:T(8,128)} %param.11) | copy-start | bytes 98308
  5.1 177.0 %collective-permute-start.1 = (bf16[3,1,8,256]{3,2,1,0:T(8,128)(2,1)S(1)}, bf16[3,1,8,256]{3,2,1,0:T(8,128)(2,1)S(1)}, u32[]{:S(2)}, u32[]{:S(2)}) collective-permute-start(bf16[3,1,8,256]{3,2,1,0:T(8,128)(2,1)S(1)} %get-tuple-element.42), channel_id=1, source_target_pairs={{64,0},{128,64},{192,128},{65,1},{129,65},{193,129},{66,2},{130,66... | collective-permute-start | bytes 36872 | tf_op jit(solution)/shard_map/ppermute | solution.py:15
  8.8 205.9 %copy-start.24 = (bf16[8,3,4,8,256]{4,0,1,3,2:T(8,128)(2,1)}, bf16[8,3,4,8,256]{4,0,1,3,2:T(8,128)(2,1)S(1)}, u32[]{:S(2)}) copy-start(bf16[8,3,4,8,256]{4,0,1,3,2:T(8,128)(2,1)S(1)} %copy.23) | copy-start | bytes 1179652
  8.8 197.2 %collective-permute-start.5 = (bf16[8,3,1,8,256]{4,0,1,3,2:T(8,128)(2,1)S(1)}, bf16[8,3,1,8,256]{4,0,1,3,2:T(8,128)(2,1)S(1)}, u32[]{:S(2)}, u32[]{:S(2)}) collective-permute-start(bf16[8,3,1,8,256]{4,0,1,3,2:T(8,128)(2,1)S(1)} %get-tuple-element.37), channel_id=1, source_target_pairs={{64,0},{128,64},{192,128},{65,1},{129,65},{193,129},{66,2},{130,66... | collective-permute-start | bytes 294920 | tf_op jit(solution)/shard_map/ppermute | solution.py:15
  10.8 195.1 %collective-permute-start.4 = (bf16[8,3,1,8,256]{4,0,1,3,2:T(8,128)(2,1)S(1)}, bf16[8,3,1,8,256]{4,0,1,3,2:T(8,128)(2,1)S(1)}, u32[]{:S(2)}, u32[]{:S(2)}) collective-permute-start(bf16[8,3,1,8,256]{4,0,1,3,2:T(8,128)(2,1)S(1)} %get-tuple-element.38), channel_id=1, source_target_pairs={{0,64},{64,128},{128,192},{1,65},{65,129},{129,193},{2,66},{66,130... | collective-permute-start | bytes 294920 | tf_op jit(solution)/shard_map/ppermute | solution.py:12
  21.4 157.2 %copy-start.78 = (f32[256]{0:T(256)}, f32[256]{0:T(256)S(1)}, u32[]{:S(2)}) copy-start(f32[256]{0:T(256)S(1)} %fusion.118) | copy-start | bytes 3076
  174.4 7.1 %copy-start.41 = (f32[2048]{0:T(1024)}, f32[2048]{0:T(1024)S(1)}, u32[]{:S(2)}) copy-start(f32[2048]{0:T(1024)S(1)} %psum.29) | copy-start | bytes 24580
  182.1 19.8 %collective-permute-start.2 = (bf16[3,6,1,256]{3,2,1,0:T(2,128)(2,1)S(1)}, bf16[3,6,1,256]{3,2,1,0:T(2,128)(2,1)S(1)}, u32[]{:S(2)}, u32[]{:S(2)}) collective-permute-start(bf16[3,6,1,256]{3,2,1,0:T(2,128)(2,1)S(1)} %get-tuple-element.39), channel_id=1, source_target_pairs={{0,1},{1,2},{2,3},{3,4},{4,5},{5,6},{6,7},{7,8},{8,9},{9,10},{10,1... | collective-permute-start | bytes 27656 | tf_op jit(solution)/shard_map/ppermute | solution.py:12
  183.8 18.1 %collective-permute-start.3 = (bf16[3,6,1,256]{3,2,1,0:T(2,128)(2,1)S(1)}, bf16[3,6,1,256]{3,2,1,0:T(2,128)(2,1)S(1)}, u32[]{:S(2)}, u32[]{:S(2)}) collective-permute-start(bf16[3,6,1,256]{3,2,1,0:T(2,128)(2,1)S(1)} %get-tuple-element.40), channel_id=1, source_target_pairs={{1,0},{2,1},{3,2},{4,3},{5,4},{6,5},{7,6},{8,7},{9,8},{10,9},{11,1... | collective-permute-start | bytes 27656 | tf_op jit(solution)/shard_map/ppermute | solution.py:15
  206.1 8.6 %copy-start.39 = (bf16[8,3,1,8,256]{4,0,1,3,2:T(8,128)(2,1)}, bf16[8,3,1,8,256]{4,0,1,3,2:T(8,128)(2,1)S(1)}, u32[]{:S(2)}) copy-start(bf16[8,3,1,8,256]{4,0,1,3,2:T(8,128)(2,1)S(1)} %collective-permute-done.5) | copy-start | bytes 294916
  207.4 27.4 %collective-permute-start.7 = (bf16[8,3,6,1,256]{4,0,3,2,1:T(8,128)(2,1)}, bf16[8,3,6,1,256]{4,0,3,2,1:T(8,128)(2,1)S(1)}, u32[]{:S(2)}, u32[]{:S(2)}) collective-permute-start(bf16[8,3,6,1,256]{4,0,3,2,1:T(8,128)(2,1)} %copy.27), channel_id=1, source_target_pairs={{1,0},{2,1},{3,2},{4,3},{5,4},{6,5},{7,6},{8,7},{9,8},{10,9},{11,1... | collective-permute-start | bytes 221192 | tf_op jit(solution)/shard_map/ppermute | solution.py:15
  208.7 26.2 %collective-permute-start.6 = (bf16[8,3,6,1,256]{4,0,3,2,1:T(8,128)(2,1)}, bf16[8,3,6,1,256]{4,0,3,2,1:T(8,128)(2,1)S(1)}, u32[]{:S(2)}, u32[]{:S(2)}) collective-permute-start(bf16[8,3,6,1,256]{4,0,3,2,1:T(8,128)(2,1)} %copy.26), channel_id=1, source_target_pairs={{0,1},{1,2},{2,3},{3,4},{4,5},{5,6},{6,7},{7,8},{8,9},{9,10},{10,1... | collective-permute-start | bytes 221192 | tf_op jit(solution)/shard_map/ppermute | solution.py:12
  287.1 6.6 %copy-start.81 = (f32[1,3,3]{1,2,0:T(4,128)S(1)}, f32[1,3,3]{1,2,0:T(4,128)}, u32[]{:S(2)}) copy-start(f32[1,3,3]{1,2,0:T(4,128)} %copy.311) | copy-start | bytes 112
  363.4 4.8 copy-start.75
  365.6 4.9 copy-start.21
  365.6 4.9 copy-start.61
  376.8 4.4 copy-start.13
  376.8 4.4 copy-start.66
  378.9 4.4 copy-start.9
  378.9 4.4 copy-start.65
  389.6 4.4 copy-start.7
  389.6 4.4 copy-start.58
  391.7 4.4 copy-start.18
  391.7 4.4 copy-start.53
  402.4 4.6 copy-start.4
  402.4 4.6 copy-start.52
  404.5 4.6 copy-start.3
  404.5 4.6 copy-start.51
  407.0 4.2 copy-start.2
  409.1 5.2 copy-start.73
  409.1 5.4 copy-start.38
  411.2 4.4 copy-start.76
  411.2 6.6 %copy-start.72 = (s32[4]{0:T(128)S(1)}, s32[4]{0:T(128)}, u32[]{:S(2)}) copy-start(s32[4]{0:T(128)} %compare_select_fusion.2) | copy-start | bytes 52
  414.3 6.1 %copy-start.37 = (f32[1,8,8,4,8,1]{4,0,5,3,2,1:T(1,128)S(1)}, f32[1,8,8,4,8,1]{4,0,5,3,2,1:T(1,128)}, u32[]{:S(2)}) copy-start(f32[1,8,8,4,8,1]{4,0,5,3,2,1:T(1,128)} %fusion.189) | copy-start | bytes 24580
  415.5 6.0 %copy-start.74 = (s32[4]{0:T(128)S(1)}, s32[4]{0:T(128)}, u32[]{:S(2)}) copy-start(s32[4]{0:T(128)} %compare_select_fusion.1) | copy-start | bytes 52
  415.7 6.2 %copy-start.49 = (f32[3,3,1,1,1,1]{1,2,0,5,4,3:T(1,128)S(1)}, f32[3,3,1,1,1,1]{1,2,0,5,4,3:T(1,128)}, u32[]{:S(2)}) copy-start(f32[3,3,1,1,1,1]{1,2,0,5,4,3:T(1,128)} %reshape.326) | copy-start | bytes 112
  420.3 5.5 copy-start.48
  420.3 5.7 copy-start.79
  421.5 81.5 %copy-start.44 = (f32[2048]{0:T(1024)S(1)}, f32[2048]{0:T(1024)}, u32[]{:S(2)}) copy-start(f32[2048]{0:T(1024)} %copy-done.43) | copy-start | bytes 24580
  421.7 155.2 %copy-start.42 = (f32[2048]{0:T(1024)S(1)}, f32[2048]{0:T(1024)}, u32[]{:S(2)}) copy-start(f32[2048]{0:T(1024)} %copy-done.41) | copy-start | bytes 24580
  421.9 155.2 %copy-start.83 = (pred[256,1]{0,1:T(4,128)(4,1)S(1)}, pred[256,1]{0,1:T(4,128)(4,1)}, u32[]{:S(2)}) copy-start(pred[256,1]{0,1:T(4,128)(4,1)} %reshape.275) | copy-start | bytes 772
  (45 other events, 159.5 us)
where the time goes:
time: 588 us; the launch traced here: 579 us
  blocking collectives  301 us (51%)
  matrix products  154 us (26%)
  local copies, waits for them, and re-layouts  85 us (14%)
  starting transfers between devices  22 us (4%)
  other arithmetic  14.3 us (2%)
    psum x2, blocking collectives, place(): lax.psum((own_slot[:, None] * values[None, :]).reshape(-1), ('narrow', 'w...  154 us
    psum x2, blocking collectives, solve(): return lax.psum(share, ('narrow', 'wide'))  147 us
    dot_general x27, matrix products, coarse_blocks_of(): jnp.einsum('aixyz,bjxyz->aibjxy', weighted, piece.astype(jnp.float32), pr...  87.9 us
    transpose x24, local copies, waits for them, and re-layouts, coarse_blocks_of(): jnp.einsum('aixyz,bjxyz->aibjxy', weighted, piece.astype(jnp.float32), pr...  58.2 us
    dot_general x24, matrix products, coarse_blocks_of(): jnp.einsum('aibjxy,ij->abxy', gram, stencil[offset], precision=lax.Precis...  52.1 us
    ppermute x4, starting transfers between devices, extended_2(): lax.ppermute(lax.slice_in_dim(block, block.shape[dim] - width, None, axis...  15 us
    squeeze x24, local copies, waits for them, and re-layouts, coarse_blocks_of(): stencil[offset]  13.5 us
  transfers between devices with their start and end apart: 8, of which 0 were waited for; matrix products, arithmetic and copies ran while one was open for 10% of the time, Pallas kernels for 0%

commit v1 on v0

v1 whole, which is shorter than its diff:
```python
import functools

import jax
import jax.numpy as jnp
from jax import lax
from jax.experimental import pallas as pl
from jax.experimental.pallas import tpu as pltpu
from jax.sharding import PartitionSpec as P

F32 = jnp.float32
AXES = ("narrow", "wide")
SLOT = 80
VMEM = pl.BlockSpec(memory_space=pltpu.VMEM)
SMEM = pl.BlockSpec(memory_space=pltpu.SMEM)


def shifted(value, offset, axis):
    if offset == 0:
        return value
    size = value.shape[axis]
    rolled = pltpu.roll(value, (-offset) % size, axis)
    at = lax.broadcasted_iota(jnp.int32, value.shape, axis)
    keep = at < size - offset if offset > 0 else at >= -offset
    return jnp.where(keep, rolled, 0.0)


def rows_sum(value):
    return jnp.sum(value[:, :128] + value[:, 128:], axis=0, keepdims=True)


def entry(s_ref, ox, oy, oz, i, j):
    return s_ref[((((ox + 1) * 3 + oy + 1) * 3 + oz + 1) * 3 + i) * 3 + j]


def centre_kernel(s_ref, z_ref, r_ref, stiff_ref, mass_ref, out_ref, rhs_ref, zf_ref):
    vectors, _, cells_x = z_ref.shape[:3]

    def convert(a, carry):
        for i in range(3):
            for x in range(cells_x):
                zf_ref[a, i, x] = z_ref[a, i, x].astype(F32)
        return carry

    lax.fori_loop(0, vectors, convert, 0)
    for a in range(vectors):
        total = None
        for i in range(3):
            for x in range(cells_x):
                term = zf_ref[a, i, x] * r_ref[i, x].astype(F32)
                total = term if total is None else total + term
        rhs_ref[a : a + 1, :] = rows_sum(total)

    def one(b, carry):
        field = [[zf_ref[b, j, x] for x in range(cells_x)] for j in range(3)]
        weighted = []
        for i in range(3):
            image = [None] * cells_x
            for oz in (-1, 0, 1):
                level = [None] * cells_x
                for oy in (-1, 0, 1):
                    for x in range(cells_x):
                        acc = None
                        for ox in (-1, 0, 1):
                            if 0 <= x + ox < cells_x:
                                for j in range(3):
                                    term = entry(s_ref, ox, oy, oz, i, j) * field[j][x + ox]
                                    acc = term if acc is None else acc + term
                        acc = shifted(acc, oy, 0)
                        level[x] = acc if level[x] is None else level[x] + acc
                for x in range(cells_x):
                    moved = shifted(level[x], oz, 1)
                    image[x] = moved if image[x] is None else image[x] + moved
            weighted.append([stiff_ref[x] * image[x] + mass_ref[x] * field[i][x] for x in range(cells_x)])
        for a in range(vectors):
            total = None
            for i in range(3):
                for x in range(cells_x):
                    term = zf_ref[a, i, x] * weighted[i][x]
                    total = term if total is None else total + term
            out_ref[b, a : a + 1, :] = rows_sum(total)
        return carry

    lax.fori_loop(0, vectors, one, 0)


def edge_kernel(
    s_ref, ids_ref, z_ref, stiff_ref, xlo_ref, xhi_ref, ylo_ref, yhi_ref, centre_ref, rhs_ref,
    blocks_ref, pay_ref, r_ref, zx_ref, zy_ref, sy_ref,
):
    vectors, _, cells_x, cells_y, depth = z_ref.shape
    own_x = (0, cells_x - 1)
    own_y = (0, cells_y - 1)
    blank = jnp.zeros((8 - cells_x, depth), F32)

    def columns(rows):
        return jnp.concatenate(rows + [blank], axis=0)

    def prepare(a, carry):
        for i in range(3):
            cells = [z_ref[a, i, x].astype(F32) for x in range(cells_x)]
            for face in range(2):
                zx_ref[face, a, i] = cells[own_x[face]]
                y = own_y[face]
                zy_ref[face, a, i] = columns([cell[y : y + 1, :] for cell in cells])
        return carry

    lax.fori_loop(0, vectors, prepare, 0)
    for face in range(2):
        y = own_y[face]
        sy_ref[face] = columns([stiff_ref[x, y : y + 1, :] for x in range(cells_x)])

    row = lax.broadcasted_iota(jnp.int32, (8, depth), 0)

    def one(b, carry):
        for face, halo_ref in ((0, xlo_ref), (1, xhi_ref)):
            ox = 2 * face - 1
            field = [halo_ref[b * 3 + j].astype(F32) for j in range(3)]
            stiff = stiff_ref[own_x[face]]
            weighted = []
            for i in range(3):
                image = None
                for oz in (-1, 0, 1):
                    level = None
                    for oy in (-1, 0, 1):
                        acc = sum(entry(s_ref, ox, oy, oz, i, j) * field[j] for j in range(3))
                        acc = shifted(acc, oy, 0)
                        level = acc if level is None else level + acc
                    moved = shifted(level, oz, 1)
                    image = moved if image is None else image + moved
                weighted.append(stiff * image)
            number = 1 if face == 0 else 7
            for a in range(vectors):
                total = sum(zx_ref[face, a, i] * weighted[i] for i in range(3))
                r_ref[number * vectors + b, a : a + 1, :] = rows_sum(total)
        for face, halo_ref in ((0, ylo_ref), (1, yhi_ref)):
            oy = 2 * face - 1
            pad = jnp.zeros((8 - halo_ref.shape[1], depth), F32)
            field = [jnp.concatenate([halo_ref[b * 3 + j].astype(F32), pad], axis=0) for j in range(3)]
            stiff = sy_ref[face]
            inner, outer = [], []
            for i in range(3):
                mid, rim = None, None
                for ox in (-1, 0, 1):
                    line = None
                    for oz in (-1, 0, 1):
                        acc = sum(entry(s_ref, ox, oy, oz, i, j) * field[j] for j in range(3))
                        acc = shifted(acc, oz, 1)
                        line = acc if line is None else line + acc
                    moved = pltpu.roll(line, (-(1 + ox)) % 8, 0) if ox != -1 else line
                    low, high = max(0, -ox), min(cells_x, cells_x - ox)
                    part = jnp.where((row >= low) & (row < high), moved, 0.0)
                    mid = part if mid is None else mid + part
                    if ox != 0:
                        edge = jnp.where(row == (0 if ox == -1 else cells_x - 1), moved, 0.0)
                        rim = edge if rim is None else rim + edge
                inner.append(stiff * mid)
                outer.append(stiff * rim)
            for a in range(vectors):
                own = [zy_ref[face, a, i] for i in range(3)]
                total = sum(own[i] * inner[i] for i in range(3))
                r_ref[(3 + 2 * face) * vectors + b, a : a + 1, :] = rows_sum(total)
                total = sum(own[i] * outer[i] for i in range(3))
                half = total[:, :128] + total[:, 128:]
                r_ref[(0 + 2 * face) * vectors + b, a : a + 1, :] = half[0:1, :]
                r_ref[(6 + 2 * face) * vectors + b, a : a + 1, :] = half[cells_x - 1 : cells_x, :]
        return carry

    lax.fori_loop(0, vectors, one, 0)
    lane = lax.broadcasted_iota(jnp.int32, (8, 128), 1)
    table = jnp.zeros((8, 128), F32)
    for k in range(9 * vectors):
        piece = centre_ref[k % vectors] if k // vectors == 4 else r_ref[k]
        table = jnp.where(lane == k, jnp.sum(piece, axis=1, keepdims=True), table)
    blocks_ref[...] = table
    table = jnp.where(lane == 72, jnp.sum(rhs_ref[...], axis=1, keepdims=True), table)
    table = jnp.where(lane == 73, ids_ref[4].astype(F32), table)
    width = pay_ref.shape[1]
    wide = jnp.concatenate([table, jnp.zeros((8, width - 128), F32)], axis=1)
    line = jnp.zeros((1, width), F32)
    for a in range(vectors):
        piece = wide[a : a + 1, :]
        line = line + (pltpu.roll(piece, a * SLOT, 1) if a else piece)
    pay_ref[...] = jnp.broadcast_to(line, pay_ref.shape)


def local_kernel(range_ref, inverse_ref, r_ref, xlo_ref, xhi_ref, ylo_ref, yhi_ref, out_ref, ext_ref, sol_ref):
    cells_x, cells_y = r_ref.shape[1:3]
    ext_x, ext_y = cells_x + 2, cells_y + 2
    half_x, half_y = ext_x // 2, ext_y // 2
    first = xlo_ref.shape[0] - 3
    halves = ((0, slice(0, 128)), (1, slice(128, 256)))
    for c in range(3):
        for e in range(ext_x):
            if e == 0:
                middle = xlo_ref[first + c]
            elif e == ext_x - 1:
                middle = xhi_ref[first + c]
            else:
                middle = r_ref[c, e - 1]
            middle = middle.astype(F32)
            low = ylo_ref[first + c].astype(F32)[e : e + 1, :]
            high = yhi_ref[first + c].astype(F32)[e : e + 1, :]
            for h, lanes in halves:
                ext_ref[c, e, h, 1 : cells_y + 1, :] = middle[:, lanes]
                ext_ref[c, e, h, 0:1, :] = low[:, lanes]
                ext_ref[c, e, h, cells_y + 1 : ext_y, :] = high[:, lanes]
    at = lax.broadcasted_iota(jnp.int32, (half_y, r_ref.shape[3]), 0)
    for u in range(half_x):
        fields = []
        for m in range(12):
            c, s, t = m // 4, m // 2 % 2, m % 2
            e, f = 2 * u + s, 2 * at + t
            keep = (f >= range_ref[2]) & (f < range_ref[3]) & (e >= range_ref[0]) & (e < range_ref[1])
            value = jnp.concatenate([ext_ref[c, e, h, pl.ds(t, half_y, stride=2), :] for h, _ in halves], axis=1)
            fields.append(jnp.where(keep, value, 0.0))
        for i in range(12):
            acc = None
            for m in range(12):
                term = inverse_ref[i, m, u].astype(F32) * fields[m]
                acc = term if acc is None else acc + term
            c, s, t = i // 4, i // 2 % 2, i % 2
            for h, lanes in halves:
                sol_ref[c, 2 * u + s, h, pl.ds(t, half_y, stride=2), :] = acc[:, lanes]
    for c in range(3):
        for x in range(cells_x):
            for h, lanes in halves:
                out_ref[c, x, :, lanes] = sol_ref[c, x + 1, h, 1 : cells_y + 1, :]


def dotted(left, right, dims):
    return lax.dot_general(
        left, right, (dims, ((), ())), precision=lax.Precision.HIGHEST, preferred_element_type=F32
    )


def slots_of(packed_ref):
    count = packed_ref.shape[1]
    ids = packed_ref[73:74, :].astype(jnp.int32)
    return (lax.broadcasted_iota(jnp.int32, (count, count), 0) == ids).astype(F32)


def share_of(vector, pieces):
    line = jnp.concatenate([vector[b : b + 1, :] for b in range(8)], axis=1)
    line = jnp.broadcast_to(line, (8, line.shape[1]))
    acc = jnp.zeros(line.shape, F32)
    for piece in pieces:
        count = piece.shape[0] // 8
        group = 4 if count % 4 == 0 else 1

        def step(t, acc, piece=piece, group=group):
            tiles, inner = [], []
            for q in range(group):
                tile = piece[pl.ds(pl.multiple_of((t * group + q) * 8, 8), 8), :]
                tiles.append(tile)
                inner.append(jnp.sum(tile * line, axis=1, keepdims=True))
            for tile, value in zip(tiles, inner):
                acc = acc + tile * value
            return acc

        acc = lax.fori_loop(0, count // group, step, acc)
    total = jnp.sum(acc, axis=0, keepdims=True)
    blocks = vector.shape[1]
    return jnp.concatenate([total[:, b * blocks : (b + 1) * blocks] for b in range(8)], axis=0)


def first_kernel(got_ref, *refs):
    pieces, (packed_ref, rhs_ref, share_ref) = refs[:-3], refs[-3:]
    packed_ref[...] = got_ref[...].T
    own = jnp.concatenate([packed_ref[a * SLOT + 72 : a * SLOT + 73, :] for a in range(8)], axis=0)
    rhs = dotted(own, slots_of(packed_ref), ((1,), (1,)))
    rhs_ref[...] = rhs
    share_ref[...] = share_of(rhs, pieces)


def second_kernel(n_wide, packed_ref, rhs_ref, part_ref, got1_ref, got2_ref, got3_ref, *refs):
    pieces, (first_ref, share_ref) = refs[:-2], refs[-2:]
    first = (part_ref[...] + got1_ref[...]) + (got2_ref[...] + got3_ref[...])
    first_ref[...] = first
    slots = slots_of(packed_ref)
    there = dotted(first, slots, ((1,), (0,)))
    count = there.shape[1]
    n_narrow = count // n_wide
    at = lax.broadcasted_iota(jnp.int32, there.shape, 1)
    row, column = at // n_wide, at % n_wide
    near = []
    for dx in (-1, 0, 1):
        for dy in (-1, 0, 1):
            move = (-(dx * n_wide + dy)) % count
            value = pltpu.roll(there, move, 1) if move else there
            keep = (row + dx >= 0) & (row + dx < n_narrow) & (column + dy >= 0) & (column + dy < n_wide)
            near.append(jnp.where(keep, value, 0.0))
    near.append(jnp.zeros_like(there))
    near = jnp.concatenate(near, axis=0)
    image = jnp.concatenate(
        [jnp.sum(packed_ref[a * SLOT : (a + 1) * SLOT, :] * near, axis=0, keepdims=True) for a in range(8)], axis=0
    )
    vector = rhs_ref[...] - dotted(image, slots, ((1,), (1,)))
    share_ref[...] = share_of(vector, pieces)


def last_kernel(ids_ref, z_ref, local_ref, first_ref, part_ref, got1_ref, got2_ref, got3_ref, out_ref, sol_ref):
    solution = first_ref[...] + ((part_ref[...] + got1_ref[...]) + (got2_ref[...] + got3_ref[...]))
    sol_ref[...] = solution
    at = lax.broadcasted_iota(jnp.int32, solution.shape, 1)
    weights = jnp.sum(jnp.where(at == ids_ref[4], solution, 0.0), axis=1, keepdims=True)
    for x in range(z_ref.shape[2]):
        for i in range(3):
            acc = local_ref[i, x]
            for a in range(8):
                acc = acc + weights[a : a + 1, :] * z_ref[a, i, x].astype(F32)
            out_ref[i, x] = acc


def call(kernel, out_shape, in_specs, scratch=(), flops=0, moved=0, name=None):
    return pl.pallas_call(
        kernel,
        out_shape=[jax.ShapeDtypeStruct(shape, F32) for shape in out_shape],
        in_specs=in_specs,
        out_specs=[VMEM] * len(out_shape),
        scratch_shapes=list(scratch),
        compiler_params=pltpu.CompilerParams(vmem_limit_bytes=40 * 2**20),
        cost_estimate=pl.CostEstimate(flops=flops, bytes_accessed=moved, transcendentals=0),
        name=name,
    )


def body(
    deflation,
    residual,
    stiffness,
    mass,
    stencil,
    local_inverse,
    inverse_factor,
    margin_range,
    neighbor_blocks,
):
    vectors, _, cells_x, cells_y, depth = deflation.shape
    n_narrow, n_wide = lax.axis_size("narrow"), lax.axis_size("wide")
    count = n_narrow * n_wide
    size_z, size_c = 8, 2
    size_y = n_wide // (size_z * size_c)

    def wide_perm(step_y, step_z, step_c):
        pairs = []
        for y in range(size_y):
            for z in range(size_z):
                for c in range(size_c):
                    to = ((y + step_y) % size_y * size_z + (z + step_z) % size_z) * size_c + (c + step_c) % size_c
                    pairs.append(((y * size_z + z) * size_c + c, to))
        return pairs

    rounded = residual.astype(jnp.bfloat16)
    flat_stencil = stencil.reshape(-1)
    ids = neighbor_blocks.reshape(-1)
    ranges = margin_range.reshape(-1)

    def ends(axis):
        size = lax.axis_size(axis)
        up = [(k, k + 1) for k in range(size - 1)]
        return up, [(b, a) for a, b in up]

    up, down = ends("narrow")
    fields = jnp.concatenate([deflation.reshape(3 * vectors, cells_x, cells_y, depth), rounded], axis=0)
    xlo = lax.ppermute(fields[:, cells_x - 1], "narrow", up)
    xhi = lax.ppermute(fields[:, 0], "narrow", down)
    up, down = ends("wide")

    def side(y):
        return jnp.concatenate([xlo[:, y : y + 1], fields[:, :, y], xhi[:, y : y + 1]], axis=1)

    ylo = lax.ppermute(side(cells_y - 1), "wide", up)
    yhi = lax.ppermute(side(0), "wide", down)

    rows = inverse_factor.shape[0]
    own = inverse_factor.reshape(rows, count, vectors).transpose(0, 2, 1).reshape(rows, count * vectors)
    left = lax.ppermute(own, "wide", wide_perm(0, 1, 0))
    right = lax.ppermute(own, "wide", wide_perm(0, -1, 0))
    three = jnp.concatenate([own, left, right], axis=0)
    far_left = lax.ppermute(three, "wide", wide_perm(0, 3, 0))
    far_right = lax.ppermute(three[: 2 * rows], "wide", wide_perm(0, -3, 0))
    line = jnp.concatenate([three, far_left, far_right], axis=0)
    pieces = [line] + [lax.ppermute(line, "wide", wide_perm(step, 0, 0)) for step in range(1, size_y)]

    centre, rhs_rows = call(
        centre_kernel,
        [(vectors, vectors, 128), (vectors, 128)],
        [SMEM] + [VMEM] * 4,
        [pltpu.VMEM((vectors, 3, cells_x, cells_y, depth), F32)],
        flops=40_000_000,
        moved=1_000_000,
        name="centre",
    )(flat_stencil, deflation, rounded, stiffness, mass)
    table, payload = call(
        edge_kernel,
        [(8, 128), (count, SLOT * vectors)],
        [SMEM, SMEM] + [VMEM] * 8,
        [
            pltpu.VMEM((9 * vectors, 8, 128), F32),
            pltpu.VMEM((2, vectors, 3, 8, depth), F32),
            pltpu.VMEM((2, vectors, 3, 8, depth), F32),
            pltpu.VMEM((2, 8, depth), F32),
        ],
        flops=10_000_000,
        moved=2_000_000,
        name="edges",
    )(flat_stencil, ids, deflation, stiffness, xlo, xhi, ylo, yhi, centre, rhs_rows)
    got = lax.all_to_all(payload, AXES, 0, 0, tiled=True)
    (local,) = call(
        local_kernel,
        [(3, cells_x, cells_y, depth)],
        [SMEM] + [VMEM] * 6,
        [pltpu.VMEM((3, cells_x + 2, 2, 16, depth // 2), F32)] * 2,
        flops=2_000_000,
        moved=3_000_000,
        name="local",
    )(ranges, local_inverse, rounded, xlo, xhi, ylo, yhi)

    def spread(share):
        part = share + lax.ppermute(share, "wide", wide_perm(0, 0, 1))
        moves = [
            lax.ppermute(part, "narrow", [(k, (k + step) % n_narrow) for k in range(n_narrow)])
            for step in range(1, n_narrow)
        ]
        return [part] + moves

    packed, rhs, share = call(
        first_kernel,
        [(SLOT * vectors, count), (vectors, count), (vectors, count)],
        [VMEM] * (1 + len(pieces)),
        flops=4_000_000,
        moved=3_000_000,
        name="first",
    )(got, *pieces)
    first, share = call(
        functools.partial(second_kernel, n_wide),
        [(vectors, count), (vectors, count)],
        [VMEM] * (6 + len(pieces)),
        flops=4_000_000,
        moved=3_000_000,
        name="second",
    )(packed, rhs, *spread(share), *pieces)
    preconditioned, solved = call(
        last_kernel,
        [(3, cells_x, cells_y, depth), (vectors, count)],
        [SMEM] + [VMEM] * 7,
        flops=1_000_000,
        moved=1_000_000,
        name="last",
    )(ids, deflation, local, first, *spread(share))
    coarse_solution = solved.T.reshape(-1)
    blocks = table[:, : 9 * vectors].reshape(vectors, 9, vectors).transpose(1, 0, 2)
    return preconditioned, blocks.reshape(1, 1, 9, vectors, vectors), coarse_solution


def solution(mesh):
    placed = (
        P(None, None, "narrow", "wide", None),
        P(None, "narrow", "wide", None),
        P("narrow", "wide", None),
        P("narrow", "wide", None),
        P(),
        P(None, None, "narrow", "wide", None),
        P(("narrow", "wide"), None),
        P("narrow", "wide", None, None),
        P("narrow", "wide", None),
    )
    return jax.shard_map(
        body,
        mesh=mesh,
        in_specs=placed,
        out_specs=(P(None, "narrow", "wide", None), P("narrow", "wide", None, None, None), P()),
        check_vma=False,
    )
```

time: 588 us -> 112 us (0.19); the launches traced: 579 us -> 112 us
  blocking collectives: 301 us -> 0 us
  matrix products: 154 us -> 0 us
  local copies, waits for them, and re-layouts: 85 us -> 8.53 us
  starting transfers between devices: 22 us -> 55.9 us
  waiting for transfers between devices: 0.02 us -> 31 us
  Pallas kernels: 0 us -> 14.8 us
  other arithmetic: 14.3 us -> 0.39 us
    psum x4 -> x0, blocking collectives: 301 us -> none  [the longest x2 154 us: place(): lax.psum((own_slot[:, None] * values[None, :]).reshape(-1), ('narrow', 'w...]
    dot_general x78 -> x0, matrix products: 154 us -> none  [the longest x27 87.9 us: coarse_blocks_of(): jnp.einsum('aixyz,bjxyz->aibjxy', weighted, piece.astype(jnp.float32), pr...]
    transpose x25 -> x2, local copies, waits for them, and re-layouts: 58.3 us -> 0.41 us  [the longest x1 0.29 us: body(): inverse_factor.reshape(rows, count, vectors).transpose(0, 2, 1)]
    all_to_all x0 -> x1, starting transfers between devices: none -> 17.1 us  [body(): got = lax.all_to_all(payload, AXES, 0, 0, tiled=True)]
    ppermute x8 -> x19, starting transfers between devices: 22 us -> 38.8 us  [the longest x6 10.3 us: spread(): lax.ppermute(part, 'narrow', [(k, (k + step) % n_narrow) for k in range(n...]
    all_to_all x0 -> x1, waiting for transfers between devices: none -> 16.2 us  [body(): got = lax.all_to_all(payload, AXES, 0, 0, tiled=True)]
    pallas_call x0 -> x6, Pallas kernels: none -> 14.8 us  [the longest x1 5.39 us: body(): call(centre_kernel, [(vectors, vectors, 128), (vectors, 128)], [SMEM] + [...]
    ppermute x8 -> x19, waiting for transfers between devices: 0.02 us -> 14.8 us  [the longest x3 10.4 us: body(): lax.ppermute(line, 'wide', wide_perm(step, 0, 0))]
  transfers between devices with their start and end apart: 8 -> 20, of which waited for: 0 -> 6; matrix products, arithmetic and copies ran while one was open for 10% -> 6% of each run, Pallas kernels for 0% -> 9%
where the time goes in v1:
time: 112 us
  starting transfers between devices  55.9 us (50%)
  waiting for transfers between devices  31 us (28%)
  Pallas kernels  14.8 us (13%)
  local copies, waits for them, and re-layouts  8.53 us (8%)
    all_to_all x1, starting transfers between devices, body(): got = lax.all_to_all(payload, AXES, 0, 0, tiled=True)  17.1 us
    all_to_all x1, waiting for transfers between devices, body(): got = lax.all_to_all(payload, AXES, 0, 0, tiled=True)  16.2 us
    ppermute x3, waiting for transfers between devices, body(): lax.ppermute(line, 'wide', wide_perm(step, 0, 0))  10.4 us
    ppermute x6, starting transfers between devices, spread(): lax.ppermute(part, 'narrow', [(k, (k + step) % n_narrow) for k in range(n...  10.3 us
    ppermute x1, starting transfers between devices, body(): far_right = lax.ppermute(three[:2 * rows], 'wide', wide_perm(0, -3, 0))  6.28 us
    ppermute x3, starting transfers between devices, body(): lax.ppermute(line, 'wide', wide_perm(step, 0, 0))  5.68 us
    pallas_call x1, Pallas kernels, body(): call(centre_kernel, [(vectors, vectors, 128), (vectors, 128)], [SMEM] + [...  5.39 us
    ppermute x1, starting transfers between devices, body(): right = lax.ppermute(own, 'wide', wide_perm(0, -1, 0))  4.03 us
  transfers between devices with their start and end apart: 20, of which 6 were waited for; matrix products, arithmetic and copies ran while one was open for 6% of the time, Pallas kernels for 9%

profile of v1, /device:TPU:2, one launch (start us, length us, event | category | flops | bytes accessed | tf_op | source)
XLA Modules:
  0.0 111.6 jit_solution(13885526971548376033)
XLA Ops:
  0.7 1.5 %reshape.39 = f32[8,256,8]{2,1,0:T(8,128)S(1)} reshape(f32[8,2048]{1,0:T(8,128)} %param.15) | data formatting | bytes 131072 | tf_op jit(solution)/shard_map/reshape | solution.py:376
  2.1 0.0 copy-start.5
  2.1 0.3 copy.47
  2.5 2.0 %collective-permute-start.4 = (f32[8,2048]{1,0:T(8,128)S(1)}, f32[8,2048]{1,0:T(8,128)S(1)}, u32[]{:S(2)}, u32[]{:S(2)}) collective-permute-start(f32[8,2048]{1,0:T(8,128)S(1)} %bitcast.32), channel_id=1, source_target_pairs={{0,2},{1,3},{2,4},{3,5},{4,6},{5,7},{6,8},{7,9},{8,10},{9,11},{10,... | collective-permute-start | bytes 196616 | tf_op jit(solution)/shard_map/ppermute | solution.py:377
  4.5 4.0 %collective-permute-start.5 = (f32[8,2048]{1,0:T(8,128)S(1)}, f32[8,2048]{1,0:T(8,128)S(1)}, u32[]{:S(2)}, u32[]{:S(2)}) collective-permute-start(f32[8,2048]{1,0:T(8,128)S(1)} %bitcast.33), channel_id=1, source_target_pairs={{0,14},{1,15},{2,0},{3,1},{4,2},{5,3},{6,4},{7,5},{8,6},{9,7},{10,... | collective-permute-start | bytes 196616 | tf_op jit(solution)/shard_map/ppermute | solution.py:378
  8.6 3.4 %collective-permute-start = (bf16[27,8,256]{2,1,0:T(8,128)(2,1)S(1)}, bf16[27,8,256]{2,1,0:T(8,128)(2,1)S(1)}, u32[]{:S(2)}, u32[]{:S(2)}) collective-permute-start(bf16[27,8,256]{2,1,0:T(8,128)(2,1)S(1)} %get-tuple-element.34), channel_id=1, source_target_pairs={{0,64},{64,128},{128,192},{1,65},{65,129},{129,193},{2,66},{66,130... | collective-permute-start | bytes 331784 | tf_op jit(solution)/shard_map/ppermute | solution.py:365
  12.0 2.4 %collective-permute-start.1 = (bf16[27,8,256]{2,1,0:T(8,128)(2,1)S(1)}, bf16[27,8,256]{2,1,0:T(8,128)(2,1)S(1)}, u32[]{:S(2)}, u32[]{:S(2)}) collective-permute-start(bf16[27,8,256]{2,1,0:T(8,128)(2,1)S(1)} %get-tuple-element.33), channel_id=1, source_target_pairs={{64,0},{128,64},{192,128},{65,1},{129,65},{193,129},{66,2},{130,66... | collective-permute-start | bytes 331784 | tf_op jit(solution)/shard_map/ppermute | solution.py:366
  14.4 0.1 pad_maximum_fusion.2
  14.7 0.1 copy.44
  14.8 0.2 reshape.38.s_ref
  15.0 5.4 %centre.1 = (f32[8,8,128]{2,1,0:T(8,128)S(1)}, f32[8,128]{1,0:T(8,128)S(1)}) custom-call(f32[243]{0:T(256)S(1)} %reshape.38.s_ref, bf16[8,3,4,8,256]{4,3,2,1,0:T(8,128)(2,1)S(1)} %copy-done, bf16[3,4,8,256]{3,2,1,0:T(8,128)(2,1)S(1)} %copy.43.r_ref, f32[4,8,256]{2,1,0:T(8,128)S(1)} %copy-done.1, f32[4,8,256]{2,1,0:T(8,128)S(1)} %copy-done.2), custom_call_target="tpu_custom_call" | custom-call | flops 40000000 | bytes 1000000 | tf_op jit(solution)/shard_map/centre/pallas_call | solution.py:385
  20.5 1.9 %collective-permute-start.6 = (f32[24,2048]{1,0:T(8,128)S(1)}, f32[24,2048]{1,0:T(8,128)S(1)}, u32[]{:S(2)}, u32[]{:S(2)}) collective-permute-start(f32[24,2048]{1,0:T(8,128)S(1)} %pad_maximum_fusion), channel_id=1, source_target_pairs={{0,6},{1,7},{2,8},{3,9},{4,10},{5,11},{6,12},{7,13},{8,14},{9,15},... | collective-permute-start | bytes 589832 | tf_op jit(solution)/shard_map/ppermute | solution.py:380
  22.5 0.1 pad_maximum_fusion.3
  22.6 1.3 %collective-permute-start.2 = (bf16[27,6,256]{2,1,0:T(8,128)(2,1)S(1)}, bf16[27,6,256]{2,1,0:T(8,128)(2,1)S(1)}, u32[]{:S(2)}, u32[]{:S(2)}) collective-permute-start(bf16[27,6,256]{2,1,0:T(8,128)(2,1)S(1)} %pad_maximum_fusion.3), channel_id=1, source_target_pairs={{0,1},{1,2},{2,3},{3,4},{4,5},{5,6},{6,7},{7,8},{8,9},{9,10},{10,1... | collective-permute-start | bytes 248840 | tf_op jit(solution)/shard_map/ppermute | solution.py:372
  23.9 0.1 pad_maximum_fusion.4
  24.0 1.3 %collective-permute-start.3 = (bf16[27,6,256]{2,1,0:T(8,128)(2,1)S(1)}, bf16[27,6,256]{2,1,0:T(8,128)(2,1)S(1)}, u32[]{:S(2)}, u32[]{:S(2)}) collective-permute-start(bf16[27,6,256]{2,1,0:T(8,128)(2,1)S(1)} %pad_maximum_fusion.4), channel_id=1, source_target_pairs={{1,0},{2,1},{3,2},{4,3},{5,4},{6,5},{7,6},{8,7},{9,8},{10,9},{11,1... | collective-permute-start | bytes 248840 | tf_op jit(solution)/shard_map/ppermute | solution.py:373
  25.3 6.3 %collective-permute-start.7 = (f32[16,2048]{1,0:T(8,128)S(1)}, f32[16,2048]{1,0:T(8,128)S(1)}, u32[]{:S(2)}, u32[]{:S(2)}) collective-permute-start(f32[16,2048]{1,0:T(8,128)S(1)} %pad_maximum_fusion.1), channel_id=1, source_target_pairs={{0,10},{1,11},{2,12},{3,13},{4,14},{5,15},{6,0},{7,1},{8,2},{9,3},... | collective-permute-start | bytes 393224 | tf_op jit(solution)/shard_map/ppermute | solution.py:381
  31.6 4.0 %edges.1 = (f32[8,128]{1,0:T(8,128)S(1)}, f32[256,640]{1,0:T(8,128)S(1)}) custom-call(f32[243]{0:T(256)S(1)} %reshape.38.s_ref, s32[9]{0:T(128)S(1)} %bitcast.27, bf16[8,3,4,8,256]{4,3,2,1,0:T(8,128)(2,1)S(1)} %copy-done, f32[4,8,256]{2,1,0:T(8,128)S(1)} %copy-done.1, bf16[27,8,256]{2,1,0:T(8,128)(2,1)S(1)} %collective-permute-done.xlo_ref, ...), custom_call_target="tpu_custom_call" | custom-call | flops 10000000 | bytes 2000000 | tf_op jit(solution)/shard_map/edges/pallas_call | solution.py:394
  35.6 1.5 %copy.46 = f32[256,1,640]{2,1,0:T(1,128)} copy(f32[256,1,640]{2,0,1:T(8,128)S(1)} %bitcast.24) | data formatting | bytes 1310720 | tf_op jit(solution)/shard_map/all_to_all | solution.py:408
  37.1 17.1 %all-to-all-start = ((f32[256,1,640]{2,1,0:T(1,128)}), f32[256,1,640]{2,1,0:T(1,128)}, u32[]{:S(2)}, u32[]{:S(2)}) async-start(f32[256,1,640]{2,1,0:T(1,128)} %copy.46), calls=%async_computation | async-start | bytes 1310720 | tf_op jit(solution)/shard_map/all_to_all | solution.py:408
  54.3 1.5 %collective-permute-start.8 = (f32[64,2048]{1,0:T(8,128)S(1)}, f32[64,2048]{1,0:T(8,128)S(1)}, u32[]{:S(2)}, u32[]{:S(2)}) collective-permute-start(f32[64,2048]{1,0:T(8,128)S(1)} %constant_dynamic-update-slice_fusion.refs_0_), channel_id=1, source_target_pairs={{0,16},{1,17},{2,18},{3,19},{4,20},{5,21},{6,22},{7,23},{8,24},{9,... | collective-permute-start | bytes 1572872 | tf_op jit(solution)/shard_map/ppermute | solution.py:383
  55.8 2.7 %collective-permute-start.9 = (f32[64,2048]{1,0:T(8,128)S(1)}, f32[64,2048]{1,0:T(8,128)S(1)}, u32[]{:S(2)}, u32[]{:S(2)}) collective-permute-start(f32[64,2048]{1,0:T(8,128)S(1)} %constant_dynamic-update-slice_fusion.refs_0_), channel_id=1, source_target_pairs={{0,32},{1,33},{2,34},{3,35},{4,36},{5,37},{6,38},{7,39},{8,40},{9,... | collective-permute-start | bytes 1572872 | tf_op jit(solution)/shard_map/ppermute | solution.py:383
  58.6 1.4 %collective-permute-start.10 = (f32[64,2048]{1,0:T(8,128)S(1)}, f32[64,2048]{1,0:T(8,128)S(1)}, u32[]{:S(2)}, u32[]{:S(2)}) collective-permute-start(f32[64,2048]{1,0:T(8,128)S(1)} %constant_dynamic-update-slice_fusion.refs_0_), channel_id=1, source_target_pairs={{0,48},{1,49},{2,50},{3,51},{4,52},{5,53},{6,54},{7,55},{8,56},{9,... | collective-permute-start | bytes 1572872 | tf_op jit(solution)/shard_map/ppermute | solution.py:383
  60.0 16.2 %all-to-all-done = f32[256,1,640]{2,1,0:T(1,128)} async-done(((f32[256,1,640]{2,1,0:T(1,128)}), f32[256,1,640]{2,1,0:T(1,128)}, u32[]{:S(2)}, u32[]{:S(2)}) %all-to-all-start) | async-done | bytes 655392 | tf_op jit(solution)/shard_map/all_to_all | solution.py:408
  76.2 1.1 %copy.60 = f32[256,1,640]{2,0,1:T(8,128)S(1)} copy(f32[256,1,640]{2,1,0:T(1,128)} %all-to-all-done) | data formatting | bytes 1310720
  77.3 10.4 %collective-permute-done.9.refs_2_ = f32[64,2048]{1,0:T(8,128)S(1)} collective-permute-done((f32[64,2048]{1,0:T(8,128)S(1)}, f32[64,2048]{1,0:T(8,128)S(1)}, u32[]{:S(2)}, u32[]{:S(2)}) %collective-permute-start.9) | collective-permute-done | bytes 524320 | tf_op jit(solution)/shard_map/ppermute | solution.py:383
  87.7 1.4 %first.1 = (f32[640,256]{1,0:T(8,128)S(1)}, f32[8,256]{1,0:T(8,128)S(1)}, f32[8,256]{1,0:T(8,128)S(1)}) custom-call(f32[256,640]{1,0:T(8,128)S(1)} %bitcast.23, f32[64,2048]{1,0:T(8,128)S(1)} %constant_dynamic-update-slice_fusion.refs_0_, f32[64,2048]{1,0:T(8,128)S(1)} %collective-permute-done.8.refs_1_, f32[64,2048]{1,0:T(8,128)S(1)} %collective-permute-done.9.refs_2_, ...), custom_call_target="tpu_custom_call" | custom-call | flops 4000000 | bytes 3000000 | tf_op jit(solution)/shard_map/first/pallas_call | solution.py:427
  89.2 0.1 collective-permute-start.11
  89.3 1.2 %collective-permute-done.11 = f32[8,256]{1,0:T(8,128)S(1)} collective-permute-done((f32[8,256]{1,0:T(8,128)S(1)}, f32[8,256]{1,0:T(8,128)S(1)}, u32[]{:S(2)}, u32[]{:S(2)}) %collective-permute-start.11) | collective-permute-done | bytes 8224 | tf_op jit(solution)/shard_map/ppermute | solution.py:420
  90.5 1.3 %collective-permute-start.12 = (f32[8,256]{1,0:T(8,128)S(1)}, f32[8,256]{1,0:T(8,128)S(1)}, u32[]{:S(2)}, u32[]{:S(2)}) collective-permute-start(f32[8,256]{1,0:T(8,128)S(1)} %add.6.part_ref), channel_id=1, source_target_pairs={{0,64},{64,128},{128,192},{192,0},{1,65},{65,129},{129,193},{193,1... | collective-permute-start | bytes 24584 | tf_op jit(solution)/shard_map/ppermute | solution.py:422
  91.8 1.6 %collective-permute-start.13 = (f32[8,256]{1,0:T(8,128)S(1)}, f32[8,256]{1,0:T(8,128)S(1)}, u32[]{:S(2)}, u32[]{:S(2)}) collective-permute-start(f32[8,256]{1,0:T(8,128)S(1)} %add.6.part_ref), channel_id=1, source_target_pairs={{0,128},{64,192},{128,0},{192,64},{1,129},{65,193},{129,1},{193,65... | collective-permute-start | bytes 24584 | tf_op jit(solution)/shard_map/ppermute | solution.py:422
  93.4 1.7 %collective-permute-start.14 = (f32[8,256]{1,0:T(8,128)S(1)}, f32[8,256]{1,0:T(8,128)S(1)}, u32[]{:S(2)}, u32[]{:S(2)}) collective-permute-start(f32[8,256]{1,0:T(8,128)S(1)} %add.6.part_ref), channel_id=1, source_target_pairs={{0,192},{64,0},{128,64},{192,128},{1,193},{65,1},{129,65},{193,129... | collective-permute-start | bytes 24584 | tf_op jit(solution)/shard_map/ppermute | solution.py:422
  95.0 1.9 %collective-permute-done.13.got2_ref = f32[8,256]{1,0:T(8,128)S(1)} collective-permute-done((f32[8,256]{1,0:T(8,128)S(1)}, f32[8,256]{1,0:T(8,128)S(1)}, u32[]{:S(2)}, u32[]{:S(2)}) %collective-permute-start.13) | collective-permute-done | bytes 8224 | tf_op jit(solution)/shard_map/ppermute | solution.py:422
  96.9 0.1 collective-permute-done.14.got3_ref
  97.0 1.8 %second.1 = (f32[8,256]{1,0:T(8,128)S(1)}, f32[8,256]{1,0:T(8,128)S(1)}) custom-call(f32[640,256]{1,0:T(8,128)S(1)} %get-tuple-element.17.packed_ref, f32[8,256]{1,0:T(8,128)S(1)} %get-tuple-element.18.rhs_ref, f32[8,256]{1,0:T(8,128)S(1)} %add.6.part_ref, f32[8,256]{1,0:T(8,128)S(1)} %collective-permute-done.12.got1_ref, ...), custom_call_target="tpu_custom_call" | custom-call | flops 4000000 | bytes 3000000 | tf_op jit(solution)/shard_map/second/pallas_call | solution.py:435
  98.8 0.1 collective-permute-start.15
  98.9 1.2 %collective-permute-done.15 = f32[8,256]{1,0:T(8,128)S(1)} collective-permute-done((f32[8,256]{1,0:T(8,128)S(1)}, f32[8,256]{1,0:T(8,128)S(1)}, u32[]{:S(2)}, u32[]{:S(2)}) %collective-permute-start.15) | collective-permute-done | bytes 8224 | tf_op jit(solution)/shard_map/ppermute | solution.py:420
  100.1 1.1 collective-permute-start.16
  101.2 2.6 %collective-permute-start.17 = (f32[8,256]{1,0:T(8,128)S(1)}, f32[8,256]{1,0:T(8,128)S(1)}, u32[]{:S(2)}, u32[]{:S(2)}) collective-permute-start(f32[8,256]{1,0:T(8,128)S(1)} %add.7.part_ref), channel_id=1, source_target_pairs={{0,128},{64,192},{128,0},{192,64},{1,129},{65,193},{129,1},{193,65... | collective-permute-start | bytes 24584 | tf_op jit(solution)/shard_map/ppermute | solution.py:422
  103.8 2.1 %collective-permute-start.18 = (f32[8,256]{1,0:T(8,128)S(1)}, f32[8,256]{1,0:T(8,128)S(1)}, u32[]{:S(2)}, u32[]{:S(2)}) collective-permute-start(f32[8,256]{1,0:T(8,128)S(1)} %add.7.part_ref), channel_id=1, source_target_pairs={{0,192},{64,0},{128,64},{192,128},{1,193},{65,1},{129,65},{193,129... | collective-permute-start | bytes 24584 | tf_op jit(solution)/shard_map/ppermute | solution.py:422
  105.9 0.1 reshape.36.range_ref
  106.0 1.8 %copy.42.inverse_ref = bf16[12,12,3,5,256]{4,3,2,1,0:T(8,128)(2,1)S(1)} copy(bf16[12,12,3,5,256]{4,2,3,1,0:T(4,128)(2,1)} %param.14) | data formatting | bytes 2211840 | tf_op args[5]
  107.8 0.1 reshape.41
  107.8 0.7 copy.49
  108.6 0.8 local.1.local_ref
  109.4 1.3 %last.1 = (f32[3,4,8,256]{3,2,1,0:T(8,128)}, f32[8,256]{1,0:T(8,128)S(1)}) custom-call(s32[9]{0:T(128)S(1)} %bitcast.28, bf16[8,3,4,8,256]{4,3,2,1,0:T(8,128)(2,1)S(1)} %copy-done, f32[3,4,8,256]{3,2,1,0:T(8,128)S(1)} %local.1.local_ref, f32[8,256]{1,0:T(8,128)S(1)} %get-tuple-element.20.first_ref, f32[8,256]{1,0:T(8,128)S(1)} %add.7.part_ref, ...), custom_call_target="tpu_custom_call" | custom-call | flops 1000000 | bytes 1000000 | tf_op jit(solution)/shard_map/last/pallas_call | solution.py:443
  110.8 0.1 copy.48
  110.9 0.7 reshape.43
  (44 shorter events, 0.4 us)
Async XLA Ops:
  0.6 7.9 %copy-start = (bf16[8,3,4,8,256]{4,3,2,1,0:T(8,128)(2,1)S(1)}, bf16[8,3,4,8,256]{4,3,2,1,0:T(8,128)(2,1)}, u32[]{:S(2)}) copy-start(bf16[8,3,4,8,256]{4,3,2,1,0:T(8,128)(2,1)} %z_ref.5) | copy-start | bytes 1179652
  0.6 7.9 %copy-start.4 = (f32[3,4,8,256]{3,2,1,0:T(8,128)S(1)}, f32[3,4,8,256]{3,2,1,0:T(8,128)}, u32[]{:S(2)}) copy-start(f32[3,4,8,256]{3,2,1,0:T(8,128)} %param.10) | copy-start | bytes 294916
  2.1 12.6 %copy-start.5 = (f32[27,3,3]{0,2,1:T(4,128)S(1)}, f32[27,3,3]{0,2,1:T(4,128)}, u32[]{:S(2)}) copy-start(f32[27,3,3]{0,2,1:T(4,128)} %param.13) | copy-start | bytes 2920
  2.4 12.6 %copy-start.1 = (f32[4,8,256]{2,1,0:T(8,128)S(1)}, f32[4,8,256]{2,1,0:T(8,128)}, u32[]{:S(2)}) copy-start(f32[4,8,256]{2,1,0:T(8,128)} %stiff_ref.3) | copy-start | bytes 98308
  2.5 12.6 %copy-start.2 = (f32[4,8,256]{2,1,0:T(8,128)S(1)}, f32[4,8,256]{2,1,0:T(8,128)}, u32[]{:S(2)}) copy-start(f32[4,8,256]{2,1,0:T(8,128)} %mass_ref.1) | copy-start | bytes 98308
  2.5 18.0 %collective-permute-start.4 = (f32[8,2048]{1,0:T(8,128)S(1)}, f32[8,2048]{1,0:T(8,128)S(1)}, u32[]{:S(2)}, u32[]{:S(2)}) collective-permute-start(f32[8,2048]{1,0:T(8,128)S(1)} %bitcast.32), channel_id=1, source_target_pairs={{0,2},{1,3},{2,4},{3,5},{4,6},{5,7},{6,8},{7,9},{8,10},{9,11},{10,... | collective-permute-start | bytes 196616 | tf_op jit(solution)/shard_map/ppermute | solution.py:377
  4.5 16.0 %collective-permute-start.5 = (f32[8,2048]{1,0:T(8,128)S(1)}, f32[8,2048]{1,0:T(8,128)S(1)}, u32[]{:S(2)}, u32[]{:S(2)}) collective-permute-start(f32[8,2048]{1,0:T(8,128)S(1)} %bitcast.33), channel_id=1, source_target_pairs={{0,14},{1,15},{2,0},{3,1},{4,2},{5,3},{6,4},{7,5},{8,6},{9,7},{10,... | collective-permute-start | bytes 196616 | tf_op jit(solution)/shard_map/ppermute | solution.py:378
  8.6 23.0 %copy-start.3 = (s32[1,1,9]{2,1,0:T(1,128)S(1)}, s32[1,1,9]{2,1,0:T(1,128)}, u32[]{:S(2)}) copy-start(s32[1,1,9]{2,1,0:T(1,128)} %param.17) | copy-start | bytes 112
  8.6 13.8 %collective-permute-start = (bf16[27,8,256]{2,1,0:T(8,128)(2,1)S(1)}, bf16[27,8,256]{2,1,0:T(8,128)(2,1)S(1)}, u32[]{:S(2)}, u32[]{:S(2)}) collective-permute-start(bf16[27,8,256]{2,1,0:T(8,128)(2,1)S(1)} %get-tuple-element.34), channel_id=1, source_target_pairs={{0,64},{64,128},{128,192},{1,65},{65,129},{129,193},{2,66},{66,130... | collective-permute-start | bytes 331784 | tf_op jit(solution)/shard_map/ppermute | solution.py:365
  12.0 10.4 %collective-permute-start.1 = (bf16[27,8,256]{2,1,0:T(8,128)(2,1)S(1)}, bf16[27,8,256]{2,1,0:T(8,128)(2,1)S(1)}, u32[]{:S(2)}, u32[]{:S(2)}) collective-permute-start(bf16[27,8,256]{2,1,0:T(8,128)(2,1)S(1)} %get-tuple-element.33), channel_id=1, source_target_pairs={{64,0},{128,64},{192,128},{65,1},{129,65},{193,129},{66,2},{130,66... | collective-permute-start | bytes 331784 | tf_op jit(solution)/shard_map/ppermute | solution.py:366
  20.5 33.8 %collective-permute-start.6 = (f32[24,2048]{1,0:T(8,128)S(1)}, f32[24,2048]{1,0:T(8,128)S(1)}, u32[]{:S(2)}, u32[]{:S(2)}) collective-permute-start(f32[24,2048]{1,0:T(8,128)S(1)} %pad_maximum_fusion), channel_id=1, source_target_pairs={{0,6},{1,7},{2,8},{3,9},{4,10},{5,11},{6,12},{7,13},{8,14},{9,15},... | collective-permute-start | bytes 589832 | tf_op jit(solution)/shard_map/ppermute | solution.py:380
  22.6 9.0 %collective-permute-start.2 = (bf16[27,6,256]{2,1,0:T(8,128)(2,1)S(1)}, bf16[27,6,256]{2,1,0:T(8,128)(2,1)S(1)}, u32[]{:S(2)}, u32[]{:S(2)}) collective-permute-start(bf16[27,6,256]{2,1,0:T(8,128)(2,1)S(1)} %pad_maximum_fusion.3), channel_id=1, source_target_pairs={{0,1},{1,2},{2,3},{3,4},{4,5},{5,6},{6,7},{7,8},{8,9},{9,10},{10,1... | collective-permute-start | bytes 248840 | tf_op jit(solution)/shard_map/ppermute | solution.py:372
  24.0 7.6 %collective-permute-start.3 = (bf16[27,6,256]{2,1,0:T(8,128)(2,1)S(1)}, bf16[27,6,256]{2,1,0:T(8,128)(2,1)S(1)}, u32[]{:S(2)}, u32[]{:S(2)}) collective-permute-start(bf16[27,6,256]{2,1,0:T(8,128)(2,1)S(1)} %pad_maximum_fusion.4), channel_id=1, source_target_pairs={{1,0},{2,1},{3,2},{4,3},{5,4},{6,5},{7,6},{8,7},{9,8},{10,9},{11,1... | collective-permute-start | bytes 248840 | tf_op jit(solution)/shard_map/ppermute | solution.py:373
  25.3 29.0 %collective-permute-start.7 = (f32[16,2048]{1,0:T(8,128)S(1)}, f32[16,2048]{1,0:T(8,128)S(1)}, u32[]{:S(2)}, u32[]{:S(2)}) collective-permute-start(f32[16,2048]{1,0:T(8,128)S(1)} %pad_maximum_fusion.1), channel_id=1, source_target_pairs={{0,10},{1,11},{2,12},{3,13},{4,14},{5,15},{6,0},{7,1},{8,2},{9,3},... | collective-permute-start | bytes 393224 | tf_op jit(solution)/shard_map/ppermute | solution.py:381
  37.1 39.1 %all-to-all-start = ((f32[256,1,640]{2,1,0:T(1,128)}), f32[256,1,640]{2,1,0:T(1,128)}, u32[]{:S(2)}, u32[]{:S(2)}) async-start(f32[256,1,640]{2,1,0:T(1,128)} %copy.46), calls=%async_computation | async-start | bytes 1310720 | tf_op jit(solution)/shard_map/all_to_all | solution.py:408
  54.3 23.0 %collective-permute-start.8 = (f32[64,2048]{1,0:T(8,128)S(1)}, f32[64,2048]{1,0:T(8,128)S(1)}, u32[]{:S(2)}, u32[]{:S(2)}) collective-permute-start(f32[64,2048]{1,0:T(8,128)S(1)} %constant_dynamic-update-slice_fusion.refs_0_), channel_id=1, source_target_pairs={{0,16},{1,17},{2,18},{3,19},{4,20},{5,21},{6,22},{7,23},{8,24},{9,... | collective-permute-start | bytes 1572872 | tf_op jit(solution)/shard_map/ppermute | solution.py:383
  55.8 31.9 %collective-permute-start.9 = (f32[64,2048]{1,0:T(8,128)S(1)}, f32[64,2048]{1,0:T(8,128)S(1)}, u32[]{:S(2)}, u32[]{:S(2)}) collective-permute-start(f32[64,2048]{1,0:T(8,128)S(1)} %constant_dynamic-update-slice_fusion.refs_0_), channel_id=1, source_target_pairs={{0,32},{1,33},{2,34},{3,35},{4,36},{5,37},{6,38},{7,39},{8,40},{9,... | collective-permute-start | bytes 1572872 | tf_op jit(solution)/shard_map/ppermute | solution.py:383
  58.6 29.2 %collective-permute-start.10 = (f32[64,2048]{1,0:T(8,128)S(1)}, f32[64,2048]{1,0:T(8,128)S(1)}, u32[]{:S(2)}, u32[]{:S(2)}) collective-permute-start(f32[64,2048]{1,0:T(8,128)S(1)} %constant_dynamic-update-slice_fusion.refs_0_), channel_id=1, source_target_pairs={{0,48},{1,49},{2,50},{3,51},{4,52},{5,53},{6,54},{7,55},{8,56},{9,... | collective-permute-start | bytes 1572872 | tf_op jit(solution)/shard_map/ppermute | solution.py:383
  89.2 16.7 %copy-start.6 = (s32[1,1,2,2]{3,2,1,0:T(2,128)S(1)}, s32[1,1,2,2]{3,2,1,0:T(2,128)}, u32[]{:S(2)}) copy-start(s32[1,1,2,2]{3,2,1,0:T(2,128)} %param.16) | copy-start | bytes 52
  89.2 1.3 %collective-permute-start.11 = (f32[8,256]{1,0:T(8,128)S(1)}, f32[8,256]{1,0:T(8,128)S(1)}, u32[]{:S(2)}, u32[]{:S(2)}) collective-permute-start(f32[8,256]{1,0:T(8,128)S(1)} %get-tuple-element.19), channel_id=1, source_target_pairs={{0,1},{1,0},{2,3},{3,2},{4,5},{5,4},{6,7},{7,6},{8,9},{9,8},{10,11... | collective-permute-start | bytes 24584 | tf_op jit(solution)/shard_map/ppermute | solution.py:420
  90.5 4.6 %collective-permute-start.12 = (f32[8,256]{1,0:T(8,128)S(1)}, f32[8,256]{1,0:T(8,128)S(1)}, u32[]{:S(2)}, u32[]{:S(2)}) collective-permute-start(f32[8,256]{1,0:T(8,128)S(1)} %add.6.part_ref), channel_id=1, source_target_pairs={{0,64},{64,128},{128,192},{192,0},{1,65},{65,129},{129,193},{193,1... | collective-permute-start | bytes 24584 | tf_op jit(solution)/shard_map/ppermute | solution.py:422
  91.8 5.2 %collective-permute-start.13 = (f32[8,256]{1,0:T(8,128)S(1)}, f32[8,256]{1,0:T(8,128)S(1)}, u32[]{:S(2)}, u32[]{:S(2)}) collective-permute-start(f32[8,256]{1,0:T(8,128)S(1)} %add.6.part_ref), channel_id=1, source_target_pairs={{0,128},{64,192},{128,0},{192,64},{1,129},{65,193},{129,1},{193,65... | collective-permute-start | bytes 24584 | tf_op jit(solution)/shard_map/ppermute | solution.py:422
  93.4 3.7 %collective-permute-start.14 = (f32[8,256]{1,0:T(8,128)S(1)}, f32[8,256]{1,0:T(8,128)S(1)}, u32[]{:S(2)}, u32[]{:S(2)}) collective-permute-start(f32[8,256]{1,0:T(8,128)S(1)} %add.6.part_ref), channel_id=1, source_target_pairs={{0,192},{64,0},{128,64},{192,128},{1,193},{65,1},{129,65},{193,129... | collective-permute-start | bytes 24584 | tf_op jit(solution)/shard_map/ppermute | solution.py:422
  98.8 1.3 %collective-permute-start.15 = (f32[8,256]{1,0:T(8,128)S(1)}, f32[8,256]{1,0:T(8,128)S(1)}, u32[]{:S(2)}, u32[]{:S(2)}) collective-permute-start(f32[8,256]{1,0:T(8,128)S(1)} %get-tuple-element.21), channel_id=1, source_target_pairs={{0,1},{1,0},{2,3},{3,2},{4,5},{5,4},{6,7},{7,6},{8,9},{9,8},{10,11... | collective-permute-start | bytes 24584 | tf_op jit(solution)/shard_map/ppermute | solution.py:420
  100.1 9.3 %collective-permute-start.16 = (f32[8,256]{1,0:T(8,128)S(1)}, f32[8,256]{1,0:T(8,128)S(1)}, u32[]{:S(2)}, u32[]{:S(2)}) collective-permute-start(f32[8,256]{1,0:T(8,128)S(1)} %add.7.part_ref), channel_id=1, source_target_pairs={{0,64},{64,128},{128,192},{192,0},{1,65},{65,129},{129,193},{193,1... | collective-permute-start | bytes 24584 | tf_op jit(solution)/shard_map/ppermute | solution.py:422
  101.2 8.2 %collective-permute-start.17 = (f32[8,256]{1,0:T(8,128)S(1)}, f32[8,256]{1,0:T(8,128)S(1)}, u32[]{:S(2)}, u32[]{:S(2)}) collective-permute-start(f32[8,256]{1,0:T(8,128)S(1)} %add.7.part_ref), channel_id=1, source_target_pairs={{0,128},{64,192},{128,0},{192,64},{1,129},{65,193},{129,1},{193,65... | collective-permute-start | bytes 24584 | tf_op jit(solution)/shard_map/ppermute | solution.py:422
  103.8 5.6 %collective-permute-start.18 = (f32[8,256]{1,0:T(8,128)S(1)}, f32[8,256]{1,0:T(8,128)S(1)}, u32[]{:S(2)}, u32[]{:S(2)}) collective-permute-start(f32[8,256]{1,0:T(8,128)S(1)} %add.7.part_ref), channel_id=1, source_target_pairs={{0,192},{64,0},{128,64},{192,128},{1,193},{65,1},{129,65},{193,129... | collective-permute-start | bytes 24584 | tf_op jit(solution)/shard_map/ppermute | solution.py:422

commit v2 on v1

v2 whole, which is shorter than its diff:
```python
import functools

import jax
import jax.numpy as jnp
from jax import lax
from jax.experimental import pallas as pl
from jax.experimental.pallas import tpu as pltpu
from jax.sharding import PartitionSpec as P

F32 = jnp.float32
WIDE = ("y", "z", "core")
SLOT = 80
VMEM = pl.BlockSpec(memory_space=pltpu.VMEM)
SMEM = pl.BlockSpec(memory_space=pltpu.SMEM)


def shifted(value, offset, axis):
    if offset == 0:
        return value
    size = value.shape[axis]
    rolled = pltpu.roll(value, (-offset) % size, axis)
    at = lax.broadcasted_iota(jnp.int32, value.shape, axis)
    keep = at < size - offset if offset > 0 else at >= -offset
    return jnp.where(keep, rolled, 0.0)


def rows_sum(value):
    return jnp.sum(value[:, :128] + value[:, 128:], axis=0, keepdims=True)


def entry(s_ref, ox, oy, oz, i, j):
    return s_ref[i, j, ((ox + 1) * 3 + oy + 1) * 3 + oz + 1]


def faces(total):
    return jnp.sum(total, axis=1, keepdims=True)


def centre_rows(b, s_ref, zf_ref, stiff_ref, mass_ref, rows_ref, place):
    vectors, _, cells_x = zf_ref.shape[:3]
    field = [[zf_ref[b, j, x] for x in range(cells_x)] for j in range(3)]
    weighted = []
    for i in range(3):
        image = [None] * cells_x
        for oz in (-1, 0, 1):
            level = [None] * cells_x
            for oy in (-1, 0, 1):
                for x in range(cells_x):
                    acc = None
                    for ox in (-1, 0, 1):
                        if 0 <= x + ox < cells_x:
                            for j in range(3):
                                term = entry(s_ref, ox, oy, oz, i, j) * field[j][x + ox]
                                acc = term if acc is None else acc + term
                    acc = shifted(acc, oy, 0)
                    level[x] = acc if level[x] is None else level[x] + acc
            for x in range(cells_x):
                moved = shifted(level[x], oz, 1)
                image[x] = moved if image[x] is None else image[x] + moved
        weighted.append([stiff_ref[x] * image[x] + mass_ref[x] * field[i][x] for x in range(cells_x)])
    for a in range(vectors):
        total = None
        for i in range(3):
            for x in range(cells_x):
                term = zf_ref[a, i, x] * weighted[i][x]
                total = term if total is None else total + term
        rows_ref[place, a : a + 1, :] = rows_sum(total)


def before_kernel(
    done, s_ref, ids_ref, z_ref, r_ref, stiff_ref, mass_ref, zf_ref, zy_ref, sy_ref, table_ref, rows_ref
):
    vectors, _, cells_x, cells_y, depth = z_ref.shape
    own_y = (0, cells_y - 1)
    blank = jnp.zeros((8 - cells_x, depth), F32)

    def columns(rows):
        return jnp.concatenate(rows + [blank], axis=0)

    def convert(a, carry):
        for i in range(3):
            cells = [z_ref[a, i, x].astype(F32) for x in range(cells_x)]
            for x in range(cells_x):
                zf_ref[a, i, x] = cells[x]
            for face, y in enumerate(own_y):
                zy_ref[face, a, i] = columns([cell[y : y + 1, :] for cell in cells])
        return carry

    lax.fori_loop(0, vectors, convert, 0)
    for face, y in enumerate(own_y):
        sy_ref[face] = columns([stiff_ref[x, y : y + 1, :] for x in range(cells_x)])
    for a in range(vectors):
        total = None
        for i in range(3):
            for x in range(cells_x):
                term = zf_ref[a, i, x] * r_ref[i, x].astype(F32)
                total = term if total is None else total + term
        rows_ref[done, a : a + 1, :] = rows_sum(total)

    def one(b, carry):
        centre_rows(b, s_ref, zf_ref, stiff_ref, mass_ref, rows_ref, b)
        return carry

    lax.fori_loop(0, done, one, 0)
    lane = lax.broadcasted_iota(jnp.int32, (8, 128), 1)
    table = jnp.where(lane == 9 * vectors + 1, ids_ref[4].astype(F32), 0.0)
    table = jnp.where(lane == 9 * vectors, faces(rows_ref[done]), table)
    for b in range(done):
        table = jnp.where(lane == 4 * vectors + b, faces(rows_ref[b]), table)
    table_ref[...] = table


def inner_kernel(done, s_ref, zf_ref, stiff_ref, mass_ref, xlo_ref, xhi_ref, before_ref, table_ref, rows_ref):
    vectors, _, cells_x = zf_ref.shape[:3]
    own_x = (0, cells_x - 1)

    def one(b, carry):
        centre_rows(b, s_ref, zf_ref, stiff_ref, mass_ref, rows_ref, vectors + b)
        return carry

    lax.fori_loop(done, vectors, one, 0)

    def other(b, carry):
        for face, halo_ref in ((0, xlo_ref), (1, xhi_ref)):
            ox = 2 * face - 1
            field = [halo_ref[b * 3 + j].astype(F32) for j in range(3)]
            stiff = stiff_ref[own_x[face]]
            weighted = []
            for i in range(3):
                image = None
                for oz in (-1, 0, 1):
                    level = None
                    for oy in (-1, 0, 1):
                        acc = sum(entry(s_ref, ox, oy, oz, i, j) * field[j] for j in range(3))
                        acc = shifted(acc, oy, 0)
                        level = acc if level is None else level + acc
                    moved = shifted(level, oz, 1)
                    image = moved if image is None else image + moved
                weighted.append(stiff * image)
            for a in range(vectors):
                total = sum(zf_ref[a, i, own_x[face]] * weighted[i] for i in range(3))
                rows_ref[2 * face * vectors + b, a : a + 1, :] = rows_sum(total)
        return carry

    lax.fori_loop(0, vectors, other, 0)
    lane = lax.broadcasted_iota(jnp.int32, (8, 128), 1)
    table = before_ref[...]
    for place, number in enumerate((1, 4, 7)):
        for b in range(done if number == 4 else 0, vectors):
            table = jnp.where(lane == number * vectors + b, faces(rows_ref[place * vectors + b]), table)
    table_ref[...] = table


def outer_kernel(s_ref, table_ref, zy_ref, sy_ref, ylo_ref, yhi_ref, blocks_ref, pay_ref, rows_ref):
    vectors, depth = zy_ref.shape[1], zy_ref.shape[4]
    cells_x = ylo_ref.shape[1] - 2
    row = lax.broadcasted_iota(jnp.int32, (8, depth), 0)

    def one(b, carry):
        for face, halo_ref in ((0, ylo_ref), (1, yhi_ref)):
            oy = 2 * face - 1
            pad = jnp.zeros((8 - halo_ref.shape[1], depth), F32)
            field = [jnp.concatenate([halo_ref[b * 3 + j].astype(F32), pad], axis=0) for j in range(3)]
            stiff = sy_ref[face]
            inner, outer = [], []
            for i in range(3):
                mid, rim = None, None
                for ox in (-1, 0, 1):
                    line = None
                    for oz in (-1, 0, 1):
                        acc = sum(entry(s_ref, ox, oy, oz, i, j) * field[j] for j in range(3))
                        acc = shifted(acc, oz, 1)
                        line = acc if line is None else line + acc
                    moved = pltpu.roll(line, (-(1 + ox)) % 8, 0) if ox != -1 else line
                    low, high = max(0, -ox), min(cells_x, cells_x - ox)
                    part = jnp.where((row >= low) & (row < high), moved, 0.0)
                    mid = part if mid is None else mid + part
                    if ox != 0:
                        edge = jnp.where(row == (0 if ox == -1 else cells_x - 1), moved, 0.0)
                        rim = edge if rim is None else rim + edge
                inner.append(stiff * mid)
                outer.append(stiff * rim)
            for a in range(vectors):
                own = [zy_ref[face, a, i] for i in range(3)]
                total = sum(own[i] * inner[i] for i in range(3))
                rows_ref[(3 * face + 1) * vectors + b, a : a + 1, :] = rows_sum(total)
                total = sum(own[i] * outer[i] for i in range(3))
                half = total[:, :128] + total[:, 128:]
                rows_ref[3 * face * vectors + b, a : a + 1, :] = half[0:1, :]
                rows_ref[(3 * face + 2) * vectors + b, a : a + 1, :] = half[cells_x - 1 : cells_x, :]
        return carry

    lax.fori_loop(0, vectors, one, 0)
    lane = lax.broadcasted_iota(jnp.int32, (8, 128), 1)
    table = table_ref[...]
    for place, number in enumerate((0, 3, 6, 2, 5, 8)):
        for b in range(vectors):
            table = jnp.where(lane == number * vectors + b, faces(rows_ref[place * vectors + b]), table)
    blocks_ref[...] = table
    width = pay_ref.shape[2]
    wide = jnp.concatenate([table, jnp.zeros((8, width - 128), F32)], axis=1)
    line = jnp.zeros((1, width), F32)
    for a in range(vectors):
        piece = wide[a : a + 1, :]
        line = line + (pltpu.roll(piece, a * SLOT, 1) if a else piece)
    for place in range(pay_ref.shape[0]):
        pay_ref[place] = line


def local_kernel(range_ref, inverse_ref, r_ref, xlo_ref, xhi_ref, ylo_ref, yhi_ref, out_ref, ext_ref, sol_ref):
    cells_x, cells_y = r_ref.shape[1:3]
    ext_x, ext_y = cells_x + 2, cells_y + 2
    half_x, half_y = ext_x // 2, ext_y // 2
    first = xlo_ref.shape[0] - 3
    halves = ((0, slice(0, 128)), (1, slice(128, 256)))
    for c in range(3):
        layers = [xlo_ref[first + c]] + [r_ref[c, x] for x in range(cells_x)] + [xhi_ref[first + c]]
        layers = [layer.astype(F32) for layer in layers]
        low, high = ylo_ref[first + c].astype(F32), yhi_ref[first + c].astype(F32)
        for h, lanes in halves:
            ext_ref[c, 0, h, 0:ext_x, :] = low[:, lanes]
            ext_ref[c, ext_y - 1, h, 0:ext_x, :] = high[:, lanes]
            for e, layer in enumerate(layers):
                for y in range(cells_y):
                    ext_ref[c, y + 1, h, e : e + 1, :] = layer[y : y + 1, lanes]
    at = lax.broadcasted_iota(jnp.int32, (half_x, r_ref.shape[3]), 0)
    for v in range(half_y):
        fields = []
        for m in range(12):
            c, s, t = m // 4, m // 2 % 2, m % 2
            e, f = 2 * at + s, 2 * v + t
            keep = (f >= range_ref[2]) & (f < range_ref[3]) & (e >= range_ref[0]) & (e < range_ref[1])
            value = jnp.concatenate([ext_ref[c, f, h, pl.ds(s, half_x, stride=2), :] for h, _ in halves], axis=1)
            fields.append(jnp.where(keep, value, 0.0))
        for i in range(12):
            acc = None
            for m in range(12):
                term = inverse_ref[i, m, v].astype(F32) * fields[m]
                acc = term if acc is None else acc + term
            c, s, t = i // 4, i // 2 % 2, i % 2
            for h, lanes in halves:
                sol_ref[c, 2 * v + t, h, pl.ds(s, half_x, stride=2), :] = acc[:, lanes]
    for c in range(3):
        for y in range(cells_y):
            for h, lanes in halves:
                for x in range(cells_x):
                    out_ref[c, x, y : y + 1, lanes] = sol_ref[c, y + 1, h, x + 1 : x + 2, :]


def moved_by(value, choice, dims):
    high = value.astype(jnp.bfloat16).astype(F32)
    middle = (value - high).astype(jnp.bfloat16).astype(F32)
    parts = jnp.concatenate([high, middle, (value - high) - middle], axis=0).astype(jnp.bfloat16)
    result = lax.dot_general(parts, choice, (dims, ((), ())), preferred_element_type=F32)
    return (result[0:8] + result[8:16]) + result[16:24]


def slots_of(packed_ref):
    count = packed_ref.shape[1]
    ids = packed_ref[73:74, :].astype(jnp.int32)
    return (lax.broadcasted_iota(jnp.int32, (count, count), 0) == ids).astype(F32).astype(jnp.bfloat16)


def share_of(vector, piece):
    line = jnp.concatenate([vector[b : b + 1, :] for b in range(8)], axis=1)
    line = jnp.broadcast_to(line, (8, line.shape[1]))
    acc = jnp.zeros(line.shape, F32)
    group = 4

    def step(t, acc):
        tiles, inner = [], []
        for q in range(group):
            tile = piece[pl.ds(pl.multiple_of((t * group + q) * 8, 8), 8), :]
            tiles.append(tile)
            inner.append(jnp.sum(tile * line, axis=1, keepdims=True))
        for tile, value in zip(tiles, inner):
            acc = acc + tile * value
        return acc

    acc = lax.fori_loop(0, piece.shape[0] // 8 // group, step, acc)
    total = jnp.sum(acc, axis=0, keepdims=True)
    blocks = vector.shape[1]
    return jnp.concatenate([total[:, b * blocks : (b + 1) * blocks] for b in range(8)], axis=0)


def first_kernel(
    n_narrow, size_z, core_ref, own_ref, other_ref, piece, packed_ref, rhs_ref, share_ref, rows_ref
):
    size_y = own_ref.shape[0]
    chips = n_narrow * size_y * size_z
    for got_ref, core in ((own_ref, core_ref[0]), (other_ref, 1 - core_ref[0])):
        for y in range(size_y):
            for x in range(n_narrow):
                place = pl.multiple_of(core * chips + (x * size_y + y) * size_z, 8)
                block = got_ref[y, x * size_z : (x + 1) * size_z]
                rows_ref[pl.ds(place, size_z), :] = block.reshape(size_z, block.shape[2])
    packed_ref[...] = rows_ref[...].T
    own = jnp.concatenate([packed_ref[a * SLOT + 72 : a * SLOT + 73, :] for a in range(8)], axis=0)
    rhs = moved_by(own, slots_of(packed_ref), ((1,), (1,)))
    rhs_ref[...] = rhs
    share = share_of(rhs, piece)
    for place in range(share_ref.shape[0]):
        share_ref[place] = share


def summed(parts_ref):
    parts = [parts_ref[k] for k in range(parts_ref.shape[0])]
    while len(parts) > 1:
        parts = [parts[k] + parts[k + 1] for k in range(0, len(parts), 2)]
    return parts[0]


def second_kernel(n_narrow, packed_ref, rhs_ref, parts_ref, piece, first_ref, share_ref):
    first = summed(parts_ref)
    first_ref[...] = first
    slots = slots_of(packed_ref)
    there = moved_by(first, slots, ((1,), (0,)))
    size = there.shape[1] // 2
    chips = size // n_narrow
    halves = [there[:, :size], there[:, size:]]
    at = lax.broadcasted_iota(jnp.int32, halves[0].shape, 1)
    row, column = at // chips, at % chips
    near = []
    for dx in (-1, 0, 1):
        for dy in (-1, 0, 1):
            sides = []
            for core in range(2):
                step = (core + dy) // 2
                move = (-(dx * chips + step)) % size
                value = halves[(core + dy) % 2]
                value = pltpu.roll(value, move, 1) if move else value
                keep = (row + dx >= 0) & (row + dx < n_narrow) & (column + step >= 0) & (column + step < chips)
                sides.append(jnp.where(keep, value, 0.0))
            near.append(jnp.concatenate(sides, axis=1))
    near.append(jnp.zeros_like(there))
    near = jnp.concatenate(near, axis=0)
    image = jnp.concatenate(
        [jnp.sum(packed_ref[a * SLOT : (a + 1) * SLOT, :] * near, axis=0, keepdims=True) for a in range(8)], axis=0
    )
    vector = rhs_ref[...] - moved_by(image, slots, ((1,), (1,)))
    share = share_of(vector, piece)
    for place in range(share_ref.shape[0]):
        share_ref[place] = share


def last_kernel(ids_ref, z_ref, local_ref, first_ref, parts_ref, out_ref, sol_ref):
    solution = first_ref[...] + summed(parts_ref)
    sol_ref[...] = solution
    at = lax.broadcasted_iota(jnp.int32, solution.shape, 1)
    weights = jnp.sum(jnp.where(at == ids_ref[4], solution, 0.0), axis=1, keepdims=True)
    for x in range(z_ref.shape[2]):
        for i in range(3):
            acc = local_ref[i, x]
            for a in range(8):
                acc = acc + weights[a : a + 1, :] * z_ref[a, i, x].astype(F32)
            out_ref[i, x] = acc


def call(kernel, out_shape, in_specs, scratch=(), flops=0, moved=0, name=None):
    return pl.pallas_call(
        kernel,
        out_shape=[jax.ShapeDtypeStruct(shape, F32) for shape in out_shape],
        in_specs=in_specs,
        out_specs=[VMEM] * len(out_shape),
        scratch_shapes=list(scratch),
        compiler_params=pltpu.CompilerParams(vmem_limit_bytes=24 * 2**20),
        cost_estimate=pl.CostEstimate(flops=flops, bytes_accessed=moved, transcendentals=0),
        name=name,
    )


def body(
    deflation,
    residual,
    stiffness,
    mass,
    stencil,
    local_inverse,
    inverse_factor,
    margin_range,
    neighbor_blocks,
):
    vectors, _, cells_x, cells_y, depth = deflation.shape
    n_narrow, size_z = lax.axis_size("narrow"), lax.axis_size("z")
    count = lax.axis_size(WIDE) * n_narrow
    n_near = n_narrow * size_z
    size_y = lax.axis_size("y")

    rounded = residual.astype(jnp.bfloat16)
    couplings = stencil.transpose(1, 2, 0)
    ids = neighbor_blocks.reshape(-1)
    ranges = margin_range.reshape(-1)

    def swaps(axis):
        size = lax.axis_size(axis)
        even = [(k, k ^ 1) for k in range(size)]
        odd = [(k, ((k + 1) ^ 1) - 1) for k in range(1, size - 1)]
        return even, odd, lax.axis_index(axis) % 2 == 0

    def exchanged(sending_low, sending_high, axis):
        even, odd, is_even = swaps(axis)

        def chosen(first, second):
            return jnp.concatenate([jnp.where(is_even, x, y) for x, y in zip(first, second)], axis=0)

        one = lax.ppermute(chosen(sending_high, sending_low), axis, even)
        two = lax.ppermute(chosen(sending_low, sending_high), axis, odd)
        return one, two, is_even

    vector_fields = deflation.reshape(3 * vectors, cells_x, cells_y, depth)
    fields = (vector_fields, rounded)
    one, two, is_even = exchanged([f[:, 0] for f in fields], [f[:, cells_x - 1] for f in fields], "narrow")

    done = vectors // 2
    zf, zy, sy, table = call(
        functools.partial(before_kernel, done),
        [(vectors, 3, cells_x, cells_y, depth), (2, vectors, 3, 8, depth), (2, 8, depth), (8, 128)],
        [SMEM, SMEM] + [VMEM] * 4,
        [pltpu.VMEM((done + 1, 8, 128), F32)],
        flops=20_000_000,
        moved=1_000_000,
        name="before",
    )(couplings, ids, deflation, rounded, stiffness, mass)
    one, two, table = lax.optimization_barrier((one, two, table))
    xlo, xhi = jnp.where(is_even, two, one), jnp.where(is_even, one, two)

    def side(y):
        middle = jnp.concatenate([f[:, :, y] for f in fields], axis=0)
        return [jnp.concatenate([xlo[:, y : y + 1], middle, xhi[:, y : y + 1]], axis=1)]

    one, two, is_even = exchanged(side(0), side(cells_y - 1), WIDE)
    ylo, yhi = jnp.where(is_even, two, one), jnp.where(is_even, one, two)

    rows = inverse_factor.shape[0]
    own = inverse_factor.reshape(rows, count, vectors).transpose(0, 2, 1).reshape(rows, count * vectors)

    held = lax.all_gather(own, ("z", "core"), tiled=True)

    (table,) = call(
        functools.partial(inner_kernel, done),
        [(8, 128)],
        [SMEM] + [VMEM] * 6,
        [pltpu.VMEM((3 * vectors, 8, 128), F32)],
        flops=30_000_000,
        moved=1_000_000,
        name="inner",
    )(couplings, zf, stiffness, mass, xlo, xhi, table)
    table, payload = call(
        outer_kernel,
        [(8, 128), (n_near, 1, SLOT * vectors)],
        [SMEM] + [VMEM] * 5,
        [pltpu.VMEM((6 * vectors, 8, 128), F32)],
        flops=10_000_000,
        moved=2_000_000,
        name="outer",
    )(couplings, table, zy, sy, ylo, yhi)
    got = lax.all_to_all(payload, ("narrow", "z"), 0, 0)
    got = lax.all_to_all(jnp.broadcast_to(got[None], (size_y,) + got.shape), "y", 0, 0)
    got, held = lax.optimization_barrier((got, held))
    other = lax.ppermute(got, "core", [(0, 1), (1, 0)])
    (local,) = call(
        local_kernel,
        [(3, cells_x, cells_y, depth)],
        [SMEM] + [VMEM] * 6,
        [pltpu.VMEM((3, cells_y + 2, 2, 8, depth // 2), F32)] * 2,
        flops=2_000_000,
        moved=3_000_000,
        name="local",
    )(ranges, local_inverse.transpose(0, 1, 3, 2, 4), rounded, xlo, xhi, ylo, yhi)

    group = ("narrow", "y")
    members = lax.axis_size(group)

    def spread(share):
        return lax.all_to_all(share, group, 0, 0)

    core = lax.axis_index("core").astype(jnp.int32).reshape(1)
    packed, rhs, share = call(
        functools.partial(first_kernel, n_narrow, size_z),
        [(SLOT * vectors, count), (vectors, count), (members, vectors, count)],
        [SMEM] + [VMEM] * 3,
        [pltpu.VMEM((count, SLOT * vectors), F32)],
        flops=2_000_000,
        moved=3_000_000,
        name="first",
    )(core, got, other, held)
    first, share = call(
        functools.partial(second_kernel, n_narrow),
        [(vectors, count), (members, vectors, count)],
        [VMEM] * 4,
        flops=2_000_000,
        moved=3_000_000,
        name="second",
    )(packed, rhs, spread(share), held)
    preconditioned, solved = call(
        last_kernel,
        [(3, cells_x, cells_y, depth), (vectors, count)],
        [SMEM] + [VMEM] * 4,
        flops=1_000_000,
        moved=1_000_000,
        name="last",
    )(ids, deflation, local, first, spread(share))
    coarse_solution = solved.T.reshape(-1)
    blocks = table[:, : 9 * vectors].reshape(vectors, 9, vectors).transpose(1, 0, 2)
    return preconditioned, blocks.reshape(1, 1, 9, vectors, vectors), coarse_solution


def solution(mesh):
    n_narrow, n_wide = mesh.devices.shape
    fine = jax.sharding.Mesh(mesh.devices.reshape(n_narrow, n_wide // 16, 8, 2), ("narrow",) + WIDE)
    placed = (
        P(None, None, "narrow", WIDE, None),
        P(None, "narrow", WIDE, None),
        P("narrow", WIDE, None),
        P("narrow", WIDE, None),
        P(),
        P(None, None, "narrow", WIDE, None),
        P(("narrow",) + WIDE, None),
        P("narrow", WIDE, None, None),
        P("narrow", WIDE, None),
    )
    return jax.shard_map(
        body,
        mesh=fine,
        in_specs=placed,
        out_specs=(P(None, "narrow", WIDE, None), P("narrow", WIDE, None, None, None), P()),
        check_vma=False,
    )
```

time: 112 us -> 97.7 us (0.87)
  starting transfers between devices: 55.9 us -> 10.7 us
  blocking collectives: 0 us -> 43.4 us
  waiting for transfers between devices: 31 us -> 6.23 us
  between operations: 1.06 us -> 14.4 us
  local copies, waits for them, and re-layouts: 8.53 us -> 6.06 us
    all_to_all x0 -> x3, blocking collectives: none -> 43.4 us  [the longest x1 21.1 us: body(): got = lax.all_to_all(payload, ('narrow', 'z'), 0, 0)]
    ppermute x19 -> x5, starting transfers between devices: 38.8 us -> 5.58 us  [the longest x2 3.13 us: exchanged(): two = lax.ppermute(chosen(sending_low, sending_high), axis, odd)]
    ppermute x19 -> x5, waiting for transfers between devices: 14.8 us -> 1.64 us  [the longest x1 1.63 us: body(): other = lax.ppermute(got, 'core', [(0, 1), (1, 0)])]
    all_to_all x1, starting transfers between devices: 17.1 us -> 5.05 us  [spread(): return lax.all_to_all(share, group, 0, 0)]
    all_to_all x1, waiting for transfers between devices: 16.2 us -> 4.57 us  [spread(): return lax.all_to_all(share, group, 0, 0)]
    all_to_all x1 -> x0, local copies, waits for them, and re-layouts: 1.54 us -> none  [body(): got = lax.all_to_all(payload, AXES, 0, 0, tiled=True)]
    unnamed x24 -> x26, local copies, waits for them, and re-layouts: 3.91 us -> 3.06 us
    pallas_call x4 -> x5, Pallas kernels: 12.6 us -> 13 us  [the longest x1 4.54 us: body(): call(functools.partial(inner_kernel, done), [(8, 128)], [SMEM] + [VMEM] *...]
  transfers between devices with their start and end apart: 20 -> 7, of which waited for: 6 -> 2; matrix products, arithmetic and copies ran while one was open for 6% -> 3% of each run, Pallas kernels for 9% -> 12%
where the time goes in v2:
time: 97.7 us; the launch traced here: 97 us
  blocking collectives  43.4 us (44%)
  Pallas kernels  15.2 us (16%)
  between operations  14.4 us (15%)
  starting transfers between devices  10.7 us (11%)
  waiting for transfers between devices  6.23 us (6%)
  local copies, waits for them, and re-layouts  6.06 us (6%)
  other arithmetic  1.05 us (1%)
    all_to_all x1, blocking collectives, body(): got = lax.all_to_all(payload, ('narrow', 'z'), 0, 0)  21.1 us
    all_to_all x1, blocking collectives, body(): lax.all_to_all(jnp.broadcast_to(got[None], (size_y,) + got.shape), 'y', 0...  11.4 us
    all_to_all x1, blocking collectives, spread(): return lax.all_to_all(share, group, 0, 0)  10.9 us
    all_to_all x1, starting transfers between devices, spread(): return lax.all_to_all(share, group, 0, 0)  5.05 us
    all_to_all x1, waiting for transfers between devices, spread(): return lax.all_to_all(share, group, 0, 0)  4.57 us
    pallas_call x1, Pallas kernels, body(): call(functools.partial(inner_kernel, done), [(8, 128)], [SMEM] + [VMEM] *...  4.54 us
    pallas_call x1, Pallas kernels, body(): call(functools.partial(before_kernel, done), [(vectors, 3, cells_x, cells...  3.3 us
    ppermute x2, starting transfers between devices, exchanged(): two = lax.ppermute(chosen(sending_low, sending_high), axis, odd)  3.13 us
  transfers between devices with their start and end apart: 7, of which 2 were waited for; matrix products, arithmetic and copies ran while one was open for 3% of the time, Pallas kernels for 12%

profile of v2, /device:TPU:2, one launch (start us, length us, event | category | flops | bytes accessed | tf_op | source)
XLA Modules:
  0.0 97.0 jit_solution(17071600287997486076)
XLA Ops:
  7.2 0.0 all-gather.2.cloned.1.call-start
  7.2 1.0 %copy.21 = bf16[8,3,4,8,256]{4,3,1,0,2:T(8,128)(2,1)S(1)} copy(bf16[8,3,4,8,256]{4,3,2,1,0:T(8,128)(2,1)} %z_ref.3) | data formatting | bytes 786432 | tf_op args[0]
  8.3 0.8 select_bitcast_fusion.2
  9.1 0.0 copy-start.8
  9.1 2.4 %collective-permute-start = (bf16[27,8,256]{2,1,0:T(8,128)(2,1)S(1)}, bf16[27,8,256]{2,1,0:T(8,128)(2,1)S(1)}, u32[]{:S(2)}, u32[]{:S(2)}) collective-permute-start(bf16[27,8,256]{2,1,0:T(8,128)(2,1)S(1)} %pad_maximum_fusion), channel_id=1, source_target_pairs={{0,64},{64,0},{128,192},{192,128},{1,65},{65,1},{129,193},{193,129... | collective-permute-start | bytes 331784 | tf_op jit(solution)/shard_map/ppermute | solution.py:406
  11.5 0.0 copy-start.2
  11.5 0.0 copy-start.4
  11.5 0.0 copy-start.5
  11.5 0.0 copy-start.6
  11.5 0.0 copy-start.7
  11.5 2.5 %collective-permute-start.1 = (bf16[27,8,256]{2,1,0:T(8,128)(2,1)S(1)}, bf16[27,8,256]{2,1,0:T(8,128)(2,1)S(1)}, u32[]{:S(2)}, u32[]{:S(2)}) collective-permute-start(bf16[27,8,256]{2,1,0:T(8,128)(2,1)S(1)} %pad_maximum_fusion.1), channel_id=1, source_target_pairs={{64,128},{128,64},{65,129},{129,65},{66,130},{130,66},{67,131},{13... | collective-permute-start | bytes 331784 | tf_op jit(solution)/shard_map/ppermute | solution.py:407
  14.0 0.6 reshape.48
  14.6 0.9 copy.28
  15.5 0.0 all-gather.2.cloned.1.call-update
  15.5 0.1 fusion
  15.7 0.1 copy_bitcast_fusion.1
  15.9 3.3 %before.1 = (f32[8,3,4,8,256]{4,3,2,1,0:T(8,128)S(1)}, f32[2,8,3,8,256]{4,3,2,1,0:T(8,128)S(1)}, f32[2,8,256]{2,1,0:T(8,128)S(1)}, f32[8,128]{1,0:T(8,128)S(1)}) custom-call(f32[3,3,27]{2,1,0:T(4,128)S(1)} %bitcast.32, s32[9]{0:T(128)S(1)} %bitcast.37, bf16[8,3,4,8,256]{4,3,2,1,0:T(8,128)(2,1)S(1)} %copy-done.2, bf16[3,4,8,256]{3,2,1,0:T(8,128)(2,1)S(1)} %copy.27.r_ref, ...), custom_call_target="tpu_custom_call" | custom-call | flops 20000000 | bytes 1000000 | tf_op jit(solution)/shard_map/before/pallas_call | solution.py:415
  19.2 0.0 collective-permute-done
  19.2 0.0 collective-permute-done.1
  19.3 0.1 fusion.1
  19.3 0.2 broadcast_select_fusion.2
  19.6 0.1 collective-permute-start.3
  19.7 0.7 collective-permute-start.2
  20.3 4.5 %inner.1.table_ref = f32[8,128]{1,0:T(8,128)S(1)} custom-call(f32[3,3,27]{2,1,0:T(4,128)S(1)} %bitcast.33, f32[8,3,4,8,256]{4,3,2,1,0:T(8,128)S(1)} %get-tuple-element.24.zf_ref, f32[4,8,256]{2,1,0:T(8,128)S(1)} %copy-done.4, f32[4,8,256]{2,1,0:T(8,128)S(1)} %copy-done.5, bf16[27,8,256]{2,1,0:T(8,128)(2,1)S(1)} %get-tuple-element.51.xlo_ref, ...), custom_call_target="tpu_custom_call" | custom-call | flops 30000000 | bytes 1000000 | tf_op jit(solution)/shard_map/inner/pallas_call | solution.py:439
  24.9 0.0 collective-permute-done.3
  24.9 0.0 collective-permute-done.2
  24.9 2.6 %outer.1 = (f32[8,128]{1,0:T(8,128)S(1)}, f32[32,1,640]{2,1,0:T(1,128)S(1)}) custom-call(f32[3,3,27]{2,1,0:T(4,128)S(1)} %bitcast.34, f32[8,128]{1,0:T(8,128)S(1)} %inner.1.table_ref, f32[2,8,3,8,256]{4,3,2,1,0:T(8,128)S(1)} %get-tuple-element.26.zy_ref, f32[2,8,256]{2,1,0:T(8,128)S(1)} %get-tuple-element.27.sy_ref, ...), custom_call_target="tpu_custom_call" | custom-call | flops 10000000 | bytes 2000000 | tf_op jit(solution)/shard_map/outer/pallas_call | solution.py:448
  27.5 21.1 %all_to_all.20 = f32[32,1,640]{2,1,0:T(1,128)S(1)} all-to-all(f32[32,1,640]{2,1,0:T(1,128)S(1)} %get-tuple-element.28), channel_id=1, replica_groups=mesh['narrow'=4,'y'=4,'z'=8,'core'=2] {'narrow','z'}, dimensions={0} | all-to-all | bytes 163840 | tf_op jit(solution)/shard_map/all_to_all | solution.py:457
  48.6 0.2 broadcast_in_dim.9
  48.8 11.4 %all_to_all.21.own_ref = f32[4,32,1,640]{3,2,1,0:T(1,128)S(1)} all-to-all(f32[4,32,1,640]{3,2,1,0:T(1,128)S(1)} %broadcast_in_dim.9), channel_id=1, replica_groups=mesh['narrow'=4,'y'=4,'z'=8,'core'=2] {'y'}, dimensions={0} | all-to-all | bytes 655360 | tf_op jit(solution)/shard_map/all_to_all | solution.py:458
  60.2 0.0 collective-permute-start.4
  60.2 1.6 %collective-permute-done.4.other_ref = f32[4,32,1,640]{3,2,1,0:T(1,128)S(1)} collective-permute-done((f32[4,32,1,640]{3,2,1,0:T(1,128)S(1)}, f32[4,32,1,640]{3,2,1,0:T(1,128)S(1)}, u32[]{:S(2)}, u32[]{:S(2)}) %collective-permute-start.4) | collective-permute-done | bytes 327712 | tf_op jit(solution)/shard_map/ppermute | solution.py:460
  61.9 1.2 %copy-done = f32[128,2048]{1,0:T(8,128)S(1)} copy-done((f32[128,2048]{1,0:T(8,128)S(1)}, f32[128,2048]{1,0:T(8,128)}, u32[]{:S(2)}) %copy-start) | copy-done | bytes 1048600
  63.1 1.0 first.1
  64.1 0.0 copy-start.10
  64.1 0.0 copy-start.3
  64.1 10.9 %all_to_all.22.parts_ref = f32[16,8,256]{2,1,0:T(8,128)S(1)} all-to-all(f32[16,8,256]{2,1,0:T(8,128)S(1)} %get-tuple-element.33), channel_id=1, replica_groups=mesh['narrow'=4,'y'=4,'z'=8,'core'=2] {'narrow','y'}, dimensions={0} | all-to-all | bytes 262144 | tf_op jit(solution)/shard_map/all_to_all | solution.py:475
  75.0 1.6 %second.1 = (f32[8,256]{1,0:T(8,128)S(1)}, f32[16,8,256]{2,1,0:T(8,128)}) custom-call(f32[640,256]{1,0:T(8,128)S(1)} %get-tuple-element.31.packed_ref, f32[8,256]{1,0:T(8,128)S(1)} %get-tuple-element.32.rhs_ref, f32[16,8,256]{2,1,0:T(8,128)S(1)} %all_to_all.22.parts_ref, f32[128,2048]{1,0:T(8,128)S(1)} %copy-done.1), custom_call_target="tpu_custom_call" | custom-call | flops 2000000 | bytes 3000000 | tf_op jit(solution)/shard_map/second/pallas_call | solution.py:487
  76.6 5.1 %all-to-all-start.3 = ((f32[16,8,256]{2,1,0:T(8,128)}), f32[16,8,256]{2,1,0:T(8,128)S(1)}, u32[]{:S(2)}, u32[]{:S(2)}) async-start(f32[16,8,256]{2,1,0:T(8,128)} %get-tuple-element.35), calls=%async_computation.3 | async-start | bytes 262144 | tf_op jit(solution)/shard_map/all_to_all | solution.py:475
  81.6 0.0 copy-done.10
  81.6 0.1 reshape.45.range_ref
  81.7 0.1 reshape.50
  81.8 0.7 copy.30
  82.5 0.9 local.1.local_ref
  83.4 4.6 %all-to-all-done.3.parts_ref = f32[16,8,256]{2,1,0:T(8,128)S(1)} async-done(((f32[16,8,256]{2,1,0:T(8,128)}), f32[16,8,256]{2,1,0:T(8,128)S(1)}, u32[]{:S(2)}, u32[]{:S(2)}) %all-to-all-start.3) | async-done | bytes 131104 | tf_op jit(solution)/shard_map/all_to_all | solution.py:475
  88.0 1.3 %last.1 = (f32[3,4,8,256]{3,2,1,0:T(8,128)}, f32[8,256]{1,0:T(8,128)S(1)}) custom-call(s32[9]{0:T(128)S(1)} %bitcast.38, bf16[8,3,4,8,256]{4,3,2,1,0:T(8,128)(2,1)S(1)} %copy-done.2, f32[3,4,8,256]{3,2,1,0:T(8,128)S(1)} %local.1.local_ref, f32[8,256]{1,0:T(8,128)S(1)} %get-tuple-element.34.first_ref, f32[16,8,256]{2,1,0:T(8,128)S(1)} %all-to-all-done.3.parts_ref), custom_call_target="tpu_custom_call" | custom-call | flops 1000000 | bytes 1000000 | tf_op jit(solution)/shard_map/last/pallas_call | solution.py:495
  89.3 0.1 copy.29
  89.5 0.7 reshape.52
  (23 shorter events, 0.2 us)
Async XLA Ops:
  7.2 6.8 %copy-start.9 = (f32[8,2048]{1,0:T(8,128)S(1)}, f32[8,2048]{1,0:T(8,128)}, u32[]{:S(2)}) copy-start(f32[8,2048]{1,0:T(8,128)} %param.15) | copy-start | bytes 196612
  7.2 53.1 %all-gather.2.cloned.1.call-start = ((), (), s32[]{:S(2)}) async-start(), calls=%async_computation.4 | async-start | bytes 1114112 | tf_op jit(solution)/shard_map/all_gather | solution.py:437
  9.1 6.6 %copy-start.8 = (f32[3,4,8,256]{3,2,1,0:T(8,128)S(1)}, f32[3,4,8,256]{3,2,1,0:T(8,128)}, u32[]{:S(2)}) copy-start(f32[3,4,8,256]{3,2,1,0:T(8,128)} %param.10) | copy-start | bytes 294916
  9.1 10.1 %collective-permute-start = (bf16[27,8,256]{2,1,0:T(8,128)(2,1)S(1)}, bf16[27,8,256]{2,1,0:T(8,128)(2,1)S(1)}, u32[]{:S(2)}, u32[]{:S(2)}) collective-permute-start(bf16[27,8,256]{2,1,0:T(8,128)(2,1)S(1)} %pad_maximum_fusion), channel_id=1, source_target_pairs={{0,64},{64,0},{128,192},{192,128},{1,65},{65,1},{129,193},{193,129... | collective-permute-start | bytes 331784 | tf_op jit(solution)/shard_map/ppermute | solution.py:406
  11.5 4.4 %copy-start.2 = (bf16[8,3,4,8,256]{4,3,2,1,0:T(8,128)(2,1)S(1)}, bf16[8,3,4,8,256]{4,3,2,1,0:T(8,128)(2,1)}, u32[]{:S(2)}) copy-start(bf16[8,3,4,8,256]{4,3,2,1,0:T(8,128)(2,1)} %z_ref.3) | copy-start | bytes 1179652
  11.5 4.4 %copy-start.4 = (f32[4,8,256]{2,1,0:T(8,128)S(1)}, f32[4,8,256]{2,1,0:T(8,128)}, u32[]{:S(2)}) copy-start(f32[4,8,256]{2,1,0:T(8,128)} %stiff_ref.3) | copy-start | bytes 98308
  11.5 4.4 %copy-start.5 = (f32[4,8,256]{2,1,0:T(8,128)S(1)}, f32[4,8,256]{2,1,0:T(8,128)}, u32[]{:S(2)}) copy-start(f32[4,8,256]{2,1,0:T(8,128)} %mass_ref.3) | copy-start | bytes 98308
  11.5 4.4 %copy-start.6 = (f32[27,3,3]{0,2,1:T(4,128)S(1)}, f32[27,3,3]{0,2,1:T(4,128)}, u32[]{:S(2)}) copy-start(f32[27,3,3]{0,2,1:T(4,128)} %param.13) | copy-start | bytes 2920
  11.5 4.4 %copy-start.7 = (s32[1,1,9]{2,1,0:T(1,128)S(1)}, s32[1,1,9]{2,1,0:T(1,128)}, u32[]{:S(2)}) copy-start(s32[1,1,9]{2,1,0:T(1,128)} %param.17) | copy-start | bytes 112
  11.5 7.7 %collective-permute-start.1 = (bf16[27,8,256]{2,1,0:T(8,128)(2,1)S(1)}, bf16[27,8,256]{2,1,0:T(8,128)(2,1)S(1)}, u32[]{:S(2)}, u32[]{:S(2)}) collective-permute-start(bf16[27,8,256]{2,1,0:T(8,128)(2,1)S(1)} %pad_maximum_fusion.1), channel_id=1, source_target_pairs={{64,128},{128,64},{65,129},{129,65},{66,130},{130,66},{67,131},{13... | collective-permute-start | bytes 331784 | tf_op jit(solution)/shard_map/ppermute | solution.py:407
  19.6 5.3 %collective-permute-start.3 = (bf16[27,6,256]{2,1,0:T(8,128)(2,1)S(1)}, bf16[27,6,256]{2,1,0:T(8,128)(2,1)S(1)}, u32[]{:S(2)}, u32[]{:S(2)}) collective-permute-start(bf16[27,6,256]{2,1,0:T(8,128)(2,1)S(1)} %get-tuple-element.48), channel_id=1, source_target_pairs={{0,1},{1,0},{2,3},{3,2},{4,5},{5,4},{6,7},{7,6},{8,9},{9,8},{10,11... | collective-permute-start | bytes 248840 | tf_op jit(solution)/shard_map/ppermute | solution.py:406
  19.7 5.2 %collective-permute-start.2 = (bf16[27,6,256]{2,1,0:T(8,128)(2,1)S(1)}, bf16[27,6,256]{2,1,0:T(8,128)(2,1)S(1)}, u32[]{:S(2)}, u32[]{:S(2)}) collective-permute-start(bf16[27,6,256]{2,1,0:T(8,128)(2,1)S(1)} %get-tuple-element.49), channel_id=1, source_target_pairs={{1,2},{2,1},{3,4},{4,3},{5,6},{6,5},{7,8},{8,7},{9,10},{10,9},{11,... | collective-permute-start | bytes 248840 | tf_op jit(solution)/shard_map/ppermute | solution.py:407
  60.2 1.6 %collective-permute-start.4 = (f32[4,32,1,640]{3,2,1,0:T(1,128)S(1)}, f32[4,32,1,640]{3,2,1,0:T(1,128)S(1)}, u32[]{:S(2)}, u32[]{:S(2)}) collective-permute-start(f32[4,32,1,640]{3,2,1,0:T(1,128)S(1)} %all_to_all.21.own_ref), channel_id=1, source_target_pairs={{0,1},{1,0},{2,3},{3,2},{4,5},{5,4},{6,7},{7,6},{8,9},{9,8},{10,11... | collective-permute-start | bytes 983048 | tf_op jit(solution)/shard_map/ppermute | solution.py:460
  61.9 1.2 %copy-start = (f32[128,2048]{1,0:T(8,128)S(1)}, f32[128,2048]{1,0:T(8,128)}, u32[]{:S(2)}) copy-start(f32[128,2048]{1,0:T(8,128)} %all-gather.2.cloned.1.call-done.piece) | copy-start | bytes 3145732
  63.1 11.9 %copy-start.1 = (f32[128,2048]{1,0:T(8,128)S(1)}, f32[128,2048]{1,0:T(8,128)}, u32[]{:S(2)}) copy-start(f32[128,2048]{1,0:T(8,128)} %all-gather.2.cloned.1.call-done.piece) | copy-start | bytes 3145732
  64.1 17.5 %copy-start.10 = (s32[1,1,2,2]{3,2,1,0:T(2,128)S(1)}, s32[1,1,2,2]{3,2,1,0:T(2,128)}, u32[]{:S(2)}) copy-start(s32[1,1,2,2]{3,2,1,0:T(2,128)} %param.16) | copy-start | bytes 52
  64.1 18.4 %copy-start.3 = (bf16[12,12,3,5,256]{4,2,3,1,0:T(4,128)(2,1)S(1)}, bf16[12,12,3,5,256]{4,2,3,1,0:T(4,128)(2,1)}, u32[]{:S(2)}) copy-start(bf16[12,12,3,5,256]{4,2,3,1,0:T(4,128)(2,1)} %param.14) | copy-start | bytes 3317764
  76.6 11.4 %all-to-all-start.3 = ((f32[16,8,256]{2,1,0:T(8,128)}), f32[16,8,256]{2,1,0:T(8,128)S(1)}, u32[]{:S(2)}, u32[]{:S(2)}) async-start(f32[16,8,256]{2,1,0:T(8,128)} %get-tuple-element.35), calls=%async_computation.3 | async-start | bytes 262144 | tf_op jit(solution)/shard_map/all_to_all | solution.py:475
Sparse Core Ops, SparseCore 0:
  15.7 40.1 all-gather.1

commit v3 on v2

--- a/solution.py
+++ b/solution.py
@@ -36,39 +36,72 @@
     return jnp.sum(total, axis=1, keepdims=True)
 
 
-def centre_rows(b, s_ref, zf_ref, stiff_ref, mass_ref, rows_ref, place):
-    vectors, _, cells_x = zf_ref.shape[:3]
-    field = [[zf_ref[b, j, x] for x in range(cells_x)] for j in range(3)]
-    weighted = []
-    for i in range(3):
-        image = [None] * cells_x
-        for oz in (-1, 0, 1):
-            level = [None] * cells_x
+def halved(value):
+    high = value.astype(jnp.bfloat16)
+    return high, (value - high.astype(F32)).astype(jnp.bfloat16)
+
+
+def laid(s_ref, out_ref, begin, rows, choices):
+    value = jnp.zeros((rows, 128), F32)
+    for mask, which in choices:
+        value = jnp.where(mask, entry(s_ref, *which), value)
+    high, low = halved(value)
+    out_ref[begin : begin + rows, :128] = high
+    out_ref[begin : begin + rows, 128:] = low
+
+
+def matrices(s_ref, own_ref, x_ref, y_ref, cells_x, cells_y):
+    rows = cells_x * cells_y
+    row = lax.broadcasted_iota(jnp.int32, (rows, 128), 0)
+    col = lax.broadcasted_iota(jnp.int32, (rows, 128), 1)
+    dx = col // cells_y % cells_x - row // cells_y
+    dy = col % cells_y - row % cells_y
+    masks = []
+    for j in range(3):
+        for ox in (-1, 0, 1):
             for oy in (-1, 0, 1):
-                for x in range(cells_x):
-                    acc = None
-                    for ox in (-1, 0, 1):
-                        if 0 <= x + ox < cells_x:
-                            for j in range(3):
-                                term = entry(s_ref, ox, oy, oz, i, j) * field[j][x + ox]
-                                acc = term if acc is None else acc + term
-                    acc = shifted(acc, oy, 0)
-                    level[x] = acc if level[x] is None else level[x] + acc
-            for x in range(cells_x):
-                moved = shifted(level[x], oz, 1)
-                image[x] = moved if image[x] is None else image[x] + moved
-        weighted.append([stiff_ref[x] * image[x] + mass_ref[x] * field[i][x] for x in range(cells_x)])
-    for a in range(vectors):
-        total = None
+                masks.append((j, ox, oy, (col // rows == j) & (dx == ox) & (dy == oy)))
+    for oz in (-1, 0, 1):
         for i in range(3):
-            for x in range(cells_x):
-                term = zf_ref[a, i, x] * weighted[i][x]
-                total = term if total is None else total + term
-        rows_ref[place, a : a + 1, :] = rows_sum(total)
+            choices = [(mask, (ox, oy, oz, i, j)) for j, ox, oy, mask in masks]
+            laid(s_ref, own_ref, ((oz + 1) * 3 + i) * rows, rows, choices)
+    row = lax.broadcasted_iota(jnp.int32, (8, 128), 0)
+    col = lax.broadcasted_iota(jnp.int32, (8, 128), 1)
+    at = col % 8
+    for oz in (-1, 0, 1):
+        for face in range(2):
+            side = 2 * face - 1
+            here = [col // 8 == face * 3 + j for j in range(3)]
+            for i in range(3):
+                choices = [
+                    (here[j] & (at - row == oy), (side, oy, oz, i, j)) for j in range(3) for oy in (-1, 0, 1)
+                ]
+                laid(s_ref, x_ref, (((oz + 1) * 2 + face) * 3 + i) * 8, 8, choices)
+                inside = (row < cells_x) & (at >= 1) & (at <= cells_x)
+                choices = [
+                    (here[j] & inside & (at - 1 - row == ox), (ox, side, oz, i, j))
+                    for j in range(3)
+                    for ox in (-1, 0, 1)
+                ]
+                laid(s_ref, y_ref, ((((oz + 1) * 2 + face) * 2) * 3 + i) * 8, 8, choices)
+                choices = []
+                for j in range(3):
+                    choices.append((here[j] & (row == 0) & (at == 0), (-1, side, oz, i, j)))
+                    choices.append((here[j] & (row == cells_x - 1) & (at == cells_x + 1), (1, side, oz, i, j)))
+                laid(s_ref, y_ref, ((((oz + 1) * 2 + face) * 2 + 1) * 3 + i) * 8, 8, choices)
+
+
+def images(matrix, cells):
+    blank = jnp.zeros((128 - cells.shape[0], cells.shape[1]), F32)
+    twice = jnp.concatenate([cells, blank, cells, blank], axis=0).astype(jnp.bfloat16)
+    result = jnp.dot(matrix, twice, preferred_element_type=F32)
+    third = result.shape[0] // 3
+    low, mid, high = result[:third], result[third : 2 * third], result[2 * third :]
+    return shifted(low, -1, 1) + mid + shifted(high, 1, 1)
 
 
 def before_kernel(
-    done, s_ref, ids_ref, z_ref, r_ref, stiff_ref, mass_ref, zf_ref, zy_ref, sy_ref, table_ref, rows_ref
+    s_ref, ids_ref, z_ref, r_ref, stiff_ref, zf_ref, zy_ref, sy_ref, table_ref, own_ref, x_ref, y_ref, rows_ref
 ):
     vectors, _, cells_x, cells_y, depth = z_ref.shape
     own_y = (0, cells_y - 1)
@@ -76,6 +109,8 @@
 
     def columns(rows):
         return jnp.concatenate(rows + [blank], axis=0)
+
+    matrices(s_ref, own_ref, x_ref, y_ref, cells_x, cells_y)
 
     def convert(a, carry):
         for i in range(3):
@@ -95,91 +130,67 @@
             for x in range(cells_x):
                 term = zf_ref[a, i, x] * r_ref[i, x].astype(F32)
                 total = term if total is None else total + term
-        rows_ref[done, a : a + 1, :] = rows_sum(total)
-
-    def one(b, carry):
-        centre_rows(b, s_ref, zf_ref, stiff_ref, mass_ref, rows_ref, b)
-        return carry
-
-    lax.fori_loop(0, done, one, 0)
+        rows_ref[0, a : a + 1, :] = rows_sum(total)
+
     lane = lax.broadcasted_iota(jnp.int32, (8, 128), 1)
     table = jnp.where(lane == 9 * vectors + 1, ids_ref[4].astype(F32), 0.0)
-    table = jnp.where(lane == 9 * vectors, faces(rows_ref[done]), table)
-    for b in range(done):
-        table = jnp.where(lane == 4 * vectors + b, faces(rows_ref[b]), table)
-    table_ref[...] = table
-
-
-def inner_kernel(done, s_ref, zf_ref, stiff_ref, mass_ref, xlo_ref, xhi_ref, before_ref, table_ref, rows_ref):
-    vectors, _, cells_x = zf_ref.shape[:3]
+    table_ref[...] = jnp.where(lane == 9 * vectors, faces(rows_ref[0]), table)
+
+
+def inner_kernel(
+    own_ref, x_ref, zf_ref, stiff_ref, mass_ref, xlo_ref, xhi_ref, before_ref, table_ref, rows_ref
+):
+    vectors, _, cells_x, cells_y, depth = zf_ref.shape
     own_x = (0, cells_x - 1)
 
     def one(b, carry):
-        centre_rows(b, s_ref, zf_ref, stiff_ref, mass_ref, rows_ref, vectors + b)
-        return carry
-
-    lax.fori_loop(done, vectors, one, 0)
-
-    def other(b, carry):
-        for face, halo_ref in ((0, xlo_ref), (1, xhi_ref)):
-            ox = 2 * face - 1
-            field = [halo_ref[b * 3 + j].astype(F32) for j in range(3)]
+        cells = zf_ref[b].reshape(3 * cells_x * cells_y, depth)
+        image = images(own_ref[...], cells).reshape(3, cells_x, cells_y, depth)
+        weighted = [
+            [stiff_ref[x] * image[i, x] + mass_ref[x] * zf_ref[b, i, x] for x in range(cells_x)] for i in range(3)
+        ]
+        for a in range(vectors):
+            total = None
+            for i in range(3):
+                for x in range(cells_x):
+                    term = zf_ref[a, i, x] * weighted[i][x]
+                    total = term if total is None else total + term
+            rows_ref[vectors + b, a : a + 1, :] = rows_sum(total)
+        cells = [halo_ref[b * 3 + j].astype(F32) for halo_ref in (xlo_ref, xhi_ref) for j in range(3)]
+        image = images(x_ref[...], jnp.concatenate(cells, axis=0))
+        for face in range(2):
             stiff = stiff_ref[own_x[face]]
-            weighted = []
-            for i in range(3):
-                image = None
-                for oz in (-1, 0, 1):
-                    level = None
-                    for oy in (-1, 0, 1):
-                        acc = sum(entry(s_ref, ox, oy, oz, i, j) * field[j] for j in range(3))
-                        acc = shifted(acc, oy, 0)
-                        level = acc if level is None else level + acc
-                    moved = shifted(level, oz, 1)
-                    image = moved if image is None else image + moved
-                weighted.append(stiff * image)
+            weighted = [stiff * image[(face * 3 + i) * 8 : (face * 3 + i + 1) * 8] for i in range(3)]
             for a in range(vectors):
                 total = sum(zf_ref[a, i, own_x[face]] * weighted[i] for i in range(3))
                 rows_ref[2 * face * vectors + b, a : a + 1, :] = rows_sum(total)
         return carry
 
-    lax.fori_loop(0, vectors, other, 0)
+    lax.fori_loop(0, vectors, one, 0, unroll=4)
     lane = lax.broadcasted_iota(jnp.int32, (8, 128), 1)
     table = before_ref[...]
     for place, number in enumerate((1, 4, 7)):
-        for b in range(done if number == 4 else 0, vectors):
+        for b in range(vectors):
             table = jnp.where(lane == number * vectors + b, faces(rows_ref[place * vectors + b]), table)
     table_ref[...] = table
 
 
-def outer_kernel(s_ref, table_ref, zy_ref, sy_ref, ylo_ref, yhi_ref, blocks_ref, pay_ref, rows_ref):
+def outer_kernel(y_ref, table_ref, zy_ref, sy_ref, ylo_ref, yhi_ref, blocks_ref, pay_ref, rows_ref):
     vectors, depth = zy_ref.shape[1], zy_ref.shape[4]
     cells_x = ylo_ref.shape[1] - 2
-    row = lax.broadcasted_iota(jnp.int32, (8, depth), 0)
+    pad = jnp.zeros((8 - ylo_ref.shape[1], depth), F32)
 
     def one(b, carry):
-        for face, halo_ref in ((0, ylo_ref), (1, yhi_ref)):
-            oy = 2 * face - 1
-            pad = jnp.zeros((8 - halo_ref.shape[1], depth), F32)
-            field = [jnp.concatenate([halo_ref[b * 3 + j].astype(F32), pad], axis=0) for j in range(3)]
+        cells = []
+        for halo_ref in (ylo_ref, yhi_ref):
+            for j in range(3):
+                cells += [halo_ref[b * 3 + j].astype(F32), pad]
+        image = images(y_ref[...], jnp.concatenate(cells, axis=0))
+        for face in range(2):
             stiff = sy_ref[face]
-            inner, outer = [], []
-            for i in range(3):
-                mid, rim = None, None
-                for ox in (-1, 0, 1):
-                    line = None
-                    for oz in (-1, 0, 1):
-                        acc = sum(entry(s_ref, ox, oy, oz, i, j) * field[j] for j in range(3))
-                        acc = shifted(acc, oz, 1)
-                        line = acc if line is None else line + acc
-                    moved = pltpu.roll(line, (-(1 + ox)) % 8, 0) if ox != -1 else line
-                    low, high = max(0, -ox), min(cells_x, cells_x - ox)
-                    part = jnp.where((row >= low) & (row < high), moved, 0.0)
-                    mid = part if mid is None else mid + part
-                    if ox != 0:
-                        edge = jnp.where(row == (0 if ox == -1 else cells_x - 1), moved, 0.0)
-                        rim = edge if rim is None else rim + edge
-                inner.append(stiff * mid)
-                outer.append(stiff * rim)
+            begin = face * 6
+            inner = [stiff * image[(begin + i) * 8 : (begin + i + 1) * 8] for i in range(3)]
+            outer = [stiff * image[(begin + 3 + i) * 8 : (begin + 4 + i) * 8] for i in range(3)]
             for a in range(vectors):
                 own = [zy_ref[face, a, i] for i in range(3)]
                 total = sum(own[i] * inner[i] for i in range(3))
@@ -190,7 +201,7 @@
                 rows_ref[(3 * face + 2) * vectors + b, a : a + 1, :] = half[cells_x - 1 : cells_x, :]
         return carry
 
-    lax.fori_loop(0, vectors, one, 0)
+    lax.fori_loop(0, vectors, one, 0, unroll=8)
     lane = lax.broadcasted_iota(jnp.int32, (8, 128), 1)
     table = table_ref[...]
     for place, number in enumerate((0, 3, 6, 2, 5, 8)):
@@ -255,36 +266,44 @@
     return (result[0:8] + result[8:16]) + result[16:24]
 
 
-def slots_of(packed_ref):
-    count = packed_ref.shape[1]
-    ids = packed_ref[73:74, :].astype(jnp.int32)
-    return (lax.broadcasted_iota(jnp.int32, (count, count), 0) == ids).astype(F32).astype(jnp.bfloat16)
-
-
-def share_of(vector, piece):
-    line = jnp.concatenate([vector[b : b + 1, :] for b in range(8)], axis=1)
-    line = jnp.broadcast_to(line, (8, line.shape[1]))
+def lines_of(flat):
+    size = flat.shape[0]
+    return jnp.concatenate([jnp.broadcast_to(flat[q : q + 1, :], (8, 128)) for q in range(size)], axis=1)
+
+
+def flat_of(by_vector):
+    at = lax.broadcasted_iota(jnp.int32, by_vector.shape, 1)
+    row = lax.broadcasted_iota(jnp.int32, by_vector.shape, 0)
+    line = jnp.sum(jnp.where(at % 8 == row, by_vector, 0.0), axis=0, keepdims=True)
+    return folded(line)
+
+
+def folded(line):
+    return jnp.concatenate([line[:, q * 128 : (q + 1) * 128] for q in range(line.shape[1] // 128)], axis=0)
+
+
+def share_of(flat, pieces):
+    line = lines_of(flat)
     acc = jnp.zeros(line.shape, F32)
     group = 4
-
-    def step(t, acc):
-        tiles, inner = [], []
-        for q in range(group):
-            tile = piece[pl.ds(pl.multiple_of((t * group + q) * 8, 8), 8), :]
-            tiles.append(tile)
-            inner.append(jnp.sum(tile * line, axis=1, keepdims=True))
-        for tile, value in zip(tiles, inner):
-            acc = acc + tile * value
-        return acc
-
-    acc = lax.fori_loop(0, piece.shape[0] // 8 // group, step, acc)
-    total = jnp.sum(acc, axis=0, keepdims=True)
-    blocks = vector.shape[1]
-    return jnp.concatenate([total[:, b * blocks : (b + 1) * blocks] for b in range(8)], axis=0)
-
-
-def first_kernel(
-    n_narrow, size_z, core_ref, own_ref, other_ref, piece, packed_ref, rhs_ref, share_ref, rows_ref
+    for piece in pieces:
+
+        def step(t, acc, piece=piece):
+            tiles, inner = [], []
+            for q in range(group):
+                tile = piece[pl.ds(pl.multiple_of((t * group + q) * 8, 8), 8), :]
+                tiles.append(tile)
+                inner.append(jnp.sum(tile * line, axis=1, keepdims=True))
+            for tile, value in zip(tiles, inner):
+                acc = acc + tile * value
+            return acc
+
+        acc = lax.fori_loop(0, piece.shape[0] // 8 // group, step, acc)
+    return folded(jnp.sum(acc, axis=0, keepdims=True))
+
+
+def gathered_kernel(
+    n_narrow, size_z, core_ref, own_ref, other_ref, packed_ref, slots_ref, rhs_ref, rows_ref
 ):
     size_y = own_ref.shape[0]
     chips = n_narrow * size_y * size_z
@@ -294,11 +313,18 @@
                 place = pl.multiple_of(core * chips + (x * size_y + y) * size_z, 8)
                 block = got_ref[y, x * size_z : (x + 1) * size_z]
                 rows_ref[pl.ds(place, size_z), :] = block.reshape(size_z, block.shape[2])
-    packed_ref[...] = rows_ref[...].T
-    own = jnp.concatenate([packed_ref[a * SLOT + 72 : a * SLOT + 73, :] for a in range(8)], axis=0)
-    rhs = moved_by(own, slots_of(packed_ref), ((1,), (1,)))
-    rhs_ref[...] = rhs
-    share = share_of(rhs, piece)
+    rows = rows_ref[...]
+    ids = jnp.broadcast_to(rows[:, 73:74].astype(jnp.int32), slots_ref.shape)
+    at = lax.broadcasted_iota(jnp.int32, slots_ref.shape, 1)
+    slots_ref[...] = (at // 8 == ids).astype(F32).astype(jnp.bfloat16)
+    packed = rows.T
+    packed_ref[...] = packed
+    own = jnp.concatenate([packed[a * SLOT + 72 : a * SLOT + 73, :] for a in range(8)], axis=0)
+    rhs_ref[...] = flat_of(moved_by(own, slots_ref[...], ((1,), (0,))))
+
+
+def first_kernel(rhs_ref, own_ref, other_ref, share_ref):
+    share = share_of(rhs_ref[...], (own_ref, other_ref))
     for place in range(share_ref.shape[0]):
         share_ref[place] = share
 
@@ -310,11 +336,16 @@
     return parts[0]
 
 
-def second_kernel(n_narrow, packed_ref, rhs_ref, parts_ref, piece, first_ref, share_ref):
+def second_kernel(
+    n_narrow, packed_ref, slots_ref, rhs_ref, parts_ref, own_ref, other_ref, first_ref, share_ref
+):
     first = summed(parts_ref)
     first_ref[...] = first
-    slots = slots_of(packed_ref)
-    there = moved_by(first, slots, ((1,), (0,)))
+    lines = lines_of(first)
+    at = lax.broadcasted_iota(jnp.int32, lines.shape, 1)
+    entry_at = lax.broadcasted_iota(jnp.int32, lines.shape, 0)
+    lines = jnp.where(at % 8 == entry_at, lines, 0.0)
+    there = moved_by(lines, slots_ref[...], ((1,), (1,)))
     size = there.shape[1] // 2
     chips = size // n_narrow
     halves = [there[:, :size], there[:, size:]]
@@ -337,8 +368,8 @@
     image = jnp.concatenate(
         [jnp.sum(packed_ref[a * SLOT : (a + 1) * SLOT, :] * near, axis=0, keepdims=True) for a in range(8)], axis=0
     )
-    vector = rhs_ref[...] - moved_by(image, slots, ((1,), (1,)))
-    share = share_of(vector, piece)
+    vector = rhs_ref[...] - flat_of(moved_by(image, slots_ref[...], ((1,), (0,))))
+    share = share_of(vector, (own_ref, other_ref))
     for place in range(share_ref.shape[0]):
         share_ref[place] = share
 
@@ -346,8 +377,10 @@
 def last_kernel(ids_ref, z_ref, local_ref, first_ref, parts_ref, out_ref, sol_ref):
     solution = first_ref[...] + summed(parts_ref)
     sol_ref[...] = solution
-    at = lax.broadcasted_iota(jnp.int32, solution.shape, 1)
-    weights = jnp.sum(jnp.where(at == ids_ref[4], solution, 0.0), axis=1, keepdims=True)
+    lines = lines_of(solution)
+    at = lax.broadcasted_iota(jnp.int32, lines.shape, 1)
+    row = lax.broadcasted_iota(jnp.int32, lines.shape, 0)
+    weights = jnp.sum(jnp.where(at == ids_ref[4] * 8 + row, lines, 0.0), axis=1, keepdims=True)
     for x in range(z_ref.shape[2]):
         for i in range(3):
             acc = local_ref[i, x]
@@ -359,7 +392,9 @@
 def call(kernel, out_shape, in_specs, scratch=(), flops=0, moved=0, name=None):
     return pl.pallas_call(
         kernel,
-        out_shape=[jax.ShapeDtypeStruct(shape, F32) for shape in out_shape],
+        out_shape=[
+            shape if isinstance(shape, jax.ShapeDtypeStruct) else jax.ShapeDtypeStruct(shape, F32) for shape in out_shape
+        ],
         in_specs=in_specs,
         out_specs=[VMEM] * len(out_shape),
         scratch_shapes=list(scratch),
@@ -411,17 +446,32 @@
     fields = (vector_fields, rounded)
     one, two, is_even = exchanged([f[:, 0] for f in fields], [f[:, cells_x - 1] for f in fields], "narrow")
 
-    done = vectors // 2
-    zf, zy, sy, table = call(
-        functools.partial(before_kernel, done),
-        [(vectors, 3, cells_x, cells_y, depth), (2, vectors, 3, 8, depth), (2, 8, depth), (8, 128)],
-        [SMEM, SMEM] + [VMEM] * 4,
-        [pltpu.VMEM((done + 1, 8, 128), F32)],
+    def matrix(rows):
+        return jax.ShapeDtypeStruct((rows, 256), jnp.bfloat16)
+
+    zf, zy, sy, table, own_matrix, x_matrix, y_matrix = call(
+        before_kernel,
+        [
+            (vectors, 3, cells_x, cells_y, depth),
+            (2, vectors, 3, 8, depth),
+            (2, 8, depth),
+            (8, 128),
+            matrix(9 * cells_x * cells_y),
+            matrix(144),
+            matrix(288),
+        ],
+        [SMEM, SMEM] + [VMEM] * 3,
+        [pltpu.VMEM((1, 8, 128), F32)],
         flops=20_000_000,
         moved=1_000_000,
         name="before",
-    )(couplings, ids, deflation, rounded, stiffness, mass)
-    one, two, table = lax.optimization_barrier((one, two, table))
+    )(couplings, ids, deflation, rounded, stiffness)
+    def joined(rows, partner):
+        return jnp.concatenate([rows, lax.ppermute(rows, "z", [(k, partner(k) % size_z) for k in range(size_z)])], axis=0)
+
+    rows_z = joined(inverse_factor, lambda k: k ^ 1)
+    one, two, table, rows_z = lax.optimization_barrier((one, two, table, rows_z))
+    rows_z = joined(rows_z, lambda k: k ^ 2)
     xlo, xhi = jnp.where(is_even, two, one), jnp.where(is_even, one, two)
 
     def side(y):
@@ -431,33 +481,31 @@
     one, two, is_even = exchanged(side(0), side(cells_y - 1), WIDE)
     ylo, yhi = jnp.where(is_even, two, one), jnp.where(is_even, one, two)
 
-    rows = inverse_factor.shape[0]
-    own = inverse_factor.reshape(rows, count, vectors).transpose(0, 2, 1).reshape(rows, count * vectors)
-
-    held = lax.all_gather(own, ("z", "core"), tiled=True)
-
     (table,) = call(
-        functools.partial(inner_kernel, done),
+        inner_kernel,
         [(8, 128)],
-        [SMEM] + [VMEM] * 6,
+        [VMEM] * 8,
         [pltpu.VMEM((3 * vectors, 8, 128), F32)],
-        flops=30_000_000,
+        flops=10_000_000,
         moved=1_000_000,
         name="inner",
-    )(couplings, zf, stiffness, mass, xlo, xhi, table)
+    )(own_matrix, x_matrix, zf, stiffness, mass, xlo, xhi, table)
+    table, rows_z = lax.optimization_barrier((table, rows_z))
+    rows_z = joined(rows_z, lambda k: k + 2 if k // 2 % 2 else k - 2)
     table, payload = call(
         outer_kernel,
         [(8, 128), (n_near, 1, SLOT * vectors)],
-        [SMEM] + [VMEM] * 5,
+        [VMEM] * 6,
         [pltpu.VMEM((6 * vectors, 8, 128), F32)],
         flops=10_000_000,
         moved=2_000_000,
         name="outer",
-    )(couplings, table, zy, sy, ylo, yhi)
+    )(y_matrix, table, zy, sy, ylo, yhi)
     got = lax.all_to_all(payload, ("narrow", "z"), 0, 0)
     got = lax.all_to_all(jnp.broadcast_to(got[None], (size_y,) + got.shape), "y", 0, 0)
-    got, held = lax.optimization_barrier((got, held))
+    got, rows_z = lax.optimization_barrier((got, rows_z))
     other = lax.ppermute(got, "core", [(0, 1), (1, 0)])
+    held = [rows_z, lax.ppermute(rows_z, "core", [(0, 1), (1, 0)])]
     (local,) = call(
         local_kernel,
         [(3, cells_x, cells_y, depth)],
@@ -475,32 +523,41 @@
         return lax.all_to_all(share, group, 0, 0)
 
     core = lax.axis_index("core").astype(jnp.int32).reshape(1)
-    packed, rhs, share = call(
-        functools.partial(first_kernel, n_narrow, size_z),
-        [(SLOT * vectors, count), (vectors, count), (members, vectors, count)],
-        [SMEM] + [VMEM] * 3,
+    flat = (count * vectors // 128, 128)
+    packed, slots, rhs = call(
+        functools.partial(gathered_kernel, n_narrow, size_z),
+        [(SLOT * vectors, count), jax.ShapeDtypeStruct((count, count * vectors), jnp.bfloat16), flat],
+        [SMEM] + [VMEM] * 2,
         [pltpu.VMEM((count, SLOT * vectors), F32)],
         flops=2_000_000,
-        moved=3_000_000,
+        moved=12_000_000,
+        name="gathered",
+    )(core, got, other)
+    (share,) = call(
+        first_kernel,
+        [(members,) + flat],
+        [VMEM] * 3,
+        flops=2_000_000,
+        moved=2_000_000,
         name="first",
-    )(core, got, other, held)
+    )(rhs, *held)
     first, share = call(
         functools.partial(second_kernel, n_narrow),
-        [(vectors, count), (members, vectors, count)],
-        [VMEM] * 4,
+        [flat, (members,) + flat],
+        [VMEM] * 6,
         flops=2_000_000,
         moved=3_000_000,
         name="second",
-    )(packed, rhs, spread(share), held)
+    )(packed, slots, rhs, spread(share), *held)
     preconditioned, solved = call(
         last_kernel,
-        [(3, cells_x, cells_y, depth), (vectors, count)],
+        [(3, cells_x, cells_y, depth), flat],
         [SMEM] + [VMEM] * 4,
         flops=1_000_000,
         moved=1_000_000,
         name="last",
     )(ids, deflation, local, first, spread(share))
-    coarse_solution = solved.T.reshape(-1)
+    coarse_solution = solved.reshape(-1)
     blocks = table[:, : 9 * vectors].reshape(vectors, 9, vectors).transpose(1, 0, 2)
     return preconditioned, blocks.reshape(1, 1, 9, vectors, vectors), coarse_solution
 

time: 97.7 us -> 86 us (0.88)
  blocking collectives: 43.4 us -> 27.1 us
  starting transfers between devices: 10.7 us -> 25.5 us
  between operations: 14.4 us -> 0.96 us
  waiting for transfers between devices: 6.23 us -> 17.4 us
  Pallas kernels: 15.2 us -> 10.2 us
  local copies, waits for them, and re-layouts: 6.06 us -> 3.23 us
    all_to_all x1 -> x0, blocking collectives: 11.4 us -> none  [body(): lax.all_to_all(jnp.broadcast_to(got[None], (size_y,) + got.shape), 'y', 0...]
    ppermute x0 -> x4, starting transfers between devices: none -> 10.2 us  [the longest x3 10.2 us: joined(): lax.ppermute(rows, 'z', [(k, partner(k) % size_z) for k in range(size_z)])]
    all_to_all x0 -> x1, waiting for transfers between devices: none -> 8.25 us  [body(): lax.all_to_all(jnp.broadcast_to(got[None], (size_y,) + got.shape), 'y', 0...]
    all_to_all x1, blocking collectives: 21.1 us -> 15.9 us  [body(): got = lax.all_to_all(payload, ('narrow', 'z'), 0, 0)]
    pallas_call x6 -> x7, Pallas kernels: 14.3 us -> 9.26 us  [the longest x1 2.18 us: body(): call(functools.partial(second_kernel, n_narrow), [flat, (members,) + flat...]
    all_to_all x0 -> x1, starting transfers between devices: none -> 4.28 us  [body(): lax.all_to_all(jnp.broadcast_to(got[None], (size_y,) + got.shape), 'y', 0...]
    ppermute x0 -> x4, waiting for transfers between devices: none -> 2.67 us  [the longest x3 2.66 us: joined(): lax.ppermute(rows, 'z', [(k, partner(k) % size_z) for k in range(size_z)])]
    reshape x2 -> x0, local copies, waits for them, and re-layouts: 1.29 us -> none  [the longest x1 0.71 us: body(): coarse_solution = solved.T.reshape(-1)]
  transfers between devices with their start and end apart: 7 -> 11, of which waited for: 2 -> 5; matrix products, arithmetic and copies ran while one was open for 3% -> 3% of each run, Pallas kernels for 12% -> 7%
where the time goes in v3:
time: 86 us; the launch traced here: 85.5 us
  blocking collectives  27.1 us (32%)
  starting transfers between devices  25.5 us (30%)
  waiting for transfers between devices  17.4 us (20%)
  Pallas kernels  10.2 us (12%)
  local copies, waits for them, and re-layouts  3.23 us (4%)
  other arithmetic  1.11 us (1%)
  between operations  0.96 us (1%)
    all_to_all x1, blocking collectives, body(): got = lax.all_to_all(payload, ('narrow', 'z'), 0, 0)  15.9 us
    all_to_all x1, blocking collectives, spread(): return lax.all_to_all(share, group, 0, 0)  11.2 us
    ppermute x3, starting transfers between devices, joined(): lax.ppermute(rows, 'z', [(k, partner(k) % size_z) for k in range(size_z)])  10.2 us
    all_to_all x1, waiting for transfers between devices, body(): lax.all_to_all(jnp.broadcast_to(got[None], (size_y,) + got.shape), 'y', 0...  8.25 us
    all_to_all x1, starting transfers between devices, spread(): return lax.all_to_all(share, group, 0, 0)  5.05 us
    all_to_all x1, waiting for transfers between devices, spread(): return lax.all_to_all(share, group, 0, 0)  4.57 us
    all_to_all x1, starting transfers between devices, body(): lax.all_to_all(jnp.broadcast_to(got[None], (size_y,) + got.shape), 'y', 0...  4.28 us
    ppermute x2, starting transfers between devices, exchanged(): two = lax.ppermute(chosen(sending_low, sending_high), axis, odd)  2.99 us
  transfers between devices with their start and end apart: 11, of which 5 were waited for; matrix products, arithmetic and copies ran while one was open for 3% of the time, Pallas kernels for 7%

profile of v3, /device:TPU:2, one launch (start us, length us, event | category | flops | bytes accessed | tf_op | source)
XLA Modules:
  0.0 85.5 jit_solution(2857061030416734990)
XLA Ops:
  0.6 0.0 copy-start.6
  0.7 0.0 copy-start.7
  0.7 0.0 copy-start.5
  0.7 0.0 copy-start.4
  0.7 0.0 copy-start.2
  0.7 1.1 %copy.20 = bf16[8,3,4,8,256]{4,3,1,0,2:T(8,128)(2,1)S(1)} copy(bf16[8,3,4,8,256]{4,3,2,1,0:T(8,128)(2,1)} %z_ref.3) | data formatting | bytes 786432 | tf_op args[0]
  1.8 0.8 select_bitcast_fusion.2
  2.6 2.4 %collective-permute-start = (bf16[27,8,256]{2,1,0:T(8,128)(2,1)S(1)}, bf16[27,8,256]{2,1,0:T(8,128)(2,1)S(1)}, u32[]{:S(2)}, u32[]{:S(2)}) collective-permute-start(bf16[27,8,256]{2,1,0:T(8,128)(2,1)S(1)} %pad_maximum_fusion.3), channel_id=1, source_target_pairs={{0,64},{64,0},{128,192},{192,128},{1,65},{65,1},{129,193},{193,129... | collective-permute-start | bytes 331784 | tf_op jit(solution)/shard_map/ppermute | solution.py:441
  5.0 0.0 copy-start.3
  5.0 2.3 %collective-permute-start.1 = (bf16[27,8,256]{2,1,0:T(8,128)(2,1)S(1)}, bf16[27,8,256]{2,1,0:T(8,128)(2,1)S(1)}, u32[]{:S(2)}, u32[]{:S(2)}) collective-permute-start(bf16[27,8,256]{2,1,0:T(8,128)(2,1)S(1)} %pad_maximum_fusion.4), channel_id=1, source_target_pairs={{64,128},{128,64},{65,129},{129,65},{66,130},{130,66},{67,131},{13... | collective-permute-start | bytes 331784 | tf_op jit(solution)/shard_map/ppermute | solution.py:442
  7.3 2.0 %collective-permute-start.2 = (f32[8,2048]{1,0:T(8,128)S(1)}, f32[8,2048]{1,0:T(8,128)S(1)}, u32[]{:S(2)}, u32[]{:S(2)}) collective-permute-start(f32[8,2048]{1,0:T(8,128)S(1)} %copy-done.7), channel_id=1, source_target_pairs={{0,2},{2,0},{4,6},{6,4},{8,10},{10,8},{12,14},{14,12},{1,3},{3,1},... | collective-permute-start | bytes 196616 | tf_op jit(solution)/shard_map/ppermute | solution.py:470
  9.3 0.1 fusion
  9.5 0.1 copy_bitcast_fusion.1
  9.7 1.4 %before.1 = (f32[8,3,4,8,256]{4,3,2,1,0:T(8,128)S(1)}, f32[2,8,3,8,256]{4,3,2,1,0:T(8,128)S(1)}, f32[2,8,256]{2,1,0:T(8,128)S(1)}, f32[8,128]{1,0:T(8,128)S(1)},...) custom-call(f32[3,3,27]{2,1,0:T(4,128)S(1)} %bitcast.30, s32[9]{0:T(128)S(1)} %bitcast.32, ...), custom_call_target="tpu_custom_call" | custom-call | flops 20000000 | bytes 1000000 | tf_op jit(solution)/shard_map/before/pallas_call | solution.py:452
  11.1 0.6 collective-permute-done.2
  11.7 0.0 collective-permute-done
  11.7 0.0 collective-permute-done.1
  11.7 3.4 %collective-permute-start.5 = (f32[16,2048]{1,0:T(8,128)S(1)}, f32[16,2048]{1,0:T(8,128)S(1)}, u32[]{:S(2)}, u32[]{:S(2)}) collective-permute-start(f32[16,2048]{1,0:T(8,128)S(1)} %pad_maximum_fusion.2), channel_id=1, source_target_pairs={{0,4},{2,6},{4,0},{6,2},{8,12},{10,14},{12,8},{14,10},{1,5},{3,7},... | collective-permute-start | bytes 393224 | tf_op jit(solution)/shard_map/ppermute | solution.py:470
  15.1 0.1 fusion.1
  15.2 0.2 broadcast_select_fusion.2
  15.4 0.1 collective-permute-start.4
  15.5 0.7 collective-permute-start.3
  16.2 1.8 %inner.1.table_ref = f32[8,128]{1,0:T(8,128)S(1)} custom-call(bf16[288,256]{1,0:T(8,128)(2,1)S(1)} %get-tuple-element.31.own_ref, bf16[144,256]{1,0:T(8,128)(2,1)S(1)} %get-tuple-element.32.x_ref, f32[8,3,4,8,256]{4,3,2,1,0:T(8,128)S(1)} %get-tuple-element.33.zf_ref, f32[4,8,256]{2,1,0:T(8,128)S(1)} %copy-done.2, f32[4,8,256]{2,1,0:T(8,128)S(1)} %copy-done.3, ...), custom_call_target="tpu_custom_call" | custom-call | flops 10000000 | bytes 1000000 | tf_op jit(solution)/shard_map/inner/pallas_call | solution.py:484
  18.0 2.1 %collective-permute-done.5 = f32[16,2048]{1,0:T(8,128)S(1)} collective-permute-done((f32[16,2048]{1,0:T(8,128)S(1)}, f32[16,2048]{1,0:T(8,128)S(1)}, u32[]{:S(2)}, u32[]{:S(2)}) %collective-permute-start.5) | collective-permute-done | bytes 131104 | tf_op jit(solution)/shard_map/ppermute | solution.py:470
  20.1 4.8 %collective-permute-start.6 = (f32[32,2048]{1,0:T(8,128)S(1)}, f32[32,2048]{1,0:T(8,128)S(1)}, u32[]{:S(2)}, u32[]{:S(2)}) collective-permute-start(f32[32,2048]{1,0:T(8,128)S(1)} %pad_maximum_fusion.1), channel_id=1, source_target_pairs={{0,12},{2,14},{4,8},{6,10},{8,4},{10,6},{12,0},{14,2},{1,13},{3,15... | collective-permute-start | bytes 786440 | tf_op jit(solution)/shard_map/ppermute | solution.py:470
  24.9 0.0 collective-permute-done.4
  24.9 0.0 collective-permute-done.3
  24.9 1.4 %outer.1 = (f32[8,128]{1,0:T(8,128)S(1)}, f32[32,1,640]{2,1,0:T(1,128)S(1)}) custom-call(bf16[288,256]{1,0:T(8,128)(2,1)S(1)} %get-tuple-element.30.y_ref, f32[8,128]{1,0:T(8,128)S(1)} %inner.1.table_ref, f32[2,8,3,8,256]{4,3,2,1,0:T(8,128)S(1)} %get-tuple-element.37.zy_ref, f32[2,8,256]{2,1,0:T(8,128)S(1)} %get-tuple-element.38.sy_ref, ...), custom_call_target="tpu_custom_call" | custom-call | flops 10000000 | bytes 2000000 | tf_op jit(solution)/shard_map/outer/pallas_call | solution.py:495
  26.3 15.9 %all_to_all.20 = f32[32,1,640]{2,1,0:T(1,128)S(1)} all-to-all(f32[32,1,640]{2,1,0:T(1,128)S(1)} %get-tuple-element.39), channel_id=1, replica_groups=mesh['narrow'=4,'y'=4,'z'=8,'core'=2] {'narrow','z'}, dimensions={0} | all-to-all | bytes 163840 | tf_op jit(solution)/shard_map/all_to_all | solution.py:504
  42.3 0.9 %broadcast_in_dim.9 = f32[4,32,1,640]{3,2,1,0:T(1,128)} broadcast(f32[32,640]{1,0:T(8,128)S(1)} %bitcast.36), dimensions={1,3} | broadcast | bytes 409600 | tf_op jit(solution)/shard_map/broadcast_in_dim | solution.py:505
  43.2 4.3 %all-to-all-start.1 = ((f32[4,32,1,640]{3,2,1,0:T(1,128)}), f32[4,32,1,640]{3,2,1,0:T(1,128)S(1)}, u32[]{:S(2)}, u32[]{:S(2)}) async-start(f32[4,32,1,640]{3,2,1,0:T(1,128)} %broadcast_in_dim.9), calls=%async_computation.1 | async-start | bytes 655360 | tf_op jit(solution)/shard_map/all_to_all | solution.py:505
  47.5 0.0 collective-permute-done.6
  47.5 8.3 %all-to-all-done.1.own_ref = f32[4,32,1,640]{3,2,1,0:T(1,128)S(1)} async-done(((f32[4,32,1,640]{3,2,1,0:T(1,128)}), f32[4,32,1,640]{3,2,1,0:T(1,128)S(1)}, u32[]{:S(2)}, u32[]{:S(2)}) %all-to-all-start.1) | async-done | bytes 327712 | tf_op jit(solution)/shard_map/all_to_all | solution.py:505
  55.7 0.0 collective-permute-start.8
  55.8 0.5 collective-permute-start.7
  56.3 1.9 %collective-permute-done.7.other_ref = f32[4,32,1,640]{3,2,1,0:T(1,128)S(1)} collective-permute-done((f32[4,32,1,640]{3,2,1,0:T(1,128)S(1)}, f32[4,32,1,640]{3,2,1,0:T(1,128)S(1)}, u32[]{:S(2)}, u32[]{:S(2)}) %collective-permute-start.7) | collective-permute-done | bytes 327712 | tf_op jit(solution)/shard_map/ppermute | solution.py:507
  58.1 0.7 gathered.1
  58.8 0.0 collective-permute-done.8.other_ref
  58.8 0.5 first.1
  59.3 11.2 %all_to_all.21.parts_ref = f32[16,16,128]{2,1,0:T(8,128)S(1)} all-to-all(f32[16,16,128]{2,1,0:T(8,128)S(1)} %first.1), channel_id=1, replica_groups=mesh['narrow'=4,'y'=4,'z'=8,'core'=2] {'narrow','y'}, dimensions={0} | all-to-all | bytes 262144 | tf_op jit(solution)/shard_map/all_to_all | solution.py:523
  70.5 2.2 %second.1 = (f32[16,128]{1,0:T(8,128)S(1)}, f32[16,16,128]{2,1,0:T(8,128)}) custom-call(f32[640,256]{1,0:T(8,128)S(1)} %get-tuple-element.42.packed_ref, bf16[256,2048]{1,0:T(8,128)(2,1)S(1)} %get-tuple-element.43.slots_ref, f32[16,128]{1,0:T(8,128)S(1)} %get-tuple-element.44.rhs_ref, f32[16,16,128]{2,1,0:T(8,128)S(1)} %all_to_all.21.parts_ref, ...), custom_call_target="tpu_custom_call" | custom-call | flops 2000000 | bytes 3000000 | tf_op jit(solution)/shard_map/second/pallas_call | solution.py:544
  72.7 5.1 %all-to-all-start.3 = ((f32[16,16,128]{2,1,0:T(8,128)}), f32[16,16,128]{2,1,0:T(8,128)S(1)}, u32[]{:S(2)}, u32[]{:S(2)}) async-start(f32[16,16,128]{2,1,0:T(8,128)} %get-tuple-element.47), calls=%async_computation.3 | async-start | bytes 262144 | tf_op jit(solution)/shard_map/all_to_all | solution.py:523
  77.7 0.1 reshape.39.range_ref
  77.8 0.9 %local.1.local_ref = f32[3,4,8,256]{3,2,1,0:T(8,128)S(1)} custom-call(s32[4]{0:T(128)S(1)} %reshape.39.range_ref, bf16[12,12,5,3,256]{4,3,2,1,0:T(4,128)(2,1)S(1)} %bitcast.29, bf16[3,4,8,256]{3,2,1,0:T(8,128)(2,1)S(1)} %copy.26.r_ref, bf16[27,8,256]{2,1,0:T(8,128)(2,1)S(1)} %get-tuple-element.63.xlo_ref, bf16[27,8,256]{2,1,0:T(8,128)(2,1)S(1)} %get-tuple-element.62.xhi_ref, ...), custom_call_target="tpu_custom_call" | custom-call | flops 2000000 | bytes 3000000 | tf_op jit(solution)/shard_map/local/pallas_call | solution.py:509
  78.7 0.1 reshape.42
  78.8 0.7 copy.27
  79.5 4.6 %all-to-all-done.3.parts_ref = f32[16,16,128]{2,1,0:T(8,128)S(1)} async-done(((f32[16,16,128]{2,1,0:T(8,128)}), f32[16,16,128]{2,1,0:T(8,128)S(1)}, u32[]{:S(2)}, u32[]{:S(2)}) %all-to-all-start.3) | async-done | bytes 131104 | tf_op jit(solution)/shard_map/all_to_all | solution.py:523
  84.1 1.4 %last.1 = (f32[3,4,8,256]{3,2,1,0:T(8,128)}, f32[16,128]{1,0:T(8,128)}) custom-call(s32[9]{0:T(128)S(1)} %bitcast.33, bf16[8,3,4,8,256]{4,3,2,1,0:T(8,128)(2,1)S(1)} %copy-done, f32[3,4,8,256]{3,2,1,0:T(8,128)S(1)} %local.1.local_ref, f32[16,128]{1,0:T(8,128)S(1)} %get-tuple-element.46.first_ref, f32[16,16,128]{2,1,0:T(8,128)S(1)} %all-to-all-done.3.parts_ref), custom_call_target="tpu_custom_call" | custom-call | flops 1000000 | bytes 1000000 | tf_op jit(solution)/shard_map/last/pallas_call | solution.py:552
  (25 shorter events, 0.2 us)
Async XLA Ops:
  0.6 9.0 %copy-start = (bf16[8,3,4,8,256]{4,3,2,1,0:T(8,128)(2,1)S(1)}, bf16[8,3,4,8,256]{4,3,2,1,0:T(8,128)(2,1)}, u32[]{:S(2)}) copy-start(bf16[8,3,4,8,256]{4,3,2,1,0:T(8,128)(2,1)} %z_ref.3) | copy-start | bytes 1179652
  0.6 8.7 %copy-start.6 = (f32[3,4,8,256]{3,2,1,0:T(8,128)S(1)}, f32[3,4,8,256]{3,2,1,0:T(8,128)}, u32[]{:S(2)}) copy-start(f32[3,4,8,256]{3,2,1,0:T(8,128)} %param.10) | copy-start | bytes 294916
  0.7 6.7 %copy-start.7 = (f32[8,2048]{1,0:T(8,128)S(1)}, f32[8,2048]{1,0:T(8,128)}, u32[]{:S(2)}) copy-start(f32[8,2048]{1,0:T(8,128)} %param.15) | copy-start | bytes 196612
  0.7 9.0 %copy-start.5 = (s32[1,1,9]{2,1,0:T(1,128)S(1)}, s32[1,1,9]{2,1,0:T(1,128)}, u32[]{:S(2)}) copy-start(s32[1,1,9]{2,1,0:T(1,128)} %param.17) | copy-start | bytes 112
  0.7 9.0 %copy-start.4 = (f32[27,3,3]{0,2,1:T(4,128)S(1)}, f32[27,3,3]{0,2,1:T(4,128)}, u32[]{:S(2)}) copy-start(f32[27,3,3]{0,2,1:T(4,128)} %param.13) | copy-start | bytes 2920
  0.7 9.0 %copy-start.2 = (f32[4,8,256]{2,1,0:T(8,128)S(1)}, f32[4,8,256]{2,1,0:T(8,128)}, u32[]{:S(2)}) copy-start(f32[4,8,256]{2,1,0:T(8,128)} %stiff_ref.3) | copy-start | bytes 98308
  2.6 9.1 %collective-permute-start = (bf16[27,8,256]{2,1,0:T(8,128)(2,1)S(1)}, bf16[27,8,256]{2,1,0:T(8,128)(2,1)S(1)}, u32[]{:S(2)}, u32[]{:S(2)}) collective-permute-start(bf16[27,8,256]{2,1,0:T(8,128)(2,1)S(1)} %pad_maximum_fusion.3), channel_id=1, source_target_pairs={{0,64},{64,0},{128,192},{192,128},{1,65},{65,1},{129,193},{193,129... | collective-permute-start | bytes 331784 | tf_op jit(solution)/shard_map/ppermute | solution.py:441
  5.0 11.2 %copy-start.3 = (f32[4,8,256]{2,1,0:T(8,128)S(1)}, f32[4,8,256]{2,1,0:T(8,128)}, u32[]{:S(2)}) copy-start(f32[4,8,256]{2,1,0:T(8,128)} %mass_ref.1) | copy-start | bytes 98308
  5.0 6.7 %collective-permute-start.1 = (bf16[27,8,256]{2,1,0:T(8,128)(2,1)S(1)}, bf16[27,8,256]{2,1,0:T(8,128)(2,1)S(1)}, u32[]{:S(2)}, u32[]{:S(2)}) collective-permute-start(bf16[27,8,256]{2,1,0:T(8,128)(2,1)S(1)} %pad_maximum_fusion.4), channel_id=1, source_target_pairs={{64,128},{128,64},{65,129},{129,65},{66,130},{130,66},{67,131},{13... | collective-permute-start | bytes 331784 | tf_op jit(solution)/shard_map/ppermute | solution.py:442
  7.3 4.4 %collective-permute-start.2 = (f32[8,2048]{1,0:T(8,128)S(1)}, f32[8,2048]{1,0:T(8,128)S(1)}, u32[]{:S(2)}, u32[]{:S(2)}) collective-permute-start(f32[8,2048]{1,0:T(8,128)S(1)} %copy-done.7), channel_id=1, source_target_pairs={{0,2},{2,0},{4,6},{6,4},{8,10},{10,8},{12,14},{14,12},{1,3},{3,1},... | collective-permute-start | bytes 196616 | tf_op jit(solution)/shard_map/ppermute | solution.py:470
  11.7 8.3 %collective-permute-start.5 = (f32[16,2048]{1,0:T(8,128)S(1)}, f32[16,2048]{1,0:T(8,128)S(1)}, u32[]{:S(2)}, u32[]{:S(2)}) collective-permute-start(f32[16,2048]{1,0:T(8,128)S(1)} %pad_maximum_fusion.2), channel_id=1, source_target_pairs={{0,4},{2,6},{4,0},{6,2},{8,12},{10,14},{12,8},{14,10},{1,5},{3,7},... | collective-permute-start | bytes 393224 | tf_op jit(solution)/shard_map/ppermute | solution.py:470
  15.4 9.5 %collective-permute-start.4 = (bf16[27,6,256]{2,1,0:T(8,128)(2,1)S(1)}, bf16[27,6,256]{2,1,0:T(8,128)(2,1)S(1)}, u32[]{:S(2)}, u32[]{:S(2)}) collective-permute-start(bf16[27,6,256]{2,1,0:T(8,128)(2,1)S(1)} %get-tuple-element.60), channel_id=1, source_target_pairs={{0,1},{1,0},{2,3},{3,2},{4,5},{5,4},{6,7},{7,6},{8,9},{9,8},{10,11... | collective-permute-start | bytes 248840 | tf_op jit(solution)/shard_map/ppermute | solution.py:441
  15.5 9.4 %collective-permute-start.3 = (bf16[27,6,256]{2,1,0:T(8,128)(2,1)S(1)}, bf16[27,6,256]{2,1,0:T(8,128)(2,1)S(1)}, u32[]{:S(2)}, u32[]{:S(2)}) collective-permute-start(bf16[27,6,256]{2,1,0:T(8,128)(2,1)S(1)} %get-tuple-element.61), channel_id=1, source_target_pairs={{1,2},{2,1},{3,4},{4,3},{5,6},{6,5},{7,8},{8,7},{9,10},{10,9},{11,... | collective-permute-start | bytes 248840 | tf_op jit(solution)/shard_map/ppermute | solution.py:442
  20.1 27.4 %collective-permute-start.6 = (f32[32,2048]{1,0:T(8,128)S(1)}, f32[32,2048]{1,0:T(8,128)S(1)}, u32[]{:S(2)}, u32[]{:S(2)}) collective-permute-start(f32[32,2048]{1,0:T(8,128)S(1)} %pad_maximum_fusion.1), channel_id=1, source_target_pairs={{0,12},{2,14},{4,8},{6,10},{8,4},{10,6},{12,0},{14,2},{1,13},{3,15... | collective-permute-start | bytes 786440 | tf_op jit(solution)/shard_map/ppermute | solution.py:470
  43.2 12.6 %all-to-all-start.1 = ((f32[4,32,1,640]{3,2,1,0:T(1,128)}), f32[4,32,1,640]{3,2,1,0:T(1,128)S(1)}, u32[]{:S(2)}, u32[]{:S(2)}) async-start(f32[4,32,1,640]{3,2,1,0:T(1,128)} %broadcast_in_dim.9), calls=%async_computation.1 | async-start | bytes 655360 | tf_op jit(solution)/shard_map/all_to_all | solution.py:505
  55.7 3.1 %collective-permute-start.8 = (f32[64,2048]{1,0:T(8,128)S(1)}, f32[64,2048]{1,0:T(8,128)S(1)}, u32[]{:S(2)}, u32[]{:S(2)}) collective-permute-start(f32[64,2048]{1,0:T(8,128)S(1)} %pad_maximum_fusion.own_ref), channel_id=1, source_target_pairs={{0,1},{1,0},{2,3},{3,2},{4,5},{5,4},{6,7},{7,6},{8,9},{9,8},{10,11... | collective-permute-start | bytes 1572872 | tf_op jit(solution)/shard_map/ppermute | solution.py:508
  55.8 2.4 %collective-permute-start.7 = (f32[4,32,1,640]{3,2,1,0:T(1,128)S(1)}, f32[4,32,1,640]{3,2,1,0:T(1,128)S(1)}, u32[]{:S(2)}, u32[]{:S(2)}) collective-permute-start(f32[4,32,1,640]{3,2,1,0:T(1,128)S(1)} %all-to-all-done.1.own_ref), channel_id=1, source_target_pairs={{0,1},{1,0},{2,3},{3,2},{4,5},{5,4},{6,7},{7,6},{8,9},{9,8},{10,11... | collective-permute-start | bytes 983048 | tf_op jit(solution)/shard_map/ppermute | solution.py:507
  70.5 7.2 %copy-start.8 = (s32[1,1,2,2]{3,2,1,0:T(2,128)S(1)}, s32[1,1,2,2]{3,2,1,0:T(2,128)}, u32[]{:S(2)}) copy-start(s32[1,1,2,2]{3,2,1,0:T(2,128)} %param.16) | copy-start | bytes 52
  70.5 7.3 %copy-start.1 = (bf16[12,12,3,5,256]{4,2,3,1,0:T(4,128)(2,1)S(1)}, bf16[12,12,3,5,256]{4,2,3,1,0:T(4,128)(2,1)}, u32[]{:S(2)}) copy-start(bf16[12,12,3,5,256]{4,2,3,1,0:T(4,128)(2,1)} %param.14) | copy-start | bytes 3317764
  72.7 11.4 %all-to-all-start.3 = ((f32[16,16,128]{2,1,0:T(8,128)}), f32[16,16,128]{2,1,0:T(8,128)S(1)}, u32[]{:S(2)}, u32[]{:S(2)}) async-start(f32[16,16,128]{2,1,0:T(8,128)} %get-tuple-element.47), calls=%async_computation.3 | async-start | bytes 262144 | tf_op jit(solution)/shard_map/all_to_all | solution.py:523

commit v4 on v3

--- a/solution.py
+++ b/solution.py
@@ -302,15 +302,15 @@
     return folded(jnp.sum(acc, axis=0, keepdims=True))
 
 
-def gathered_kernel(
-    n_narrow, size_z, core_ref, own_ref, other_ref, packed_ref, slots_ref, rhs_ref, rows_ref
+def first_kernel(
+    n_narrow, size_z, place_ref, own_ref, other_ref, held_ref, held_other_ref, packed_ref, slots_ref, rhs_ref, share_ref, rows_ref
 ):
     size_y = own_ref.shape[0]
     chips = n_narrow * size_y * size_z
-    for got_ref, core in ((own_ref, core_ref[0]), (other_ref, 1 - core_ref[0])):
+    for got_ref, core in ((own_ref, place_ref[size_y]), (other_ref, 1 - place_ref[size_y])):
         for y in range(size_y):
             for x in range(n_narrow):
-                place = pl.multiple_of(core * chips + (x * size_y + y) * size_z, 8)
+                place = pl.multiple_of(core * chips + (x * size_y + place_ref[y]) * size_z, 8)
                 block = got_ref[y, x * size_z : (x + 1) * size_z]
                 rows_ref[pl.ds(place, size_z), :] = block.reshape(size_z, block.shape[2])
     rows = rows_ref[...]
@@ -320,11 +320,9 @@
     packed = rows.T
     packed_ref[...] = packed
     own = jnp.concatenate([packed[a * SLOT + 72 : a * SLOT + 73, :] for a in range(8)], axis=0)
-    rhs_ref[...] = flat_of(moved_by(own, slots_ref[...], ((1,), (0,))))
-
-
-def first_kernel(rhs_ref, own_ref, other_ref, share_ref):
-    share = share_of(rhs_ref[...], (own_ref, other_ref))
+    rhs = flat_of(moved_by(own, slots_ref[...], ((1,), (0,))))
+    rhs_ref[...] = rhs
+    share = share_of(rhs, (held_ref, held_other_ref))
     for place in range(share_ref.shape[0]):
         share_ref[place] = share
 
@@ -470,7 +468,7 @@
         return jnp.concatenate([rows, lax.ppermute(rows, "z", [(k, partner(k) % size_z) for k in range(size_z)])], axis=0)
 
     rows_z = joined(inverse_factor, lambda k: k ^ 1)
-    one, two, table, rows_z = lax.optimization_barrier((one, two, table, rows_z))
+    one, two, table = lax.optimization_barrier((one, two, table))
     rows_z = joined(rows_z, lambda k: k ^ 2)
     xlo, xhi = jnp.where(is_even, two, one), jnp.where(is_even, one, two)
 
@@ -490,7 +488,6 @@
         moved=1_000_000,
         name="inner",
     )(own_matrix, x_matrix, zf, stiffness, mass, xlo, xhi, table)
-    table, rows_z = lax.optimization_barrier((table, rows_z))
     rows_z = joined(rows_z, lambda k: k + 2 if k // 2 % 2 else k - 2)
     table, payload = call(
         outer_kernel,
@@ -502,8 +499,8 @@
         name="outer",
     )(y_matrix, table, zy, sy, ylo, yhi)
     got = lax.all_to_all(payload, ("narrow", "z"), 0, 0)
-    got = lax.all_to_all(jnp.broadcast_to(got[None], (size_y,) + got.shape), "y", 0, 0)
-    got, rows_z = lax.optimization_barrier((got, rows_z))
+    got = [got] + [lax.ppermute(got, "y", [(k, k ^ step) for k in range(size_y)]) for step in range(1, size_y)]
+    got = jnp.stack(got)
     other = lax.ppermute(got, "core", [(0, 1), (1, 0)])
     held = [rows_z, lax.ppermute(rows_z, "core", [(0, 1), (1, 0)])]
     (local,) = call(
@@ -522,25 +519,23 @@
     def spread(share):
         return lax.all_to_all(share, group, 0, 0)
 
-    core = lax.axis_index("core").astype(jnp.int32).reshape(1)
+    steps = jnp.arange(size_y, dtype=jnp.int32) ^ lax.axis_index("y")
+    core = jnp.append(steps, lax.axis_index("core").astype(jnp.int32))
     flat = (count * vectors // 128, 128)
-    packed, slots, rhs = call(
-        functools.partial(gathered_kernel, n_narrow, size_z),
-        [(SLOT * vectors, count), jax.ShapeDtypeStruct((count, count * vectors), jnp.bfloat16), flat],
-        [SMEM] + [VMEM] * 2,
+    packed, slots, rhs, share = call(
+        functools.partial(first_kernel, n_narrow, size_z),
+        [
+            (SLOT * vectors, count),
+            jax.ShapeDtypeStruct((count, count * vectors), jnp.bfloat16),
+            flat,
+            (members,) + flat,
+        ],
+        [SMEM] + [VMEM] * 4,
         [pltpu.VMEM((count, SLOT * vectors), F32)],
         flops=2_000_000,
-        moved=12_000_000,
-        name="gathered",
-    )(core, got, other)
-    (share,) = call(
-        first_kernel,
-        [(members,) + flat],
-        [VMEM] * 3,
-        flops=2_000_000,
-        moved=2_000_000,
+        moved=3_000_000,
         name="first",
-    )(rhs, *held)
+    )(core, got, other, *held)
     first, share = call(
         functools.partial(second_kernel, n_narrow),
         [flat, (members,) + flat],

time: 86 us -> 83.3 us (0.969)
  blocking collectives: 27.1 us -> 12.9 us
  starting transfers between devices: 25.5 us -> 31.8 us
  waiting for transfers between devices: 17.4 us -> 22.1 us
  Pallas kernels: 10.2 us -> 11.4 us
    all_to_all x1 -> x0, blocking collectives: 15.9 us -> none  [body(): got = lax.all_to_all(payload, ('narrow', 'z'), 0, 0)]
    ppermute x0 -> x3, waiting for transfers between devices: none -> 4.45 us  [body(): lax.ppermute(got, 'y', [(k, k ^ step) for k in range(size_y)])]
    ppermute x0 -> x3, starting transfers between devices: none -> 4.09 us  [body(): lax.ppermute(got, 'y', [(k, k ^ step) for k in range(size_y)])]
    all_to_all x1, starting transfers between devices: 4.28 us -> 6.17 us  [body(): got = lax.all_to_all(payload, ('narrow', 'z'), 0, 0)]
    all_to_all x1, blocking collectives: 11.2 us -> 12.9 us  [spread(): return lax.all_to_all(share, group, 0, 0)]
    broadcast_in_dim x1 -> x0, local copies, waits for them, and re-layouts: 0.9 us -> none  [body(): jnp.broadcast_to(got[None], (size_y,) + got.shape)]
    unnamed x22 -> x24, local copies, waits for them, and re-layouts: 1.87 us -> 1.88 us
  transfers between devices with their start and end apart: 11 -> 14, of which waited for: 5 -> 7; matrix products, arithmetic and copies ran while one was open for 3% -> 2% of each run, Pallas kernels for 7% -> 7%
where the time goes in v4:
time: 83.3 us; the launch traced here: 82.9 us
  starting transfers between devices  31.8 us (38%)
  waiting for transfers between devices  22.1 us (27%)
  blocking collectives  12.9 us (15%)
  Pallas kernels  11.4 us (14%)
  local copies, waits for them, and re-layouts  2.37 us (3%)
  other arithmetic  1.46 us (2%)
  between operations  0.98 us (1%)
    all_to_all x1, blocking collectives, spread(): return lax.all_to_all(share, group, 0, 0)  12.9 us
    ppermute x3, starting transfers between devices, joined(): lax.ppermute(rows, 'z', [(k, partner(k) % size_z) for k in range(size_z)])  10.2 us
    all_to_all x1, waiting for transfers between devices, body(): got = lax.all_to_all(payload, ('narrow', 'z'), 0, 0)  8.88 us
    all_to_all x1, starting transfers between devices, body(): got = lax.all_to_all(payload, ('narrow', 'z'), 0, 0)  6.17 us
    all_to_all x1, starting transfers between devices, spread(): return lax.all_to_all(share, group, 0, 0)  5.05 us
    all_to_all x1, waiting for transfers between devices, spread(): return lax.all_to_all(share, group, 0, 0)  4.57 us
    ppermute x3, waiting for transfers between devices, body(): lax.ppermute(got, 'y', [(k, k ^ step) for k in range(size_y)])  4.45 us
    ppermute x3, starting transfers between devices, body(): lax.ppermute(got, 'y', [(k, k ^ step) for k in range(size_y)])  4.09 us
  transfers between devices with their start and end apart: 14, of which 7 were waited for; matrix products, arithmetic and copies ran while one was open for 2% of the time, Pallas kernels for 7%

profile of v4, /device:TPU:2, one launch (start us, length us, event | category | flops | bytes accessed | tf_op | source)
XLA Modules:
  0.0 82.9 jit_solution(17295249688315429765)
XLA Ops:
  0.6 0.0 copy-start.7
  0.7 1.1 %copy.20 = bf16[8,3,4,8,256]{4,3,1,0,2:T(8,128)(2,1)S(1)} copy(bf16[8,3,4,8,256]{4,3,2,1,0:T(8,128)(2,1)} %z_ref.3) | data formatting | bytes 786432 | tf_op args[0]
  1.8 0.8 select_bitcast_fusion.2
  2.6 2.4 %collective-permute-start = (bf16[27,8,256]{2,1,0:T(8,128)(2,1)S(1)}, bf16[27,8,256]{2,1,0:T(8,128)(2,1)S(1)}, u32[]{:S(2)}, u32[]{:S(2)}) collective-permute-start(bf16[27,8,256]{2,1,0:T(8,128)(2,1)S(1)} %pad_maximum_fusion.3), channel_id=1, source_target_pairs={{0,64},{64,0},{128,192},{192,128},{1,65},{65,1},{129,193},{193,129... | collective-permute-start | bytes 331784 | tf_op jit(solution)/shard_map/ppermute | solution.py:439
  5.0 2.3 %collective-permute-start.1 = (bf16[27,8,256]{2,1,0:T(8,128)(2,1)S(1)}, bf16[27,8,256]{2,1,0:T(8,128)(2,1)S(1)}, u32[]{:S(2)}, u32[]{:S(2)}) collective-permute-start(bf16[27,8,256]{2,1,0:T(8,128)(2,1)S(1)} %pad_maximum_fusion.4), channel_id=1, source_target_pairs={{64,128},{128,64},{65,129},{129,65},{66,130},{130,66},{67,131},{13... | collective-permute-start | bytes 331784 | tf_op jit(solution)/shard_map/ppermute | solution.py:440
  7.3 2.0 %collective-permute-start.8 = (f32[8,2048]{1,0:T(8,128)S(1)}, f32[8,2048]{1,0:T(8,128)S(1)}, u32[]{:S(2)}, u32[]{:S(2)}) collective-permute-start(f32[8,2048]{1,0:T(8,128)S(1)} %copy-done.6), channel_id=1, source_target_pairs={{0,2},{2,0},{4,6},{6,4},{8,10},{10,8},{12,14},{14,12},{1,3},{3,1},... | collective-permute-start | bytes 196616 | tf_op jit(solution)/shard_map/ppermute | solution.py:468
  9.3 0.1 fusion
  9.5 0.0 copy-start.3
  9.5 0.1 copy_bitcast_fusion
  9.7 1.4 %before.1 = (f32[8,3,4,8,256]{4,3,2,1,0:T(8,128)S(1)}, f32[2,8,3,8,256]{4,3,2,1,0:T(8,128)S(1)}, f32[2,8,256]{2,1,0:T(8,128)S(1)}, f32[8,128]{1,0:T(8,128)S(1)},...) custom-call(f32[3,3,27]{2,1,0:T(4,128)S(1)} %bitcast.31, s32[9]{0:T(128)S(1)} %bitcast.33, ...), custom_call_target="tpu_custom_call" | custom-call | flops 20000000 | bytes 1000000 | tf_op jit(solution)/shard_map/before/pallas_call | solution.py:450
  11.1 0.5 collective-permute-done.8
  11.7 3.4 %collective-permute-start.9 = (f32[16,2048]{1,0:T(8,128)S(1)}, f32[16,2048]{1,0:T(8,128)S(1)}, u32[]{:S(2)}, u32[]{:S(2)}) collective-permute-start(f32[16,2048]{1,0:T(8,128)S(1)} %pad_maximum_fusion.2), channel_id=1, source_target_pairs={{0,4},{2,6},{4,0},{6,2},{8,12},{10,14},{12,8},{14,10},{1,5},{3,7},... | collective-permute-start | bytes 393224 | tf_op jit(solution)/shard_map/ppermute | solution.py:468
  15.0 0.0 collective-permute-done
  15.0 0.0 collective-permute-done.1
  15.1 0.1 fusion.1
  15.2 0.2 broadcast_select_fusion.2
  15.4 0.1 collective-permute-start.3
  15.5 0.7 collective-permute-start.2
  16.2 1.8 %inner.1.table_ref = f32[8,128]{1,0:T(8,128)S(1)} custom-call(bf16[288,256]{1,0:T(8,128)(2,1)S(1)} %get-tuple-element.27.own_ref, bf16[144,256]{1,0:T(8,128)(2,1)S(1)} %get-tuple-element.28.x_ref, f32[8,3,4,8,256]{4,3,2,1,0:T(8,128)S(1)} %get-tuple-element.29.zf_ref, f32[4,8,256]{2,1,0:T(8,128)S(1)} %copy-done.2, f32[4,8,256]{2,1,0:T(8,128)S(1)} %copy-done.3, ...), custom_call_target="tpu_custom_call" | custom-call | flops 10000000 | bytes 1000000 | tf_op jit(solution)/shard_map/inner/pallas_call | solution.py:482
  18.0 2.1 %collective-permute-done.9 = f32[16,2048]{1,0:T(8,128)S(1)} collective-permute-done((f32[16,2048]{1,0:T(8,128)S(1)}, f32[16,2048]{1,0:T(8,128)S(1)}, u32[]{:S(2)}, u32[]{:S(2)}) %collective-permute-start.9) | collective-permute-done | bytes 131104 | tf_op jit(solution)/shard_map/ppermute | solution.py:468
  20.0 4.9 %collective-permute-start.10 = (f32[32,2048]{1,0:T(8,128)S(1)}, f32[32,2048]{1,0:T(8,128)S(1)}, u32[]{:S(2)}, u32[]{:S(2)}) collective-permute-start(f32[32,2048]{1,0:T(8,128)S(1)} %pad_maximum_fusion.1), channel_id=1, source_target_pairs={{0,12},{2,14},{4,8},{6,10},{8,4},{10,6},{12,0},{14,2},{1,13},{3,15... | collective-permute-start | bytes 786440 | tf_op jit(solution)/shard_map/ppermute | solution.py:468
  24.9 0.0 collective-permute-done.3
  24.9 0.0 collective-permute-done.2
  24.9 2.0 %outer.1 = (f32[8,128]{1,0:T(8,128)S(1)}, f32[32,1,640]{2,1,0:T(1,128)}) custom-call(bf16[288,256]{1,0:T(8,128)(2,1)S(1)} %get-tuple-element.26.y_ref, f32[8,128]{1,0:T(8,128)S(1)} %inner.1.table_ref, f32[2,8,3,8,256]{4,3,2,1,0:T(8,128)S(1)} %get-tuple-element.31.zy_ref, f32[2,8,256]{2,1,0:T(8,128)S(1)} %get-tuple-element.32.sy_ref, ...), custom_call_target="tpu_custom_call" | custom-call | flops 10000000 | bytes 2000000 | tf_op jit(solution)/shard_map/outer/pallas_call | solution.py:492
  27.0 6.2 %all-to-all-start = ((f32[32,1,640]{2,1,0:T(1,128)}), f32[32,1,640]{2,1,0:T(1,128)S(1)}, u32[]{:S(2)}, u32[]{:S(2)}) async-start(f32[32,1,640]{2,1,0:T(1,128)} %get-tuple-element.33), calls=%async_computation | async-start | bytes 163840 | tf_op jit(solution)/shard_map/all_to_all | solution.py:501
  33.2 8.9 %all-to-all-done = f32[32,1,640]{2,1,0:T(1,128)S(1)} async-done(((f32[32,1,640]{2,1,0:T(1,128)}), f32[32,1,640]{2,1,0:T(1,128)S(1)}, u32[]{:S(2)}, u32[]{:S(2)}) %all-to-all-start) | async-done | bytes 81952 | tf_op jit(solution)/shard_map/all_to_all | solution.py:501
  42.0 3.2 %collective-permute-start.6 = (f32[32,1,640]{2,1,0:T(1,128)S(1)}, f32[32,1,640]{2,1,0:T(1,128)S(1)}, u32[]{:S(2)}, u32[]{:S(2)}) collective-permute-start(f32[32,1,640]{2,1,0:T(1,128)S(1)} %all-to-all-done), channel_id=1, source_target_pairs={{0,48},{16,32},{32,16},{48,0},{1,49},{17,33},{33,17},{49,1},{2,50}... | collective-permute-start | bytes 245768 | tf_op jit(solution)/shard_map/ppermute | solution.py:502
  45.2 0.5 collective-permute-start.5
  45.7 0.5 collective-permute-start.4
  46.2 0.7 collective-permute-start.11
  46.8 2.1 %collective-permute-done.6 = f32[32,1,640]{2,1,0:T(1,128)S(1)} collective-permute-done((f32[32,1,640]{2,1,0:T(1,128)S(1)}, f32[32,1,640]{2,1,0:T(1,128)S(1)}, u32[]{:S(2)}, u32[]{:S(2)}) %collective-permute-start.6) | collective-permute-done | bytes 81952 | tf_op jit(solution)/shard_map/ppermute | solution.py:502
  49.0 2.3 %collective-permute-done.5 = f32[32,1,640]{2,1,0:T(1,128)S(1)} collective-permute-done((f32[32,1,640]{2,1,0:T(1,128)S(1)}, f32[32,1,640]{2,1,0:T(1,128)S(1)}, u32[]{:S(2)}, u32[]{:S(2)}) %collective-permute-start.5) | collective-permute-done | bytes 81952 | tf_op jit(solution)/shard_map/ppermute | solution.py:502
  51.3 0.0 collective-permute-done.4
  51.3 0.3 pad_maximum_fusion.own_ref
  51.6 0.1 collective-permute-start.7
  51.7 0.1 pad_add_fusion.place_ref
  51.8 1.5 %collective-permute-done.7.other_ref = f32[4,32,1,640]{3,2,1,0:T(1,128)S(1)} collective-permute-done((f32[4,32,1,640]{3,2,1,0:T(1,128)S(1)}, f32[4,32,1,640]{3,2,1,0:T(1,128)S(1)}, u32[]{:S(2)}, u32[]{:S(2)}) %collective-permute-start.7) | collective-permute-done | bytes 327712 | tf_op jit(solution)/shard_map/ppermute | solution.py:504
  53.3 0.0 collective-permute-done.11.held_other_ref.other_ref
  53.3 1.7 %first.1 = (f32[640,256]{1,0:T(8,128)S(1)}, bf16[256,2048]{1,0:T(8,128)(2,1)S(1)}, f32[16,128]{1,0:T(8,128)S(1)}, f32[16,16,128]{2,1,0:T(8,128)S(1)}) custom-call(s32[5]{0:T(128)S(1)} %pad_add_fusion.place_ref, f32[4,32,1,640]{3,2,1,0:T(1,128)S(1)} %pad_maximum_fusion.own_ref, f32[4,32,1,640]{3,2,1,0:T(1,128)S(1)} %collective-permute-done.7.other_ref, ...), custom_call_target="tpu_custom_call" | custom-call | flops 2000000 | bytes 3000000 | tf_op jit(solution)/shard_map/first/pallas_call | solution.py:525
  55.0 12.9 %all_to_all.15.parts_ref = f32[16,16,128]{2,1,0:T(8,128)S(1)} all-to-all(f32[16,16,128]{2,1,0:T(8,128)S(1)} %get-tuple-element.37), channel_id=1, replica_groups=mesh['narrow'=4,'y'=4,'z'=8,'core'=2] {'narrow','y'}, dimensions={0} | all-to-all | bytes 262144 | tf_op jit(solution)/shard_map/all_to_all | solution.py:520
  67.9 2.2 %second.1 = (f32[16,128]{1,0:T(8,128)S(1)}, f32[16,16,128]{2,1,0:T(8,128)}) custom-call(f32[640,256]{1,0:T(8,128)S(1)} %get-tuple-element.34.packed_ref, bf16[256,2048]{1,0:T(8,128)(2,1)S(1)} %get-tuple-element.35.slots_ref, f32[16,128]{1,0:T(8,128)S(1)} %get-tuple-element.36.rhs_ref, f32[16,16,128]{2,1,0:T(8,128)S(1)} %all_to_all.15.parts_ref, ...), custom_call_target="tpu_custom_call" | custom-call | flops 2000000 | bytes 3000000 | tf_op jit(solution)/shard_map/second/pallas_call | solution.py:539
  70.1 5.1 %all-to-all-start.2 = ((f32[16,16,128]{2,1,0:T(8,128)}), f32[16,16,128]{2,1,0:T(8,128)S(1)}, u32[]{:S(2)}, u32[]{:S(2)}) async-start(f32[16,16,128]{2,1,0:T(8,128)} %get-tuple-element.39), calls=%async_computation.2 | async-start | bytes 262144 | tf_op jit(solution)/shard_map/all_to_all | solution.py:520
  75.2 0.1 reshape.37.range_ref
  75.3 0.1 reshape.40
  75.3 0.7 copy.27
  76.1 0.9 %local.1.local_ref = f32[3,4,8,256]{3,2,1,0:T(8,128)S(1)} custom-call(s32[4]{0:T(128)S(1)} %reshape.37.range_ref, bf16[12,12,5,3,256]{4,3,2,1,0:T(4,128)(2,1)S(1)} %bitcast.30, bf16[3,4,8,256]{3,2,1,0:T(8,128)(2,1)S(1)} %copy.26.r_ref, bf16[27,8,256]{2,1,0:T(8,128)(2,1)S(1)} %get-tuple-element.55.xlo_ref, bf16[27,8,256]{2,1,0:T(8,128)(2,1)S(1)} %get-tuple-element.54.xhi_ref, ...), custom_call_target="tpu_custom_call" | custom-call | flops 2000000 | bytes 3000000 | tf_op jit(solution)/shard_map/local/pallas_call | solution.py:506
  77.0 4.6 %all-to-all-done.2.parts_ref = f32[16,16,128]{2,1,0:T(8,128)S(1)} async-done(((f32[16,16,128]{2,1,0:T(8,128)}), f32[16,16,128]{2,1,0:T(8,128)S(1)}, u32[]{:S(2)}, u32[]{:S(2)}) %all-to-all-start.2) | async-done | bytes 131104 | tf_op jit(solution)/shard_map/all_to_all | solution.py:520
  81.6 1.4 %last.1 = (f32[3,4,8,256]{3,2,1,0:T(8,128)}, f32[16,128]{1,0:T(8,128)}) custom-call(s32[9]{0:T(128)S(1)} %bitcast.34, bf16[8,3,4,8,256]{4,3,2,1,0:T(8,128)(2,1)S(1)} %copy-done, f32[3,4,8,256]{3,2,1,0:T(8,128)S(1)} %local.1.local_ref, f32[16,128]{1,0:T(8,128)S(1)} %get-tuple-element.38.first_ref, f32[16,16,128]{2,1,0:T(8,128)S(1)} %all-to-all-done.2.parts_ref), custom_call_target="tpu_custom_call" | custom-call | flops 1000000 | bytes 1000000 | tf_op jit(solution)/shard_map/last/pallas_call | solution.py:547
  (33 shorter events, 0.2 us)
Async XLA Ops:
  0.6 9.0 %copy-start = (bf16[8,3,4,8,256]{4,3,2,1,0:T(8,128)(2,1)S(1)}, bf16[8,3,4,8,256]{4,3,2,1,0:T(8,128)(2,1)}, u32[]{:S(2)}) copy-start(bf16[8,3,4,8,256]{4,3,2,1,0:T(8,128)(2,1)} %z_ref.3) | copy-start | bytes 1179652
  0.6 8.7 %copy-start.7 = (f32[3,4,8,256]{3,2,1,0:T(8,128)S(1)}, f32[3,4,8,256]{3,2,1,0:T(8,128)}, u32[]{:S(2)}) copy-start(f32[3,4,8,256]{3,2,1,0:T(8,128)} %param.10) | copy-start | bytes 294916
  0.7 6.6 %copy-start.6 = (f32[8,2048]{1,0:T(8,128)S(1)}, f32[8,2048]{1,0:T(8,128)}, u32[]{:S(2)}) copy-start(f32[8,2048]{1,0:T(8,128)} %param.15) | copy-start | bytes 196612
  0.7 9.0 %copy-start.5 = (s32[1,1,9]{2,1,0:T(1,128)S(1)}, s32[1,1,9]{2,1,0:T(1,128)}, u32[]{:S(2)}) copy-start(s32[1,1,9]{2,1,0:T(1,128)} %param.17) | copy-start | bytes 112
  0.7 9.0 %copy-start.4 = (f32[27,3,3]{0,2,1:T(4,128)S(1)}, f32[27,3,3]{0,2,1:T(4,128)}, u32[]{:S(2)}) copy-start(f32[27,3,3]{0,2,1:T(4,128)} %param.13) | copy-start | bytes 2920
  0.7 9.0 %copy-start.2 = (f32[4,8,256]{2,1,0:T(8,128)S(1)}, f32[4,8,256]{2,1,0:T(8,128)}, u32[]{:S(2)}) copy-start(f32[4,8,256]{2,1,0:T(8,128)} %stiff_ref.3) | copy-start | bytes 98308
  2.6 12.4 %collective-permute-start = (bf16[27,8,256]{2,1,0:T(8,128)(2,1)S(1)}, bf16[27,8,256]{2,1,0:T(8,128)(2,1)S(1)}, u32[]{:S(2)}, u32[]{:S(2)}) collective-permute-start(bf16[27,8,256]{2,1,0:T(8,128)(2,1)S(1)} %pad_maximum_fusion.3), channel_id=1, source_target_pairs={{0,64},{64,0},{128,192},{192,128},{1,65},{65,1},{129,193},{193,129... | collective-permute-start | bytes 331784 | tf_op jit(solution)/shard_map/ppermute | solution.py:439
  5.0 10.1 %collective-permute-start.1 = (bf16[27,8,256]{2,1,0:T(8,128)(2,1)S(1)}, bf16[27,8,256]{2,1,0:T(8,128)(2,1)S(1)}, u32[]{:S(2)}, u32[]{:S(2)}) collective-permute-start(bf16[27,8,256]{2,1,0:T(8,128)(2,1)S(1)} %pad_maximum_fusion.4), channel_id=1, source_target_pairs={{64,128},{128,64},{65,129},{129,65},{66,130},{130,66},{67,131},{13... | collective-permute-start | bytes 331784 | tf_op jit(solution)/shard_map/ppermute | solution.py:440
  7.3 4.4 %collective-permute-start.8 = (f32[8,2048]{1,0:T(8,128)S(1)}, f32[8,2048]{1,0:T(8,128)S(1)}, u32[]{:S(2)}, u32[]{:S(2)}) collective-permute-start(f32[8,2048]{1,0:T(8,128)S(1)} %copy-done.6), channel_id=1, source_target_pairs={{0,2},{2,0},{4,6},{6,4},{8,10},{10,8},{12,14},{14,12},{1,3},{3,1},... | collective-permute-start | bytes 196616 | tf_op jit(solution)/shard_map/ppermute | solution.py:468
  9.5 6.7 %copy-start.3 = (f32[4,8,256]{2,1,0:T(8,128)S(1)}, f32[4,8,256]{2,1,0:T(8,128)}, u32[]{:S(2)}) copy-start(f32[4,8,256]{2,1,0:T(8,128)} %mass_ref.1) | copy-start | bytes 98308
  11.7 8.3 %collective-permute-start.9 = (f32[16,2048]{1,0:T(8,128)S(1)}, f32[16,2048]{1,0:T(8,128)S(1)}, u32[]{:S(2)}, u32[]{:S(2)}) collective-permute-start(f32[16,2048]{1,0:T(8,128)S(1)} %pad_maximum_fusion.2), channel_id=1, source_target_pairs={{0,4},{2,6},{4,0},{6,2},{8,12},{10,14},{12,8},{14,10},{1,5},{3,7},... | collective-permute-start | bytes 393224 | tf_op jit(solution)/shard_map/ppermute | solution.py:468
  15.4 9.5 %collective-permute-start.3 = (bf16[27,6,256]{2,1,0:T(8,128)(2,1)S(1)}, bf16[27,6,256]{2,1,0:T(8,128)(2,1)S(1)}, u32[]{:S(2)}, u32[]{:S(2)}) collective-permute-start(bf16[27,6,256]{2,1,0:T(8,128)(2,1)S(1)} %get-tuple-element.52), channel_id=1, source_target_pairs={{0,1},{1,0},{2,3},{3,2},{4,5},{5,4},{6,7},{7,6},{8,9},{9,8},{10,11... | collective-permute-start | bytes 248840 | tf_op jit(solution)/shard_map/ppermute | solution.py:439
  15.5 9.4 %collective-permute-start.2 = (bf16[27,6,256]{2,1,0:T(8,128)(2,1)S(1)}, bf16[27,6,256]{2,1,0:T(8,128)(2,1)S(1)}, u32[]{:S(2)}, u32[]{:S(2)}) collective-permute-start(bf16[27,6,256]{2,1,0:T(8,128)(2,1)S(1)} %get-tuple-element.53), channel_id=1, source_target_pairs={{1,2},{2,1},{3,4},{4,3},{5,6},{6,5},{7,8},{8,7},{9,10},{10,9},{11,... | collective-permute-start | bytes 248840 | tf_op jit(solution)/shard_map/ppermute | solution.py:440
  20.0 26.1 %collective-permute-start.10 = (f32[32,2048]{1,0:T(8,128)S(1)}, f32[32,2048]{1,0:T(8,128)S(1)}, u32[]{:S(2)}, u32[]{:S(2)}) collective-permute-start(f32[32,2048]{1,0:T(8,128)S(1)} %pad_maximum_fusion.1), channel_id=1, source_target_pairs={{0,12},{2,14},{4,8},{6,10},{8,4},{10,6},{12,0},{14,2},{1,13},{3,15... | collective-permute-start | bytes 786440 | tf_op jit(solution)/shard_map/ppermute | solution.py:468
  27.0 15.1 %all-to-all-start = ((f32[32,1,640]{2,1,0:T(1,128)}), f32[32,1,640]{2,1,0:T(1,128)S(1)}, u32[]{:S(2)}, u32[]{:S(2)}) async-start(f32[32,1,640]{2,1,0:T(1,128)} %get-tuple-element.33), calls=%async_computation | async-start | bytes 163840 | tf_op jit(solution)/shard_map/all_to_all | solution.py:501
  42.0 6.9 %collective-permute-start.6 = (f32[32,1,640]{2,1,0:T(1,128)S(1)}, f32[32,1,640]{2,1,0:T(1,128)S(1)}, u32[]{:S(2)}, u32[]{:S(2)}) collective-permute-start(f32[32,1,640]{2,1,0:T(1,128)S(1)} %all-to-all-done), channel_id=1, source_target_pairs={{0,48},{16,32},{32,16},{48,0},{1,49},{17,33},{33,17},{49,1},{2,50}... | collective-permute-start | bytes 245768 | tf_op jit(solution)/shard_map/ppermute | solution.py:502
  45.2 6.1 %collective-permute-start.5 = (f32[32,1,640]{2,1,0:T(1,128)S(1)}, f32[32,1,640]{2,1,0:T(1,128)S(1)}, u32[]{:S(2)}, u32[]{:S(2)}) collective-permute-start(f32[32,1,640]{2,1,0:T(1,128)S(1)} %all-to-all-done), channel_id=1, source_target_pairs={{0,32},{16,48},{32,0},{48,16},{1,33},{17,49},{33,1},{49,17},{2,34}... | collective-permute-start | bytes 245768 | tf_op jit(solution)/shard_map/ppermute | solution.py:502
  45.7 5.6 %collective-permute-start.4 = (f32[32,1,640]{2,1,0:T(1,128)S(1)}, f32[32,1,640]{2,1,0:T(1,128)S(1)}, u32[]{:S(2)}, u32[]{:S(2)}) collective-permute-start(f32[32,1,640]{2,1,0:T(1,128)S(1)} %all-to-all-done), channel_id=1, source_target_pairs={{0,16},{16,0},{32,48},{48,32},{1,17},{17,1},{33,49},{49,33},{2,18}... | collective-permute-start | bytes 245768 | tf_op jit(solution)/shard_map/ppermute | solution.py:502
  46.2 7.1 %collective-permute-start.11 = (f32[64,2048]{1,0:T(8,128)S(1)}, f32[64,2048]{1,0:T(8,128)S(1)}, u32[]{:S(2)}, u32[]{:S(2)}) collective-permute-start(f32[64,2048]{1,0:T(8,128)S(1)} %constant_dynamic-update-slice_fusion.held_ref.own_ref), channel_id=1, source_target_pairs={{0,1},{1,0},{2,3},{3,2},{4,5},{5,4},{6,7},{7,6},{8,9},{9,8},{10,11... | collective-permute-start | bytes 1572872 | tf_op jit(solution)/shard_map/ppermute | solution.py:505
  51.6 1.7 %collective-permute-start.7 = (f32[4,32,1,640]{3,2,1,0:T(1,128)S(1)}, f32[4,32,1,640]{3,2,1,0:T(1,128)S(1)}, u32[]{:S(2)}, u32[]{:S(2)}) collective-permute-start(f32[4,32,1,640]{3,2,1,0:T(1,128)S(1)} %pad_maximum_fusion.own_ref), channel_id=1, source_target_pairs={{0,1},{1,0},{2,3},{3,2},{4,5},{5,4},{6,7},{7,6},{8,9},{9,8},{10,11... | collective-permute-start | bytes 983048 | tf_op jit(solution)/shard_map/ppermute | solution.py:504
  67.9 7.2 %copy-start.8 = (s32[1,1,2,2]{3,2,1,0:T(2,128)S(1)}, s32[1,1,2,2]{3,2,1,0:T(2,128)}, u32[]{:S(2)}) copy-start(s32[1,1,2,2]{3,2,1,0:T(2,128)} %param.16) | copy-start | bytes 52
  67.9 8.1 %copy-start.1 = (bf16[12,12,3,5,256]{4,2,3,1,0:T(4,128)(2,1)S(1)}, bf16[12,12,3,5,256]{4,2,3,1,0:T(4,128)(2,1)}, u32[]{:S(2)}) copy-start(bf16[12,12,3,5,256]{4,2,3,1,0:T(4,128)(2,1)} %param.14) | copy-start | bytes 3317764
  70.1 11.4 %all-to-all-start.2 = ((f32[16,16,128]{2,1,0:T(8,128)}), f32[16,16,128]{2,1,0:T(8,128)S(1)}, u32[]{:S(2)}, u32[]{:S(2)}) async-start(f32[16,16,128]{2,1,0:T(8,128)} %get-tuple-element.39), calls=%async_computation.2 | async-start | bytes 262144 | tf_op jit(solution)/shard_map/all_to_all | solution.py:520

commit v5 on v4

--- a/solution.py
+++ b/solution.py
@@ -218,7 +218,16 @@
         pay_ref[place] = line
 
 
-def local_kernel(range_ref, inverse_ref, r_ref, xlo_ref, xhi_ref, ylo_ref, yhi_ref, out_ref, ext_ref, sol_ref):
+def local_kernel(
+    range_ref, inverse_ref, r_ref, xlo_ref, xhi_ref, ylo_ref, yhi_ref, table_ref, out_ref, blocks_ref, ext_ref, sol_ref
+):
+    table = table_ref[...]
+    lane = lax.broadcasted_iota(jnp.int32, table.shape, 1)
+    for b in range(8):
+        lines = jnp.zeros(table.shape, F32)
+        for n in range(9):
+            lines = jnp.where(lane == n, table[:, n * 8 + b : n * 8 + b + 1], lines)
+        blocks_ref[:, b, :] = lines[:, :9]
     cells_x, cells_y = r_ref.shape[1:3]
     ext_x, ext_y = cells_x + 2, cells_y + 2
     half_x, half_y = ext_x // 2, ext_y // 2
@@ -303,15 +312,16 @@
 
 
 def first_kernel(
-    n_narrow, size_z, place_ref, own_ref, other_ref, held_ref, held_other_ref, packed_ref, slots_ref, rhs_ref, share_ref, rows_ref
+    n_narrow, size_z, row_ref, core_ref, own_ref, other_ref, held_ref, held_other_ref, packed_ref, slots_ref, rhs_ref, share_ref, rows_ref
 ):
     size_y = own_ref.shape[0]
     chips = n_narrow * size_y * size_z
-    for got_ref, core in ((own_ref, place_ref[size_y]), (other_ref, 1 - place_ref[size_y])):
+    for got_ref, core in ((own_ref, core_ref[0]), (other_ref, 1 - core_ref[0])):
         for y in range(size_y):
+            step = jnp.bitwise_xor(row_ref[0], y)
             for x in range(n_narrow):
-                place = pl.multiple_of(core * chips + (x * size_y + place_ref[y]) * size_z, 8)
-                block = got_ref[y, x * size_z : (x + 1) * size_z]
+                place = pl.multiple_of(core * chips + (x * size_y + y) * size_z, 8)
+                block = got_ref[step, x * size_z : (x + 1) * size_z]
                 rows_ref[pl.ds(place, size_z), :] = block.reshape(size_z, block.shape[2])
     rows = rows_ref[...]
     ids = jnp.broadcast_to(rows[:, 73:74].astype(jnp.int32), slots_ref.shape)
@@ -499,28 +509,28 @@
         name="outer",
     )(y_matrix, table, zy, sy, ylo, yhi)
     got = lax.all_to_all(payload, ("narrow", "z"), 0, 0)
+    local, blocks = call(
+        local_kernel,
+        [(3, cells_x, cells_y, depth), (vectors, vectors, 9)],
+        [SMEM] + [VMEM] * 7,
+        [pltpu.VMEM((3, cells_y + 2, 2, 8, depth // 2), F32)] * 2,
+        flops=2_000_000,
+        moved=3_000_000,
+        name="local",
+    )(ranges, local_inverse.transpose(0, 1, 3, 2, 4), rounded, xlo, xhi, ylo, yhi, table)
+    got, local = lax.optimization_barrier((got, local))
     got = [got] + [lax.ppermute(got, "y", [(k, k ^ step) for k in range(size_y)]) for step in range(1, size_y)]
     got = jnp.stack(got)
     other = lax.ppermute(got, "core", [(0, 1), (1, 0)])
     held = [rows_z, lax.ppermute(rows_z, "core", [(0, 1), (1, 0)])]
-    (local,) = call(
-        local_kernel,
-        [(3, cells_x, cells_y, depth)],
-        [SMEM] + [VMEM] * 6,
-        [pltpu.VMEM((3, cells_y + 2, 2, 8, depth // 2), F32)] * 2,
-        flops=2_000_000,
-        moved=3_000_000,
-        name="local",
-    )(ranges, local_inverse.transpose(0, 1, 3, 2, 4), rounded, xlo, xhi, ylo, yhi)
-
     group = ("narrow", "y")
     members = lax.axis_size(group)
 
     def spread(share):
         return lax.all_to_all(share, group, 0, 0)
 
-    steps = jnp.arange(size_y, dtype=jnp.int32) ^ lax.axis_index("y")
-    core = jnp.append(steps, lax.axis_index("core").astype(jnp.int32))
+    row = lax.axis_index("y").astype(jnp.int32).reshape(1)
+    core = lax.axis_index("core").astype(jnp.int32).reshape(1)
     flat = (count * vectors // 128, 128)
     packed, slots, rhs, share = call(
         functools.partial(first_kernel, n_narrow, size_z),
@@ -530,12 +540,12 @@
             flat,
             (members,) + flat,
         ],
-        [SMEM] + [VMEM] * 4,
+        [SMEM] * 2 + [VMEM] * 4,
         [pltpu.VMEM((count, SLOT * vectors), F32)],
         flops=2_000_000,
         moved=3_000_000,
         name="first",
-    )(core, got, other, *held)
+    )(row, core, got, other, *held)
     first, share = call(
         functools.partial(second_kernel, n_narrow),
         [flat, (members,) + flat],
@@ -553,7 +563,7 @@
         name="last",
     )(ids, deflation, local, first, spread(share))
     coarse_solution = solved.reshape(-1)
-    blocks = table[:, : 9 * vectors].reshape(vectors, 9, vectors).transpose(1, 0, 2)
+    blocks = blocks.transpose(2, 0, 1)
     return preconditioned, blocks.reshape(1, 1, 9, vectors, vectors), coarse_solution
 
 

time: 83.3 us -> 80.6 us (0.968)
  blocking collectives: 12.9 us -> 23.3 us
  waiting for transfers between devices: 22.1 us -> 14.9 us
  starting transfers between devices: 31.8 us -> 26.1 us
    all_to_all x1 -> x2, blocking collectives: 12.9 us -> 23.3 us  [spread(): return lax.all_to_all(share, group, 0, 0)]
    all_to_all x1 -> x0, starting transfers between devices: 5.05 us -> none  [spread(): return lax.all_to_all(share, group, 0, 0)]
    all_to_all x1 -> x0, waiting for transfers between devices: 4.57 us -> none  [spread(): return lax.all_to_all(share, group, 0, 0)]
    ppermute x2, starting transfers between devices: 2.45 us -> 0.73 us  [exchanged(): one = lax.ppermute(chosen(sending_high, sending_low), axis, even)]
    ppermute x2, starting transfers between devices: 2.99 us -> 4.71 us  [exchanged(): two = lax.ppermute(chosen(sending_low, sending_high), axis, odd)]
    all_to_all x1, waiting for transfers between devices: 8.88 us -> 7.21 us  [body(): got = lax.all_to_all(payload, ('narrow', 'z'), 0, 0)]
    all_to_all x1, starting transfers between devices: 6.17 us -> 7.31 us  [body(): got = lax.all_to_all(payload, ('narrow', 'z'), 0, 0)]
    ppermute x3, starting transfers between devices: 10.2 us -> 9.1 us  [joined(): lax.ppermute(rows, 'z', [(k, partner(k) % size_z) for k in range(size_z)])]
  transfers between devices with their start and end apart: 14 -> 13, of which waited for: 7 -> 5; matrix products, arithmetic and copies ran while one was open for 2% -> 5% of each run, Pallas kernels for 7% -> 9%
where the time goes in v5:
time: 80.6 us; the launch traced here: 80.2 us
  starting transfers between devices  26.1 us (32%)
  blocking collectives  23.3 us (29%)
  waiting for transfers between devices  14.9 us (18%)
  Pallas kernels  11 us (14%)
  local copies, waits for them, and re-layouts  2.46 us (3%)
  other arithmetic  1.38 us (2%)
  between operations  0.99 us (1%)
    all_to_all x2, blocking collectives, spread(): return lax.all_to_all(share, group, 0, 0)  23.3 us
    ppermute x3, starting transfers between devices, joined(): lax.ppermute(rows, 'z', [(k, partner(k) % size_z) for k in range(size_z)])  9.1 us
    all_to_all x1, starting transfers between devices, body(): got = lax.all_to_all(payload, ('narrow', 'z'), 0, 0)  7.31 us
    all_to_all x1, waiting for transfers between devices, body(): got = lax.all_to_all(payload, ('narrow', 'z'), 0, 0)  7.21 us
    ppermute x2, starting transfers between devices, exchanged(): two = lax.ppermute(chosen(sending_low, sending_high), axis, odd)  4.71 us
    ppermute x3, starting transfers between devices, body(): lax.ppermute(got, 'y', [(k, k ^ step) for k in range(size_y)])  4.09 us
    ppermute x3, waiting for transfers between devices, body(): lax.ppermute(got, 'y', [(k, k ^ step) for k in range(size_y)])  3.79 us
    ppermute x3, waiting for transfers between devices, joined(): lax.ppermute(rows, 'z', [(k, partner(k) % size_z) for k in range(size_z)])  2.29 us
  transfers between devices with their start and end apart: 13, of which 5 were waited for; matrix products, arithmetic and copies ran while one was open for 5% of the time, Pallas kernels for 9%

profile of v5, /device:TPU:2, one launch (start us, length us, event | category | flops | bytes accessed | tf_op | source)
XLA Modules:
  0.0 80.2 jit_solution(10430934626463356359)
XLA Ops:
  0.6 0.0 copy-start.6
  0.7 0.0 copy-start.7
  0.7 2.0 %collective-permute-start.8 = (f32[8,2048]{1,0:T(8,128)}, f32[8,2048]{1,0:T(8,128)S(1)}, u32[]{:S(2)}, u32[]{:S(2)}) collective-permute-start(f32[8,2048]{1,0:T(8,128)} %param.15), channel_id=1, source_target_pairs={{0,2},{2,0},{4,6},{6,4},{8,10},{10,8},{12,14},{14,12},{1,3},{3,1},... | collective-permute-start | bytes 196616 | tf_op jit(solution)/shard_map/ppermute | solution.py:478
  2.7 1.0 %copy.20 = bf16[8,3,4,8,256]{4,3,1,0,2:T(8,128)(2,1)S(1)} copy(bf16[8,3,4,8,256]{4,3,2,1,0:T(8,128)(2,1)} %z_ref.3) | data formatting | bytes 786432 | tf_op args[0]
  3.7 0.8 select_bitcast_fusion.2
  4.5 0.6 collective-permute-start
  5.2 4.0 %collective-permute-start.1 = (bf16[27,8,256]{2,1,0:T(8,128)(2,1)S(1)}, bf16[27,8,256]{2,1,0:T(8,128)(2,1)S(1)}, u32[]{:S(2)}, u32[]{:S(2)}) collective-permute-start(bf16[27,8,256]{2,1,0:T(8,128)(2,1)S(1)} %pad_maximum_fusion.4), channel_id=1, source_target_pairs={{64,128},{128,64},{65,129},{129,65},{66,130},{130,66},{67,131},{13... | collective-permute-start | bytes 331784 | tf_op jit(solution)/shard_map/ppermute | solution.py:450
  9.3 0.1 fusion
  9.4 0.0 copy-start.3
  9.5 0.1 copy_bitcast_fusion
  9.6 0.1 reshape.37.range_ref
  9.7 1.4 %before.1 = (f32[8,3,4,8,256]{4,3,2,1,0:T(8,128)S(1)}, f32[2,8,3,8,256]{4,3,2,1,0:T(8,128)S(1)}, f32[2,8,256]{2,1,0:T(8,128)S(1)}, f32[8,128]{1,0:T(8,128)S(1)},...) custom-call(f32[3,3,27]{2,1,0:T(4,128)S(1)} %bitcast.31, s32[9]{0:T(128)S(1)} %bitcast.32, ...), custom_call_target="tpu_custom_call" | custom-call | flops 20000000 | bytes 1000000 | tf_op jit(solution)/shard_map/before/pallas_call | solution.py:460
  11.2 0.0 collective-permute-done.8
  11.2 3.4 %collective-permute-start.9 = (f32[16,2048]{1,0:T(8,128)S(1)}, f32[16,2048]{1,0:T(8,128)S(1)}, u32[]{:S(2)}, u32[]{:S(2)}) collective-permute-start(f32[16,2048]{1,0:T(8,128)S(1)} %pad_maximum_fusion.2), channel_id=1, source_target_pairs={{0,4},{2,6},{4,0},{6,2},{8,12},{10,14},{12,8},{14,10},{1,5},{3,7},... | collective-permute-start | bytes 393224 | tf_op jit(solution)/shard_map/ppermute | solution.py:478
  14.5 0.0 collective-permute-done
  14.5 0.0 collective-permute-done.1
  14.6 0.1 fusion.1
  14.7 0.2 broadcast_select_fusion.2
  14.9 0.1 collective-permute-start.3
  15.0 0.7 collective-permute-start.2
  15.7 0.0 copy-start.1
  15.7 1.9 %inner.1.table_ref = f32[8,128]{1,0:T(8,128)S(1)} custom-call(bf16[288,256]{1,0:T(8,128)(2,1)S(1)} %get-tuple-element.28.own_ref, bf16[144,256]{1,0:T(8,128)(2,1)S(1)} %get-tuple-element.29.x_ref, f32[8,3,4,8,256]{4,3,2,1,0:T(8,128)S(1)} %get-tuple-element.30.zf_ref, f32[4,8,256]{2,1,0:T(8,128)S(1)} %copy-done.2, f32[4,8,256]{2,1,0:T(8,128)S(1)} %copy-done.3, ...), custom_call_target="tpu_custom_call" | custom-call | flops 10000000 | bytes 1000000 | tf_op jit(solution)/shard_map/inner/pallas_call | solution.py:492
  17.5 2.3 %collective-permute-done.9 = f32[16,2048]{1,0:T(8,128)S(1)} collective-permute-done((f32[16,2048]{1,0:T(8,128)S(1)}, f32[16,2048]{1,0:T(8,128)S(1)}, u32[]{:S(2)}, u32[]{:S(2)}) %collective-permute-start.9) | collective-permute-done | bytes 131104 | tf_op jit(solution)/shard_map/ppermute | solution.py:478
  19.8 3.7 %collective-permute-start.10 = (f32[32,2048]{1,0:T(8,128)S(1)}, f32[32,2048]{1,0:T(8,128)}, u32[]{:S(2)}, u32[]{:S(2)}) collective-permute-start(f32[32,2048]{1,0:T(8,128)S(1)} %pad_maximum_fusion.1), channel_id=1, source_target_pairs={{0,12},{2,14},{4,8},{6,10},{8,4},{10,6},{12,0},{14,2},{1,13},{3,15... | collective-permute-start | bytes 786440 | tf_op jit(solution)/shard_map/ppermute | solution.py:478
  23.6 0.0 collective-permute-done.3
  23.6 0.0 collective-permute-done.2
  23.6 2.0 %outer.1 = (f32[8,128]{1,0:T(8,128)S(1)}, f32[32,1,640]{2,1,0:T(1,128)}) custom-call(bf16[288,256]{1,0:T(8,128)(2,1)S(1)} %get-tuple-element.27.y_ref, f32[8,128]{1,0:T(8,128)S(1)} %inner.1.table_ref, f32[2,8,3,8,256]{4,3,2,1,0:T(8,128)S(1)} %get-tuple-element.35.zy_ref, f32[2,8,256]{2,1,0:T(8,128)S(1)} %get-tuple-element.36.sy_ref, ...), custom_call_target="tpu_custom_call" | custom-call | flops 10000000 | bytes 2000000 | tf_op jit(solution)/shard_map/outer/pallas_call | solution.py:502
  25.6 7.3 %all-to-all-start = ((f32[32,1,640]{2,1,0:T(1,128)}), f32[32,1,640]{2,1,0:T(1,128)S(1)}, u32[]{:S(2)}, u32[]{:S(2)}) async-start(f32[32,1,640]{2,1,0:T(1,128)} %get-tuple-element.37), calls=%async_computation | async-start | bytes 163840 | tf_op jit(solution)/shard_map/all_to_all | solution.py:511
  33.0 1.7 %local.1 = (f32[3,4,8,256]{3,2,1,0:T(8,128)S(1)}, f32[8,8,9]{2,1,0:T(8,128)}) custom-call(s32[4]{0:T(128)S(1)} %reshape.37.range_ref, bf16[12,12,5,3,256]{4,3,2,1,0:T(4,128)(2,1)S(1)} %bitcast.30, bf16[3,4,8,256]{3,2,1,0:T(8,128)(2,1)S(1)} %copy.19.r_ref, bf16[27,8,256]{2,1,0:T(8,128)(2,1)S(1)} %get-tuple-element.60.xlo_ref, ...), custom_call_target="tpu_custom_call" | custom-call | flops 2000000 | bytes 3000000 | tf_op jit(solution)/shard_map/local/pallas_call | solution.py:512
  34.7 7.2 %all-to-all-done = f32[32,1,640]{2,1,0:T(1,128)S(1)} async-done(((f32[32,1,640]{2,1,0:T(1,128)}), f32[32,1,640]{2,1,0:T(1,128)S(1)}, u32[]{:S(2)}, u32[]{:S(2)}) %all-to-all-start) | async-done | bytes 81952 | tf_op jit(solution)/shard_map/all_to_all | solution.py:511
  41.9 3.0 %collective-permute-start.6 = (f32[32,1,640]{2,1,0:T(1,128)S(1)}, f32[32,1,640]{2,1,0:T(1,128)S(1)}, u32[]{:S(2)}, u32[]{:S(2)}) collective-permute-start(f32[32,1,640]{2,1,0:T(1,128)S(1)} %all-to-all-done), channel_id=1, source_target_pairs={{0,48},{16,32},{32,16},{48,0},{1,49},{17,33},{33,17},{49,1},{2,50}... | collective-permute-start | bytes 245768 | tf_op jit(solution)/shard_map/ppermute | solution.py:522
  44.9 0.6 collective-permute-start.5
  45.5 0.5 collective-permute-start.4
  46.0 0.0 collective-permute-done.10
  46.0 1.0 %constant_dynamic-update-slice_fusion.held_ref.own_ref = f32[64,2048]{1,0:T(8,128)S(1)} fusion(f32[64,2048]{1,0:T(8,128)S(1)} %constant_dynamic-update-slice_fusion.1, f32[32,2048]{1,0:T(8,128)} %collective-permute-done.10), kind=kLoop, calls=%fused_computation.20 | loop fusion | bytes 524288 | tf_op jit(solution)/shard_map/concatenate | solution.py:478
  46.9 0.1 collective-permute-start.11
  47.0 1.4 %collective-permute-done.6 = f32[32,1,640]{2,1,0:T(1,128)S(1)} collective-permute-done((f32[32,1,640]{2,1,0:T(1,128)S(1)}, f32[32,1,640]{2,1,0:T(1,128)S(1)}, u32[]{:S(2)}, u32[]{:S(2)}) %collective-permute-start.6) | collective-permute-done | bytes 81952 | tf_op jit(solution)/shard_map/ppermute | solution.py:522
  48.4 2.4 %collective-permute-done.5 = f32[32,1,640]{2,1,0:T(1,128)S(1)} collective-permute-done((f32[32,1,640]{2,1,0:T(1,128)S(1)}, f32[32,1,640]{2,1,0:T(1,128)S(1)}, u32[]{:S(2)}, u32[]{:S(2)}) %collective-permute-start.5) | collective-permute-done | bytes 81952 | tf_op jit(solution)/shard_map/ppermute | solution.py:522
  50.8 0.0 collective-permute-done.4
  50.8 0.3 pad_maximum_fusion.own_ref
  51.1 0.1 collective-permute-start.7
  51.2 1.6 %collective-permute-done.7.other_ref = f32[4,32,1,640]{3,2,1,0:T(1,128)S(1)} collective-permute-done((f32[4,32,1,640]{3,2,1,0:T(1,128)S(1)}, f32[4,32,1,640]{3,2,1,0:T(1,128)S(1)}, u32[]{:S(2)}, u32[]{:S(2)}) %collective-permute-start.7) | collective-permute-done | bytes 327712 | tf_op jit(solution)/shard_map/ppermute | solution.py:524
  52.8 0.0 collective-permute-done.11.held_other_ref.other_ref
  52.8 1.1 %first.1 = (f32[640,256]{1,0:T(8,128)S(1)}, bf16[256,2048]{1,0:T(8,128)(2,1)S(1)}, f32[16,128]{1,0:T(8,128)S(1)}, f32[16,16,128]{2,1,0:T(8,128)S(1)}) custom-call(s32[1]{0:T(128)} %bitcast.12.row_ref, s32[1]{0:T(128)} %bitcast.13.core_ref, f32[4,32,1,640]{3,2,1,0:T(1,128)S(1)} %pad_maximum_fusion.own_ref, ...), custom_call_target="tpu_custom_call" | custom-call | flops 2000000 | bytes 3000000 | tf_op jit(solution)/shard_map/first/pallas_call | solution.py:535
  54.0 12.0 %all_to_all.15.parts_ref = f32[16,16,128]{2,1,0:T(8,128)S(1)} all-to-all(f32[16,16,128]{2,1,0:T(8,128)S(1)} %get-tuple-element.45), channel_id=1, replica_groups=mesh['narrow'=4,'y'=4,'z'=8,'core'=2] {'narrow','y'}, dimensions={0} | all-to-all | bytes 262144 | tf_op jit(solution)/shard_map/all_to_all | solution.py:530
  66.0 1.5 %second.1 = (f32[16,128]{1,0:T(8,128)S(1)}, f32[16,16,128]{2,1,0:T(8,128)S(1)}) custom-call(f32[640,256]{1,0:T(8,128)S(1)} %get-tuple-element.42.packed_ref, bf16[256,2048]{1,0:T(8,128)(2,1)S(1)} %get-tuple-element.43.slots_ref, f32[16,128]{1,0:T(8,128)S(1)} %get-tuple-element.44.rhs_ref, f32[16,16,128]{2,1,0:T(8,128)S(1)} %all_to_all.15.parts_ref, ...), custom_call_target="tpu_custom_call" | custom-call | flops 2000000 | bytes 3000000 | tf_op jit(solution)/shard_map/second/pallas_call | solution.py:549
  67.6 11.2 %all_to_all.16.parts_ref = f32[16,16,128]{2,1,0:T(8,128)S(1)} all-to-all(f32[16,16,128]{2,1,0:T(8,128)S(1)} %get-tuple-element.47), channel_id=1, replica_groups=mesh['narrow'=4,'y'=4,'z'=8,'core'=2] {'narrow','y'}, dimensions={0} | all-to-all | bytes 262144 | tf_op jit(solution)/shard_map/all_to_all | solution.py:530
  78.8 1.4 %last.1 = (f32[3,4,8,256]{3,2,1,0:T(8,128)}, f32[16,128]{1,0:T(8,128)}) custom-call(s32[9]{0:T(128)S(1)} %bitcast.33, bf16[8,3,4,8,256]{4,3,2,1,0:T(8,128)(2,1)S(1)} %copy-done, f32[3,4,8,256]{3,2,1,0:T(8,128)S(1)} %get-tuple-element.40.local_ref, f32[16,128]{1,0:T(8,128)S(1)} %get-tuple-element.46.first_ref, f32[16,16,128]{2,1,0:T(8,128)S(1)} %all_to_all.16.parts_ref), custom_call_target="tpu_custom_call" | custom-call | flops 1000000 | bytes 1000000 | tf_op jit(solution)/shard_map/last/pallas_call | solution.py:557
  (28 shorter events, 0.2 us)
Async XLA Ops:
  0.6 8.8 %copy-start.6 = (f32[8,2048]{1,0:T(8,128)S(1)}, f32[8,2048]{1,0:T(8,128)}, u32[]{:S(2)}) copy-start(f32[8,2048]{1,0:T(8,128)} %param.15) | copy-start | bytes 196612
  0.6 9.1 %copy-start = (bf16[8,3,4,8,256]{4,3,2,1,0:T(8,128)(2,1)S(1)}, bf16[8,3,4,8,256]{4,3,2,1,0:T(8,128)(2,1)}, u32[]{:S(2)}) copy-start(bf16[8,3,4,8,256]{4,3,2,1,0:T(8,128)(2,1)} %z_ref.3) | copy-start | bytes 1179652
  0.7 8.6 %copy-start.7 = (f32[3,4,8,256]{3,2,1,0:T(8,128)S(1)}, f32[3,4,8,256]{3,2,1,0:T(8,128)}, u32[]{:S(2)}) copy-start(f32[3,4,8,256]{3,2,1,0:T(8,128)} %param.10) | copy-start | bytes 294916
  0.7 8.9 %copy-start.8 = (s32[1,1,2,2]{3,2,1,0:T(2,128)S(1)}, s32[1,1,2,2]{3,2,1,0:T(2,128)}, u32[]{:S(2)}) copy-start(s32[1,1,2,2]{3,2,1,0:T(2,128)} %param.16) | copy-start | bytes 52
  0.7 9.0 %copy-start.2 = (f32[4,8,256]{2,1,0:T(8,128)S(1)}, f32[4,8,256]{2,1,0:T(8,128)}, u32[]{:S(2)}) copy-start(f32[4,8,256]{2,1,0:T(8,128)} %stiff_ref.3) | copy-start | bytes 98308
  0.7 9.0 %copy-start.5 = (s32[1,1,9]{2,1,0:T(1,128)S(1)}, s32[1,1,9]{2,1,0:T(1,128)}, u32[]{:S(2)}) copy-start(s32[1,1,9]{2,1,0:T(1,128)} %param.17) | copy-start | bytes 112
  0.7 9.0 %copy-start.4 = (f32[27,3,3]{0,2,1:T(4,128)S(1)}, f32[27,3,3]{0,2,1:T(4,128)}, u32[]{:S(2)}) copy-start(f32[27,3,3]{0,2,1:T(4,128)} %param.13) | copy-start | bytes 2920
  0.7 10.5 %collective-permute-start.8 = (f32[8,2048]{1,0:T(8,128)}, f32[8,2048]{1,0:T(8,128)S(1)}, u32[]{:S(2)}, u32[]{:S(2)}) collective-permute-start(f32[8,2048]{1,0:T(8,128)} %param.15), channel_id=1, source_target_pairs={{0,2},{2,0},{4,6},{6,4},{8,10},{10,8},{12,14},{14,12},{1,3},{3,1},... | collective-permute-start | bytes 196616 | tf_op jit(solution)/shard_map/ppermute | solution.py:478
  4.5 10.0 %collective-permute-start = (bf16[27,8,256]{2,1,0:T(8,128)(2,1)S(1)}, bf16[27,8,256]{2,1,0:T(8,128)(2,1)S(1)}, u32[]{:S(2)}, u32[]{:S(2)}) collective-permute-start(bf16[27,8,256]{2,1,0:T(8,128)(2,1)S(1)} %pad_maximum_fusion.3), channel_id=1, source_target_pairs={{0,64},{64,0},{128,192},{192,128},{1,65},{65,1},{129,193},{193,129... | collective-permute-start | bytes 331784 | tf_op jit(solution)/shard_map/ppermute | solution.py:449
  5.2 9.3 %collective-permute-start.1 = (bf16[27,8,256]{2,1,0:T(8,128)(2,1)S(1)}, bf16[27,8,256]{2,1,0:T(8,128)(2,1)S(1)}, u32[]{:S(2)}, u32[]{:S(2)}) collective-permute-start(bf16[27,8,256]{2,1,0:T(8,128)(2,1)S(1)} %pad_maximum_fusion.4), channel_id=1, source_target_pairs={{64,128},{128,64},{65,129},{129,65},{66,130},{130,66},{67,131},{13... | collective-permute-start | bytes 331784 | tf_op jit(solution)/shard_map/ppermute | solution.py:450
  9.4 6.2 %copy-start.3 = (f32[4,8,256]{2,1,0:T(8,128)S(1)}, f32[4,8,256]{2,1,0:T(8,128)}, u32[]{:S(2)}) copy-start(f32[4,8,256]{2,1,0:T(8,128)} %mass_ref.1) | copy-start | bytes 98308
  11.2 8.6 %collective-permute-start.9 = (f32[16,2048]{1,0:T(8,128)S(1)}, f32[16,2048]{1,0:T(8,128)S(1)}, u32[]{:S(2)}, u32[]{:S(2)}) collective-permute-start(f32[16,2048]{1,0:T(8,128)S(1)} %pad_maximum_fusion.2), channel_id=1, source_target_pairs={{0,4},{2,6},{4,0},{6,2},{8,12},{10,14},{12,8},{14,10},{1,5},{3,7},... | collective-permute-start | bytes 393224 | tf_op jit(solution)/shard_map/ppermute | solution.py:478
  14.9 8.7 %collective-permute-start.3 = (bf16[27,6,256]{2,1,0:T(8,128)(2,1)S(1)}, bf16[27,6,256]{2,1,0:T(8,128)(2,1)S(1)}, u32[]{:S(2)}, u32[]{:S(2)}) collective-permute-start(bf16[27,6,256]{2,1,0:T(8,128)(2,1)S(1)} %get-tuple-element.57), channel_id=1, source_target_pairs={{0,1},{1,0},{2,3},{3,2},{4,5},{5,4},{6,7},{7,6},{8,9},{9,8},{10,11... | collective-permute-start | bytes 248840 | tf_op jit(solution)/shard_map/ppermute | solution.py:449
  15.0 8.6 %collective-permute-start.2 = (bf16[27,6,256]{2,1,0:T(8,128)(2,1)S(1)}, bf16[27,6,256]{2,1,0:T(8,128)(2,1)S(1)}, u32[]{:S(2)}, u32[]{:S(2)}) collective-permute-start(bf16[27,6,256]{2,1,0:T(8,128)(2,1)S(1)} %get-tuple-element.58), channel_id=1, source_target_pairs={{1,2},{2,1},{3,4},{4,3},{5,6},{6,5},{7,8},{8,7},{9,10},{10,9},{11,... | collective-permute-start | bytes 248840 | tf_op jit(solution)/shard_map/ppermute | solution.py:450
  15.7 17.3 %copy-start.1 = (bf16[12,12,3,5,256]{4,2,3,1,0:T(4,128)(2,1)S(1)}, bf16[12,12,3,5,256]{4,2,3,1,0:T(4,128)(2,1)}, u32[]{:S(2)}) copy-start(bf16[12,12,3,5,256]{4,2,3,1,0:T(4,128)(2,1)} %param.14) | copy-start | bytes 3317764
  19.8 26.1 %collective-permute-start.10 = (f32[32,2048]{1,0:T(8,128)S(1)}, f32[32,2048]{1,0:T(8,128)}, u32[]{:S(2)}, u32[]{:S(2)}) collective-permute-start(f32[32,2048]{1,0:T(8,128)S(1)} %pad_maximum_fusion.1), channel_id=1, source_target_pairs={{0,12},{2,14},{4,8},{6,10},{8,4},{10,6},{12,0},{14,2},{1,13},{3,15... | collective-permute-start | bytes 786440 | tf_op jit(solution)/shard_map/ppermute | solution.py:478
  25.6 16.2 %all-to-all-start = ((f32[32,1,640]{2,1,0:T(1,128)}), f32[32,1,640]{2,1,0:T(1,128)S(1)}, u32[]{:S(2)}, u32[]{:S(2)}) async-start(f32[32,1,640]{2,1,0:T(1,128)} %get-tuple-element.37), calls=%async_computation | async-start | bytes 163840 | tf_op jit(solution)/shard_map/all_to_all | solution.py:511
  41.9 6.5 %collective-permute-start.6 = (f32[32,1,640]{2,1,0:T(1,128)S(1)}, f32[32,1,640]{2,1,0:T(1,128)S(1)}, u32[]{:S(2)}, u32[]{:S(2)}) collective-permute-start(f32[32,1,640]{2,1,0:T(1,128)S(1)} %all-to-all-done), channel_id=1, source_target_pairs={{0,48},{16,32},{32,16},{48,0},{1,49},{17,33},{33,17},{49,1},{2,50}... | collective-permute-start | bytes 245768 | tf_op jit(solution)/shard_map/ppermute | solution.py:522
  44.9 5.9 %collective-permute-start.5 = (f32[32,1,640]{2,1,0:T(1,128)S(1)}, f32[32,1,640]{2,1,0:T(1,128)S(1)}, u32[]{:S(2)}, u32[]{:S(2)}) collective-permute-start(f32[32,1,640]{2,1,0:T(1,128)S(1)} %all-to-all-done), channel_id=1, source_target_pairs={{0,32},{16,48},{32,0},{48,16},{1,33},{17,49},{33,1},{49,17},{2,34}... | collective-permute-start | bytes 245768 | tf_op jit(solution)/shard_map/ppermute | solution.py:522
  45.5 5.3 %collective-permute-start.4 = (f32[32,1,640]{2,1,0:T(1,128)S(1)}, f32[32,1,640]{2,1,0:T(1,128)S(1)}, u32[]{:S(2)}, u32[]{:S(2)}) collective-permute-start(f32[32,1,640]{2,1,0:T(1,128)S(1)} %all-to-all-done), channel_id=1, source_target_pairs={{0,16},{16,0},{32,48},{48,32},{1,17},{17,1},{33,49},{49,33},{2,18}... | collective-permute-start | bytes 245768 | tf_op jit(solution)/shard_map/ppermute | solution.py:522
  46.9 5.9 %collective-permute-start.11 = (f32[64,2048]{1,0:T(8,128)S(1)}, f32[64,2048]{1,0:T(8,128)S(1)}, u32[]{:S(2)}, u32[]{:S(2)}) collective-permute-start(f32[64,2048]{1,0:T(8,128)S(1)} %constant_dynamic-update-slice_fusion.held_ref.own_ref), channel_id=1, source_target_pairs={{0,1},{1,0},{2,3},{3,2},{4,5},{5,4},{6,7},{7,6},{8,9},{9,8},{10,11... | collective-permute-start | bytes 1572872 | tf_op jit(solution)/shard_map/ppermute | solution.py:525
  51.1 1.7 %collective-permute-start.7 = (f32[4,32,1,640]{3,2,1,0:T(1,128)S(1)}, f32[4,32,1,640]{3,2,1,0:T(1,128)S(1)}, u32[]{:S(2)}, u32[]{:S(2)}) collective-permute-start(f32[4,32,1,640]{3,2,1,0:T(1,128)S(1)} %pad_maximum_fusion.own_ref), channel_id=1, source_target_pairs={{0,1},{1,0},{2,3},{3,2},{4,5},{5,4},{6,7},{7,6},{8,9},{9,8},{10,11... | collective-permute-start | bytes 983048 | tf_op jit(solution)/shard_map/ppermute | solution.py:524

commit v6 on v5

--- a/solution.py
+++ b/solution.py
@@ -312,7 +312,8 @@
 
 
 def first_kernel(
-    n_narrow, size_z, row_ref, core_ref, own_ref, other_ref, held_ref, held_other_ref, packed_ref, slots_ref, rhs_ref, share_ref, rows_ref
+    n_narrow, size_z, row_ref, core_ref, own_ref, other_ref, held0_ref, held1_ref, held2_ref,
+    packed_ref, slots_ref, rhs_ref, share_ref, rows_ref,
 ):
     size_y = own_ref.shape[0]
     chips = n_narrow * size_y * size_z
@@ -332,7 +333,7 @@
     own = jnp.concatenate([packed[a * SLOT + 72 : a * SLOT + 73, :] for a in range(8)], axis=0)
     rhs = flat_of(moved_by(own, slots_ref[...], ((1,), (0,))))
     rhs_ref[...] = rhs
-    share = share_of(rhs, (held_ref, held_other_ref))
+    share = share_of(rhs, (held0_ref, held1_ref, held2_ref))
     for place in range(share_ref.shape[0]):
         share_ref[place] = share
 
@@ -345,7 +346,7 @@
 
 
 def second_kernel(
-    n_narrow, packed_ref, slots_ref, rhs_ref, parts_ref, own_ref, other_ref, first_ref, share_ref
+    n_narrow, packed_ref, slots_ref, rhs_ref, parts_ref, held0_ref, held1_ref, held2_ref, first_ref, share_ref
 ):
     first = summed(parts_ref)
     first_ref[...] = first
@@ -377,7 +378,7 @@
         [jnp.sum(packed_ref[a * SLOT : (a + 1) * SLOT, :] * near, axis=0, keepdims=True) for a in range(8)], axis=0
     )
     vector = rhs_ref[...] - flat_of(moved_by(image, slots_ref[...], ((1,), (0,))))
-    share = share_of(vector, (own_ref, other_ref))
+    share = share_of(vector, (held0_ref, held1_ref, held2_ref))
     for place in range(share_ref.shape[0]):
         share_ref[place] = share
 
@@ -498,7 +499,8 @@
         moved=1_000_000,
         name="inner",
     )(own_matrix, x_matrix, zf, stiffness, mass, xlo, xhi, table)
-    rows_z = joined(rows_z, lambda k: k + 2 if k // 2 % 2 else k - 2)
+    far_z = lax.ppermute(rows_z, "z", [(k, (k + 2 if k // 2 % 2 else k - 2) % size_z) for k in range(size_z)])
+    all_z = jnp.concatenate([rows_z, far_z], axis=0)
     table, payload = call(
         outer_kernel,
         [(8, 128), (n_near, 1, SLOT * vectors)],
@@ -522,7 +524,7 @@
     got = [got] + [lax.ppermute(got, "y", [(k, k ^ step) for k in range(size_y)]) for step in range(1, size_y)]
     got = jnp.stack(got)
     other = lax.ppermute(got, "core", [(0, 1), (1, 0)])
-    held = [rows_z, lax.ppermute(rows_z, "core", [(0, 1), (1, 0)])]
+    held = [rows_z, far_z, lax.ppermute(all_z, "core", [(0, 1), (1, 0)])]
     group = ("narrow", "y")
     members = lax.axis_size(group)
 
@@ -540,7 +542,7 @@
             flat,
             (members,) + flat,
         ],
-        [SMEM] * 2 + [VMEM] * 4,
+        [SMEM] * 2 + [VMEM] * 5,
         [pltpu.VMEM((count, SLOT * vectors), F32)],
         flops=2_000_000,
         moved=3_000_000,
@@ -549,7 +551,7 @@
     first, share = call(
         functools.partial(second_kernel, n_narrow),
         [flat, (members,) + flat],
-        [VMEM] * 6,
+        [VMEM] * 7,
         flops=2_000_000,
         moved=3_000_000,
         name="second",

time: 80.6 us -> 80.3 us (level)
  local copies, waits for them, and re-layouts: 2.46 us -> 1.5 us
  waiting for transfers between devices: 14.9 us -> 15.8 us
    ppermute x1 -> x2, starting transfers between devices: 0.09 us -> 3.85 us  [the longest x1 3.76 us: body(): lax.ppermute(rows_z, 'z', [(k, (k + 2 if k // 2 % 2 else k - 2) % size_z)...]
    ppermute x3 -> x2, starting transfers between devices: 9.1 us -> 5.36 us  [joined(): lax.ppermute(rows, 'z', [(k, partner(k) % size_z) for k in range(size_z)])]
    concatenate x1, local copies, waits for them, and re-layouts: 0.97 us -> 0.01 us  [joined(): jnp.concatenate([rows, lax.ppermute(rows, 'z', [(k, partner(k) % size_z)...]
    ppermute x3, waiting for transfers between devices: 3.79 us -> 4.72 us  [body(): lax.ppermute(got, 'y', [(k, k ^ step) for k in range(size_y)])]
    ppermute x3 -> x2, waiting for transfers between devices: 2.29 us -> 2.28 us  [joined(): lax.ppermute(rows, 'z', [(k, partner(k) % size_z) for k in range(size_z)])]
  transfers between devices with their start and end apart: 13 -> 13, of which waited for: 5 -> 5; matrix products, arithmetic and copies ran while one was open for 5% -> 4% of each run, Pallas kernels for 9% -> 9%
where the time goes in v6:
time: 80.3 us; the launch traced here: 79.9 us
  starting transfers between devices  26.2 us (33%)
  blocking collectives  23.2 us (29%)
  waiting for transfers between devices  15.8 us (20%)
  Pallas kernels  10.8 us (13%)
  local copies, waits for them, and re-layouts  1.5 us (2%)
  other arithmetic  1.4 us (2%)
  between operations  0.99 us (1%)
    all_to_all x2, blocking collectives, spread(): return lax.all_to_all(share, group, 0, 0)  23.2 us
    all_to_all x1, starting transfers between devices, body(): got = lax.all_to_all(payload, ('narrow', 'z'), 0, 0)  7.37 us
    all_to_all x1, waiting for transfers between devices, body(): got = lax.all_to_all(payload, ('narrow', 'z'), 0, 0)  7.14 us
    ppermute x2, starting transfers between devices, joined(): lax.ppermute(rows, 'z', [(k, partner(k) % size_z) for k in range(size_z)])  5.36 us
    ppermute x3, waiting for transfers between devices, body(): lax.ppermute(got, 'y', [(k, k ^ step) for k in range(size_y)])  4.72 us
    ppermute x2, starting transfers between devices, exchanged(): two = lax.ppermute(chosen(sending_low, sending_high), axis, odd)  4.7 us
    ppermute x3, starting transfers between devices, body(): lax.ppermute(got, 'y', [(k, k ^ step) for k in range(size_y)])  4.09 us
    ppermute x1, starting transfers between devices, body(): lax.ppermute(rows_z, 'z', [(k, (k + 2 if k // 2 % 2 else k - 2) % size_z)...  3.76 us
  transfers between devices with their start and end apart: 13, of which 5 were waited for; matrix products, arithmetic and copies ran while one was open for 4% of the time, Pallas kernels for 9%

profile of v6, /device:TPU:2, one launch (start us, length us, event | category | flops | bytes accessed | tf_op | source)
XLA Modules:
  0.0 79.9 jit_solution(1884598990514848454)
XLA Ops:
  0.7 0.0 copy-start.7
  0.7 0.0 copy-start.2
  0.7 2.0 %collective-permute-start.8 = (f32[8,2048]{1,0:T(8,128)}, f32[8,2048]{1,0:T(8,128)S(1)}, u32[]{:S(2)}, u32[]{:S(2)}) collective-permute-start(f32[8,2048]{1,0:T(8,128)} %param.15), channel_id=1, source_target_pairs={{0,2},{2,0},{4,6},{6,4},{8,10},{10,8},{12,14},{14,12},{1,3},{3,1},... | collective-permute-start | bytes 196616 | tf_op jit(solution)/shard_map/ppermute | solution.py:479
  2.7 1.0 %copy.20 = bf16[8,3,4,8,256]{4,3,1,0,2:T(8,128)(2,1)S(1)} copy(bf16[8,3,4,8,256]{4,3,2,1,0:T(8,128)(2,1)} %z_ref.3) | data formatting | bytes 786432 | tf_op args[0]
  3.7 0.8 select_bitcast_fusion.2
  4.5 0.7 collective-permute-start
  5.2 4.0 %collective-permute-start.1 = (bf16[27,8,256]{2,1,0:T(8,128)(2,1)S(1)}, bf16[27,8,256]{2,1,0:T(8,128)(2,1)S(1)}, u32[]{:S(2)}, u32[]{:S(2)}) collective-permute-start(bf16[27,8,256]{2,1,0:T(8,128)(2,1)S(1)} %pad_maximum_fusion.4), channel_id=1, source_target_pairs={{64,128},{128,64},{65,129},{129,65},{66,130},{130,66},{67,131},{13... | collective-permute-start | bytes 331784 | tf_op jit(solution)/shard_map/ppermute | solution.py:451
  9.3 0.0 copy-start.3
  9.3 0.1 fusion
  9.4 0.1 copy_bitcast_fusion
  9.6 1.4 %before.1 = (f32[8,3,4,8,256]{4,3,2,1,0:T(8,128)S(1)}, f32[2,8,3,8,256]{4,3,2,1,0:T(8,128)S(1)}, f32[2,8,256]{2,1,0:T(8,128)S(1)}, f32[8,128]{1,0:T(8,128)S(1)},...) custom-call(f32[3,3,27]{2,1,0:T(4,128)S(1)} %bitcast.31, s32[9]{0:T(128)S(1)} %bitcast.32, ...), custom_call_target="tpu_custom_call" | custom-call | flops 20000000 | bytes 1000000 | tf_op jit(solution)/shard_map/before/pallas_call | solution.py:461
  11.1 0.0 collective-permute-done.8
  11.1 3.4 %collective-permute-start.9 = (f32[16,2048]{1,0:T(8,128)S(1)}, f32[16,2048]{1,0:T(8,128)S(1)}, u32[]{:S(2)}, u32[]{:S(2)}) collective-permute-start(f32[16,2048]{1,0:T(8,128)S(1)} %pad_maximum_fusion.2), channel_id=1, source_target_pairs={{0,4},{2,6},{4,0},{6,2},{8,12},{10,14},{12,8},{14,10},{1,5},{3,7},... | collective-permute-start | bytes 393224 | tf_op jit(solution)/shard_map/ppermute | solution.py:479
  14.5 0.0 collective-permute-done
  14.5 0.0 collective-permute-done.1
  14.5 0.1 fusion.1
  14.6 0.2 broadcast_select_fusion.2
  14.8 0.1 collective-permute-start.3
  14.9 0.7 collective-permute-start.2
  15.6 0.0 copy-start.8
  15.6 0.0 copy-start.1
  15.6 1.9 %inner.1.table_ref = f32[8,128]{1,0:T(8,128)S(1)} custom-call(bf16[288,256]{1,0:T(8,128)(2,1)S(1)} %get-tuple-element.28.own_ref, bf16[144,256]{1,0:T(8,128)(2,1)S(1)} %get-tuple-element.29.x_ref, f32[8,3,4,8,256]{4,3,2,1,0:T(8,128)S(1)} %get-tuple-element.30.zf_ref, f32[4,8,256]{2,1,0:T(8,128)S(1)} %copy-done.2, f32[4,8,256]{2,1,0:T(8,128)S(1)} %copy-done.3, ...), custom_call_target="tpu_custom_call" | custom-call | flops 10000000 | bytes 1000000 | tf_op jit(solution)/shard_map/inner/pallas_call | solution.py:493
  17.5 2.3 %collective-permute-done.9 = f32[16,2048]{1,0:T(8,128)S(1)} collective-permute-done((f32[16,2048]{1,0:T(8,128)S(1)}, f32[16,2048]{1,0:T(8,128)S(1)}, u32[]{:S(2)}, u32[]{:S(2)}) %collective-permute-start.9) | collective-permute-done | bytes 131104 | tf_op jit(solution)/shard_map/ppermute | solution.py:479
  19.7 3.8 %collective-permute-start.10 = (f32[32,2048]{1,0:T(8,128)S(1)}, f32[32,2048]{1,0:T(8,128)S(1)}, u32[]{:S(2)}, u32[]{:S(2)}) collective-permute-start(f32[32,2048]{1,0:T(8,128)S(1)} %constant_dynamic-update-slice_fusion.held0_ref), channel_id=1, source_target_pairs={{0,12},{2,14},{4,8},{6,10},{8,4},{10,6},{12,0},{14,2},{1,13},{3,15... | collective-permute-start | bytes 786440 | tf_op jit(solution)/shard_map/ppermute | solution.py:502
  23.5 0.0 collective-permute-done.3
  23.5 0.0 collective-permute-done.2
  23.5 2.0 %outer.1 = (f32[8,128]{1,0:T(8,128)S(1)}, f32[32,1,640]{2,1,0:T(1,128)}) custom-call(bf16[288,256]{1,0:T(8,128)(2,1)S(1)} %get-tuple-element.27.y_ref, f32[8,128]{1,0:T(8,128)S(1)} %inner.1.table_ref, f32[2,8,3,8,256]{4,3,2,1,0:T(8,128)S(1)} %get-tuple-element.35.zy_ref, f32[2,8,256]{2,1,0:T(8,128)S(1)} %get-tuple-element.36.sy_ref, ...), custom_call_target="tpu_custom_call" | custom-call | flops 10000000 | bytes 2000000 | tf_op jit(solution)/shard_map/outer/pallas_call | solution.py:504
  25.6 7.4 %all-to-all-start = ((f32[32,1,640]{2,1,0:T(1,128)}), f32[32,1,640]{2,1,0:T(1,128)S(1)}, u32[]{:S(2)}, u32[]{:S(2)}) async-start(f32[32,1,640]{2,1,0:T(1,128)} %get-tuple-element.37), calls=%async_computation | async-start | bytes 163840 | tf_op jit(solution)/shard_map/all_to_all | solution.py:513
  33.0 0.1 reshape.37.range_ref
  33.0 1.7 %local.1 = (f32[3,4,8,256]{3,2,1,0:T(8,128)S(1)}, f32[8,8,9]{2,1,0:T(8,128)}) custom-call(s32[4]{0:T(128)S(1)} %reshape.37.range_ref, bf16[12,12,5,3,256]{4,3,2,1,0:T(4,128)(2,1)S(1)} %bitcast.30, bf16[3,4,8,256]{3,2,1,0:T(8,128)(2,1)S(1)} %copy.19.r_ref, bf16[27,8,256]{2,1,0:T(8,128)(2,1)S(1)} %get-tuple-element.60.xlo_ref, ...), custom_call_target="tpu_custom_call" | custom-call | flops 2000000 | bytes 3000000 | tf_op jit(solution)/shard_map/local/pallas_call | solution.py:514
  34.7 7.1 %all-to-all-done = f32[32,1,640]{2,1,0:T(1,128)S(1)} async-done(((f32[32,1,640]{2,1,0:T(1,128)}), f32[32,1,640]{2,1,0:T(1,128)S(1)}, u32[]{:S(2)}, u32[]{:S(2)}) %all-to-all-start) | async-done | bytes 81952 | tf_op jit(solution)/shard_map/all_to_all | solution.py:513
  41.9 3.0 %collective-permute-start.6 = (f32[32,1,640]{2,1,0:T(1,128)S(1)}, f32[32,1,640]{2,1,0:T(1,128)S(1)}, u32[]{:S(2)}, u32[]{:S(2)}) collective-permute-start(f32[32,1,640]{2,1,0:T(1,128)S(1)} %all-to-all-done), channel_id=1, source_target_pairs={{0,48},{16,32},{32,16},{48,0},{1,49},{17,33},{33,17},{49,1},{2,50}... | collective-permute-start | bytes 245768 | tf_op jit(solution)/shard_map/ppermute | solution.py:524
  44.9 0.6 collective-permute-start.5
  45.5 0.4 collective-permute-start.4
  45.9 0.0 collective-permute-done.10.held1_ref
  46.0 0.1 collective-permute-start.11
  46.1 2.3 %collective-permute-done.6 = f32[32,1,640]{2,1,0:T(1,128)S(1)} collective-permute-done((f32[32,1,640]{2,1,0:T(1,128)S(1)}, f32[32,1,640]{2,1,0:T(1,128)S(1)}, u32[]{:S(2)}, u32[]{:S(2)}) %collective-permute-start.6) | collective-permute-done | bytes 81952 | tf_op jit(solution)/shard_map/ppermute | solution.py:524
  48.4 2.4 %collective-permute-done.5 = f32[32,1,640]{2,1,0:T(1,128)S(1)} collective-permute-done((f32[32,1,640]{2,1,0:T(1,128)S(1)}, f32[32,1,640]{2,1,0:T(1,128)S(1)}, u32[]{:S(2)}, u32[]{:S(2)}) %collective-permute-start.5) | collective-permute-done | bytes 81952 | tf_op jit(solution)/shard_map/ppermute | solution.py:524
  50.8 0.0 collective-permute-done.4
  50.8 0.3 pad_maximum_fusion.1.own_ref
  51.1 0.1 collective-permute-start.7
  51.2 1.6 %collective-permute-done.7.other_ref = f32[4,32,1,640]{3,2,1,0:T(1,128)S(1)} collective-permute-done((f32[4,32,1,640]{3,2,1,0:T(1,128)S(1)}, f32[4,32,1,640]{3,2,1,0:T(1,128)S(1)}, u32[]{:S(2)}, u32[]{:S(2)}) %collective-permute-start.7) | collective-permute-done | bytes 327712 | tf_op jit(solution)/shard_map/ppermute | solution.py:526
  52.8 0.0 collective-permute-done.11.held2_ref
  52.8 1.0 %first.1 = (f32[640,256]{1,0:T(8,128)S(1)}, bf16[256,2048]{1,0:T(8,128)(2,1)S(1)}, f32[16,128]{1,0:T(8,128)S(1)}, f32[16,16,128]{2,1,0:T(8,128)S(1)}) custom-call(s32[1]{0:T(128)} %bitcast.12.row_ref, s32[1]{0:T(128)} %bitcast.13.core_ref, f32[4,32,1,640]{3,2,1,0:T(1,128)S(1)} %pad_maximum_fusion.1.own_ref, ...), custom_call_target="tpu_custom_call" | custom-call | flops 2000000 | bytes 3000000 | tf_op jit(solution)/shard_map/first/pallas_call | solution.py:537
  53.9 12.0 %all_to_all.15.parts_ref = f32[16,16,128]{2,1,0:T(8,128)S(1)} all-to-all(f32[16,16,128]{2,1,0:T(8,128)S(1)} %get-tuple-element.45), channel_id=1, replica_groups=mesh['narrow'=4,'y'=4,'z'=8,'core'=2] {'narrow','y'}, dimensions={0} | all-to-all | bytes 262144 | tf_op jit(solution)/shard_map/all_to_all | solution.py:532
  65.9 1.4 %second.1 = (f32[16,128]{1,0:T(8,128)S(1)}, f32[16,16,128]{2,1,0:T(8,128)S(1)}) custom-call(f32[640,256]{1,0:T(8,128)S(1)} %get-tuple-element.42.packed_ref, bf16[256,2048]{1,0:T(8,128)(2,1)S(1)} %get-tuple-element.43.slots_ref, f32[16,128]{1,0:T(8,128)S(1)} %get-tuple-element.44.rhs_ref, f32[16,16,128]{2,1,0:T(8,128)S(1)} %all_to_all.15.parts_ref, ...), custom_call_target="tpu_custom_call" | custom-call | flops 2000000 | bytes 3000000 | tf_op jit(solution)/shard_map/second/pallas_call | solution.py:551
  67.3 11.2 %all_to_all.16.parts_ref = f32[16,16,128]{2,1,0:T(8,128)S(1)} all-to-all(f32[16,16,128]{2,1,0:T(8,128)S(1)} %get-tuple-element.47), channel_id=1, replica_groups=mesh['narrow'=4,'y'=4,'z'=8,'core'=2] {'narrow','y'}, dimensions={0} | all-to-all | bytes 262144 | tf_op jit(solution)/shard_map/all_to_all | solution.py:532
  78.5 1.4 %last.1 = (f32[3,4,8,256]{3,2,1,0:T(8,128)}, f32[16,128]{1,0:T(8,128)}) custom-call(s32[9]{0:T(128)S(1)} %bitcast.33, bf16[8,3,4,8,256]{4,3,2,1,0:T(8,128)(2,1)S(1)} %copy-done, f32[3,4,8,256]{3,2,1,0:T(8,128)S(1)} %get-tuple-element.40.local_ref, f32[16,128]{1,0:T(8,128)S(1)} %get-tuple-element.46.first_ref, f32[16,16,128]{2,1,0:T(8,128)S(1)} %all_to_all.16.parts_ref), custom_call_target="tpu_custom_call" | custom-call | flops 1000000 | bytes 1000000 | tf_op jit(solution)/shard_map/last/pallas_call | solution.py:559
  (27 shorter events, 0.2 us)
Async XLA Ops:
  0.6 8.6 %copy-start.6 = (f32[8,2048]{1,0:T(8,128)S(1)}, f32[8,2048]{1,0:T(8,128)}, u32[]{:S(2)}) copy-start(f32[8,2048]{1,0:T(8,128)} %param.15) | copy-start | bytes 196612
  0.6 9.0 %copy-start = (bf16[8,3,4,8,256]{4,3,2,1,0:T(8,128)(2,1)S(1)}, bf16[8,3,4,8,256]{4,3,2,1,0:T(8,128)(2,1)}, u32[]{:S(2)}) copy-start(bf16[8,3,4,8,256]{4,3,2,1,0:T(8,128)(2,1)} %z_ref.3) | copy-start | bytes 1179652
  0.7 8.6 %copy-start.7 = (f32[3,4,8,256]{3,2,1,0:T(8,128)S(1)}, f32[3,4,8,256]{3,2,1,0:T(8,128)}, u32[]{:S(2)}) copy-start(f32[3,4,8,256]{3,2,1,0:T(8,128)} %param.10) | copy-start | bytes 294916
  0.7 9.0 %copy-start.2 = (f32[4,8,256]{2,1,0:T(8,128)S(1)}, f32[4,8,256]{2,1,0:T(8,128)}, u32[]{:S(2)}) copy-start(f32[4,8,256]{2,1,0:T(8,128)} %stiff_ref.3) | copy-start | bytes 98308
  0.7 9.0 %copy-start.5 = (s32[1,1,9]{2,1,0:T(1,128)S(1)}, s32[1,1,9]{2,1,0:T(1,128)}, u32[]{:S(2)}) copy-start(s32[1,1,9]{2,1,0:T(1,128)} %param.17) | copy-start | bytes 112
  0.7 9.0 %copy-start.4 = (f32[27,3,3]{0,2,1:T(4,128)S(1)}, f32[27,3,3]{0,2,1:T(4,128)}, u32[]{:S(2)}) copy-start(f32[27,3,3]{0,2,1:T(4,128)} %param.13) | copy-start | bytes 2920
  0.7 10.4 %collective-permute-start.8 = (f32[8,2048]{1,0:T(8,128)}, f32[8,2048]{1,0:T(8,128)S(1)}, u32[]{:S(2)}, u32[]{:S(2)}) collective-permute-start(f32[8,2048]{1,0:T(8,128)} %param.15), channel_id=1, source_target_pairs={{0,2},{2,0},{4,6},{6,4},{8,10},{10,8},{12,14},{14,12},{1,3},{3,1},... | collective-permute-start | bytes 196616 | tf_op jit(solution)/shard_map/ppermute | solution.py:479
  4.5 9.9 %collective-permute-start = (bf16[27,8,256]{2,1,0:T(8,128)(2,1)S(1)}, bf16[27,8,256]{2,1,0:T(8,128)(2,1)S(1)}, u32[]{:S(2)}, u32[]{:S(2)}) collective-permute-start(bf16[27,8,256]{2,1,0:T(8,128)(2,1)S(1)} %pad_maximum_fusion.3), channel_id=1, source_target_pairs={{0,64},{64,0},{128,192},{192,128},{1,65},{65,1},{129,193},{193,129... | collective-permute-start | bytes 331784 | tf_op jit(solution)/shard_map/ppermute | solution.py:450
  5.2 9.3 %collective-permute-start.1 = (bf16[27,8,256]{2,1,0:T(8,128)(2,1)S(1)}, bf16[27,8,256]{2,1,0:T(8,128)(2,1)S(1)}, u32[]{:S(2)}, u32[]{:S(2)}) collective-permute-start(bf16[27,8,256]{2,1,0:T(8,128)(2,1)S(1)} %pad_maximum_fusion.4), channel_id=1, source_target_pairs={{64,128},{128,64},{65,129},{129,65},{66,130},{130,66},{67,131},{13... | collective-permute-start | bytes 331784 | tf_op jit(solution)/shard_map/ppermute | solution.py:451
  9.3 6.3 %copy-start.3 = (f32[4,8,256]{2,1,0:T(8,128)S(1)}, f32[4,8,256]{2,1,0:T(8,128)}, u32[]{:S(2)}) copy-start(f32[4,8,256]{2,1,0:T(8,128)} %mass_ref.1) | copy-start | bytes 98308
  11.1 8.6 %collective-permute-start.9 = (f32[16,2048]{1,0:T(8,128)S(1)}, f32[16,2048]{1,0:T(8,128)S(1)}, u32[]{:S(2)}, u32[]{:S(2)}) collective-permute-start(f32[16,2048]{1,0:T(8,128)S(1)} %pad_maximum_fusion.2), channel_id=1, source_target_pairs={{0,4},{2,6},{4,0},{6,2},{8,12},{10,14},{12,8},{14,10},{1,5},{3,7},... | collective-permute-start | bytes 393224 | tf_op jit(solution)/shard_map/ppermute | solution.py:479
  14.8 8.7 %collective-permute-start.3 = (bf16[27,6,256]{2,1,0:T(8,128)(2,1)S(1)}, bf16[27,6,256]{2,1,0:T(8,128)(2,1)S(1)}, u32[]{:S(2)}, u32[]{:S(2)}) collective-permute-start(bf16[27,6,256]{2,1,0:T(8,128)(2,1)S(1)} %get-tuple-element.57), channel_id=1, source_target_pairs={{0,1},{1,0},{2,3},{3,2},{4,5},{5,4},{6,7},{7,6},{8,9},{9,8},{10,11... | collective-permute-start | bytes 248840 | tf_op jit(solution)/shard_map/ppermute | solution.py:450
  14.9 8.6 %collective-permute-start.2 = (bf16[27,6,256]{2,1,0:T(8,128)(2,1)S(1)}, bf16[27,6,256]{2,1,0:T(8,128)(2,1)S(1)}, u32[]{:S(2)}, u32[]{:S(2)}) collective-permute-start(bf16[27,6,256]{2,1,0:T(8,128)(2,1)S(1)} %get-tuple-element.58), channel_id=1, source_target_pairs={{1,2},{2,1},{3,4},{4,3},{5,6},{6,5},{7,8},{8,7},{9,10},{10,9},{11,... | collective-permute-start | bytes 248840 | tf_op jit(solution)/shard_map/ppermute | solution.py:451
  15.6 17.4 %copy-start.8 = (s32[1,1,2,2]{3,2,1,0:T(2,128)S(1)}, s32[1,1,2,2]{3,2,1,0:T(2,128)}, u32[]{:S(2)}) copy-start(s32[1,1,2,2]{3,2,1,0:T(2,128)} %param.16) | copy-start | bytes 52
  15.6 17.5 %copy-start.1 = (bf16[12,12,3,5,256]{4,2,3,1,0:T(4,128)(2,1)S(1)}, bf16[12,12,3,5,256]{4,2,3,1,0:T(4,128)(2,1)}, u32[]{:S(2)}) copy-start(bf16[12,12,3,5,256]{4,2,3,1,0:T(4,128)(2,1)} %param.14) | copy-start | bytes 3317764
  19.7 26.2 %collective-permute-start.10 = (f32[32,2048]{1,0:T(8,128)S(1)}, f32[32,2048]{1,0:T(8,128)S(1)}, u32[]{:S(2)}, u32[]{:S(2)}) collective-permute-start(f32[32,2048]{1,0:T(8,128)S(1)} %constant_dynamic-update-slice_fusion.held0_ref), channel_id=1, source_target_pairs={{0,12},{2,14},{4,8},{6,10},{8,4},{10,6},{12,0},{14,2},{1,13},{3,15... | collective-permute-start | bytes 786440 | tf_op jit(solution)/shard_map/ppermute | solution.py:502
  25.6 16.3 %all-to-all-start = ((f32[32,1,640]{2,1,0:T(1,128)}), f32[32,1,640]{2,1,0:T(1,128)S(1)}, u32[]{:S(2)}, u32[]{:S(2)}) async-start(f32[32,1,640]{2,1,0:T(1,128)} %get-tuple-element.37), calls=%async_computation | async-start | bytes 163840 | tf_op jit(solution)/shard_map/all_to_all | solution.py:513
  41.9 6.5 %collective-permute-start.6 = (f32[32,1,640]{2,1,0:T(1,128)S(1)}, f32[32,1,640]{2,1,0:T(1,128)S(1)}, u32[]{:S(2)}, u32[]{:S(2)}) collective-permute-start(f32[32,1,640]{2,1,0:T(1,128)S(1)} %all-to-all-done), channel_id=1, source_target_pairs={{0,48},{16,32},{32,16},{48,0},{1,49},{17,33},{33,17},{49,1},{2,50}... | collective-permute-start | bytes 245768 | tf_op jit(solution)/shard_map/ppermute | solution.py:524
  44.9 5.9 %collective-permute-start.5 = (f32[32,1,640]{2,1,0:T(1,128)S(1)}, f32[32,1,640]{2,1,0:T(1,128)S(1)}, u32[]{:S(2)}, u32[]{:S(2)}) collective-permute-start(f32[32,1,640]{2,1,0:T(1,128)S(1)} %all-to-all-done), channel_id=1, source_target_pairs={{0,32},{16,48},{32,0},{48,16},{1,33},{17,49},{33,1},{49,17},{2,34}... | collective-permute-start | bytes 245768 | tf_op jit(solution)/shard_map/ppermute | solution.py:524
  45.5 5.3 %collective-permute-start.4 = (f32[32,1,640]{2,1,0:T(1,128)S(1)}, f32[32,1,640]{2,1,0:T(1,128)S(1)}, u32[]{:S(2)}, u32[]{:S(2)}) collective-permute-start(f32[32,1,640]{2,1,0:T(1,128)S(1)} %all-to-all-done), channel_id=1, source_target_pairs={{0,16},{16,0},{32,48},{48,32},{1,17},{17,1},{33,49},{49,33},{2,18}... | collective-permute-start | bytes 245768 | tf_op jit(solution)/shard_map/ppermute | solution.py:524
  46.0 6.8 %collective-permute-start.11 = (f32[64,2048]{1,0:T(8,128)S(1)}, f32[64,2048]{1,0:T(8,128)S(1)}, u32[]{:S(2)}, u32[]{:S(2)}) collective-permute-start(f32[64,2048]{1,0:T(8,128)S(1)} %pad_maximum_fusion), channel_id=1, source_target_pairs={{0,1},{1,0},{2,3},{3,2},{4,5},{5,4},{6,7},{7,6},{8,9},{9,8},{10,11... | collective-permute-start | bytes 1572872 | tf_op jit(solution)/shard_map/ppermute | solution.py:527
  51.1 1.7 %collective-permute-start.7 = (f32[4,32,1,640]{3,2,1,0:T(1,128)S(1)}, f32[4,32,1,640]{3,2,1,0:T(1,128)S(1)}, u32[]{:S(2)}, u32[]{:S(2)}) collective-permute-start(f32[4,32,1,640]{3,2,1,0:T(1,128)S(1)} %pad_maximum_fusion.1.own_ref), channel_id=1, source_target_pairs={{0,1},{1,0},{2,3},{3,2},{4,5},{5,4},{6,7},{7,6},{8,9},{9,8},{10,11... | collective-permute-start | bytes 983048 | tf_op jit(solution)/shard_map/ppermute | solution.py:526

commit v7 on v6

--- a/solution.py
+++ b/solution.py
@@ -307,7 +307,7 @@
                 acc = acc + tile * value
             return acc
 
-        acc = lax.fori_loop(0, piece.shape[0] // 8 // group, step, acc)
+        acc = lax.fori_loop(0, piece.shape[0] // 8 // group, step, acc, unroll=True)
     return folded(jnp.sum(acc, axis=0, keepdims=True))
 
 

time: 80.3 us -> 79.9 us (level)
  no operation moved by 1% of the time
where the time goes in v7:
time: 79.9 us; the launch traced here: 79.5 us
  starting transfers between devices  26.2 us (33%)
  blocking collectives  23.2 us (29%)
  waiting for transfers between devices  15.8 us (20%)
  Pallas kernels  10.4 us (13%)
  local copies, waits for them, and re-layouts  1.5 us (2%)
  other arithmetic  1.4 us (2%)
  between operations  1 us (1%)
    all_to_all x2, blocking collectives, spread(): return lax.all_to_all(share, group, 0, 0)  23.2 us
    all_to_all x1, starting transfers between devices, body(): got = lax.all_to_all(payload, ('narrow', 'z'), 0, 0)  7.37 us
    all_to_all x1, waiting for transfers between devices, body(): got = lax.all_to_all(payload, ('narrow', 'z'), 0, 0)  7.14 us
    ppermute x2, starting transfers between devices, joined(): lax.ppermute(rows, 'z', [(k, partner(k) % size_z) for k in range(size_z)])  5.36 us
    ppermute x3, waiting for transfers between devices, body(): lax.ppermute(got, 'y', [(k, k ^ step) for k in range(size_y)])  4.72 us
    ppermute x2, starting transfers between devices, exchanged(): two = lax.ppermute(chosen(sending_low, sending_high), axis, odd)  4.7 us
    ppermute x3, starting transfers between devices, body(): lax.ppermute(got, 'y', [(k, k ^ step) for k in range(size_y)])  4.09 us
    ppermute x1, starting transfers between devices, body(): lax.ppermute(rows_z, 'z', [(k, (k + 2 if k // 2 % 2 else k - 2) % size_z)...  3.76 us
  transfers between devices with their start and end apart: 13, of which 5 were waited for; matrix products, arithmetic and copies ran while one was open for 4% of the time, Pallas kernels for 9%

profile of v7, /device:TPU:2, one launch (start us, length us, event | category | flops | bytes accessed | tf_op | source)
XLA Modules:
  0.0 79.5 jit_solution(5039732073987078562)
XLA Ops:
  0.7 0.0 copy-start.7
  0.7 0.0 copy-start.2
  0.7 2.0 %collective-permute-start.8 = (f32[8,2048]{1,0:T(8,128)}, f32[8,2048]{1,0:T(8,128)S(1)}, u32[]{:S(2)}, u32[]{:S(2)}) collective-permute-start(f32[8,2048]{1,0:T(8,128)} %param.15), channel_id=1, source_target_pairs={{0,2},{2,0},{4,6},{6,4},{8,10},{10,8},{12,14},{14,12},{1,3},{3,1},... | collective-permute-start | bytes 196616 | tf_op jit(solution)/shard_map/ppermute | solution.py:479
  2.7 1.0 %copy.20 = bf16[8,3,4,8,256]{4,3,1,0,2:T(8,128)(2,1)S(1)} copy(bf16[8,3,4,8,256]{4,3,2,1,0:T(8,128)(2,1)} %z_ref.3) | data formatting | bytes 786432 | tf_op args[0]
  3.7 0.8 select_bitcast_fusion.2
  4.5 0.7 collective-permute-start
  5.2 4.0 %collective-permute-start.1 = (bf16[27,8,256]{2,1,0:T(8,128)(2,1)S(1)}, bf16[27,8,256]{2,1,0:T(8,128)(2,1)S(1)}, u32[]{:S(2)}, u32[]{:S(2)}) collective-permute-start(bf16[27,8,256]{2,1,0:T(8,128)(2,1)S(1)} %pad_maximum_fusion.4), channel_id=1, source_target_pairs={{64,128},{128,64},{65,129},{129,65},{66,130},{130,66},{67,131},{13... | collective-permute-start | bytes 331784 | tf_op jit(solution)/shard_map/ppermute | solution.py:451
  9.3 0.0 copy-start.3
  9.3 0.1 fusion
  9.4 0.1 copy_bitcast_fusion
  9.6 1.4 %before.1 = (f32[8,3,4,8,256]{4,3,2,1,0:T(8,128)S(1)}, f32[2,8,3,8,256]{4,3,2,1,0:T(8,128)S(1)}, f32[2,8,256]{2,1,0:T(8,128)S(1)}, f32[8,128]{1,0:T(8,128)S(1)},...) custom-call(f32[3,3,27]{2,1,0:T(4,128)S(1)} %bitcast.31, s32[9]{0:T(128)S(1)} %bitcast.32, ...), custom_call_target="tpu_custom_call" | custom-call | flops 20000000 | bytes 1000000 | tf_op jit(solution)/shard_map/before/pallas_call | solution.py:461
  11.1 0.0 collective-permute-done.8
  11.1 3.4 %collective-permute-start.9 = (f32[16,2048]{1,0:T(8,128)S(1)}, f32[16,2048]{1,0:T(8,128)S(1)}, u32[]{:S(2)}, u32[]{:S(2)}) collective-permute-start(f32[16,2048]{1,0:T(8,128)S(1)} %pad_maximum_fusion.2), channel_id=1, source_target_pairs={{0,4},{2,6},{4,0},{6,2},{8,12},{10,14},{12,8},{14,10},{1,5},{3,7},... | collective-permute-start | bytes 393224 | tf_op jit(solution)/shard_map/ppermute | solution.py:479
  14.5 0.0 collective-permute-done
  14.5 0.0 collective-permute-done.1
  14.5 0.1 fusion.1
  14.6 0.2 broadcast_select_fusion.2
  14.8 0.1 collective-permute-start.3
  14.9 0.7 collective-permute-start.2
  15.6 0.0 copy-start.8
  15.6 0.0 copy-start.1
  15.6 1.9 %inner.1.table_ref = f32[8,128]{1,0:T(8,128)S(1)} custom-call(bf16[288,256]{1,0:T(8,128)(2,1)S(1)} %get-tuple-element.28.own_ref, bf16[144,256]{1,0:T(8,128)(2,1)S(1)} %get-tuple-element.29.x_ref, f32[8,3,4,8,256]{4,3,2,1,0:T(8,128)S(1)} %get-tuple-element.30.zf_ref, f32[4,8,256]{2,1,0:T(8,128)S(1)} %copy-done.2, f32[4,8,256]{2,1,0:T(8,128)S(1)} %copy-done.3, ...), custom_call_target="tpu_custom_call" | custom-call | flops 10000000 | bytes 1000000 | tf_op jit(solution)/shard_map/inner/pallas_call | solution.py:493
  17.5 2.3 %collective-permute-done.9 = f32[16,2048]{1,0:T(8,128)S(1)} collective-permute-done((f32[16,2048]{1,0:T(8,128)S(1)}, f32[16,2048]{1,0:T(8,128)S(1)}, u32[]{:S(2)}, u32[]{:S(2)}) %collective-permute-start.9) | collective-permute-done | bytes 131104 | tf_op jit(solution)/shard_map/ppermute | solution.py:479
  19.7 3.8 %collective-permute-start.10 = (f32[32,2048]{1,0:T(8,128)S(1)}, f32[32,2048]{1,0:T(8,128)S(1)}, u32[]{:S(2)}, u32[]{:S(2)}) collective-permute-start(f32[32,2048]{1,0:T(8,128)S(1)} %constant_dynamic-update-slice_fusion.held0_ref), channel_id=1, source_target_pairs={{0,12},{2,14},{4,8},{6,10},{8,4},{10,6},{12,0},{14,2},{1,13},{3,15... | collective-permute-start | bytes 786440 | tf_op jit(solution)/shard_map/ppermute | solution.py:502
  23.5 0.0 collective-permute-done.3
  23.5 0.0 collective-permute-done.2
  23.5 2.0 %outer.1 = (f32[8,128]{1,0:T(8,128)S(1)}, f32[32,1,640]{2,1,0:T(1,128)}) custom-call(bf16[288,256]{1,0:T(8,128)(2,1)S(1)} %get-tuple-element.27.y_ref, f32[8,128]{1,0:T(8,128)S(1)} %inner.1.table_ref, f32[2,8,3,8,256]{4,3,2,1,0:T(8,128)S(1)} %get-tuple-element.35.zy_ref, f32[2,8,256]{2,1,0:T(8,128)S(1)} %get-tuple-element.36.sy_ref, ...), custom_call_target="tpu_custom_call" | custom-call | flops 10000000 | bytes 2000000 | tf_op jit(solution)/shard_map/outer/pallas_call | solution.py:504
  25.6 7.4 %all-to-all-start = ((f32[32,1,640]{2,1,0:T(1,128)}), f32[32,1,640]{2,1,0:T(1,128)S(1)}, u32[]{:S(2)}, u32[]{:S(2)}) async-start(f32[32,1,640]{2,1,0:T(1,128)} %get-tuple-element.37), calls=%async_computation | async-start | bytes 163840 | tf_op jit(solution)/shard_map/all_to_all | solution.py:513
  33.0 0.1 reshape.37.range_ref
  33.0 1.7 %local.1 = (f32[3,4,8,256]{3,2,1,0:T(8,128)S(1)}, f32[8,8,9]{2,1,0:T(8,128)}) custom-call(s32[4]{0:T(128)S(1)} %reshape.37.range_ref, bf16[12,12,5,3,256]{4,3,2,1,0:T(4,128)(2,1)S(1)} %bitcast.30, bf16[3,4,8,256]{3,2,1,0:T(8,128)(2,1)S(1)} %copy.19.r_ref, bf16[27,8,256]{2,1,0:T(8,128)(2,1)S(1)} %get-tuple-element.60.xlo_ref, ...), custom_call_target="tpu_custom_call" | custom-call | flops 2000000 | bytes 3000000 | tf_op jit(solution)/shard_map/local/pallas_call | solution.py:514
  34.7 7.1 %all-to-all-done = f32[32,1,640]{2,1,0:T(1,128)S(1)} async-done(((f32[32,1,640]{2,1,0:T(1,128)}), f32[32,1,640]{2,1,0:T(1,128)S(1)}, u32[]{:S(2)}, u32[]{:S(2)}) %all-to-all-start) | async-done | bytes 81952 | tf_op jit(solution)/shard_map/all_to_all | solution.py:513
  41.9 3.0 %collective-permute-start.6 = (f32[32,1,640]{2,1,0:T(1,128)S(1)}, f32[32,1,640]{2,1,0:T(1,128)S(1)}, u32[]{:S(2)}, u32[]{:S(2)}) collective-permute-start(f32[32,1,640]{2,1,0:T(1,128)S(1)} %all-to-all-done), channel_id=1, source_target_pairs={{0,48},{16,32},{32,16},{48,0},{1,49},{17,33},{33,17},{49,1},{2,50}... | collective-permute-start | bytes 245768 | tf_op jit(solution)/shard_map/ppermute | solution.py:524
  44.9 0.6 collective-permute-start.5
  45.5 0.4 collective-permute-start.4
  45.9 0.0 collective-permute-done.10.held1_ref
  46.0 0.1 collective-permute-start.11
  46.1 2.3 %collective-permute-done.6 = f32[32,1,640]{2,1,0:T(1,128)S(1)} collective-permute-done((f32[32,1,640]{2,1,0:T(1,128)S(1)}, f32[32,1,640]{2,1,0:T(1,128)S(1)}, u32[]{:S(2)}, u32[]{:S(2)}) %collective-permute-start.6) | collective-permute-done | bytes 81952 | tf_op jit(solution)/shard_map/ppermute | solution.py:524
  48.4 2.4 %collective-permute-done.5 = f32[32,1,640]{2,1,0:T(1,128)S(1)} collective-permute-done((f32[32,1,640]{2,1,0:T(1,128)S(1)}, f32[32,1,640]{2,1,0:T(1,128)S(1)}, u32[]{:S(2)}, u32[]{:S(2)}) %collective-permute-start.5) | collective-permute-done | bytes 81952 | tf_op jit(solution)/shard_map/ppermute | solution.py:524
  50.8 0.0 collective-permute-done.4
  50.8 0.3 pad_maximum_fusion.1.own_ref
  51.1 0.1 collective-permute-start.7
  51.2 1.6 %collective-permute-done.7.other_ref = f32[4,32,1,640]{3,2,1,0:T(1,128)S(1)} collective-permute-done((f32[4,32,1,640]{3,2,1,0:T(1,128)S(1)}, f32[4,32,1,640]{3,2,1,0:T(1,128)S(1)}, u32[]{:S(2)}, u32[]{:S(2)}) %collective-permute-start.7) | collective-permute-done | bytes 327712 | tf_op jit(solution)/shard_map/ppermute | solution.py:526
  52.8 0.0 collective-permute-done.11.held2_ref
  52.8 0.8 %first.1 = (f32[640,256]{1,0:T(8,128)S(1)}, bf16[256,2048]{1,0:T(8,128)(2,1)S(1)}, f32[16,128]{1,0:T(8,128)S(1)}, f32[16,16,128]{2,1,0:T(8,128)S(1)}) custom-call(s32[1]{0:T(128)} %bitcast.12.row_ref, s32[1]{0:T(128)} %bitcast.13.core_ref, f32[4,32,1,640]{3,2,1,0:T(1,128)S(1)} %pad_maximum_fusion.1.own_ref, ...), custom_call_target="tpu_custom_call" | custom-call | flops 2000000 | bytes 3000000 | tf_op jit(solution)/shard_map/first/pallas_call | solution.py:537
  53.7 12.0 %all_to_all.15.parts_ref = f32[16,16,128]{2,1,0:T(8,128)S(1)} all-to-all(f32[16,16,128]{2,1,0:T(8,128)S(1)} %get-tuple-element.45), channel_id=1, replica_groups=mesh['narrow'=4,'y'=4,'z'=8,'core'=2] {'narrow','y'}, dimensions={0} | all-to-all | bytes 262144 | tf_op jit(solution)/shard_map/all_to_all | solution.py:532
  65.7 1.2 %second.1 = (f32[16,128]{1,0:T(8,128)S(1)}, f32[16,16,128]{2,1,0:T(8,128)S(1)}) custom-call(f32[640,256]{1,0:T(8,128)S(1)} %get-tuple-element.42.packed_ref, bf16[256,2048]{1,0:T(8,128)(2,1)S(1)} %get-tuple-element.43.slots_ref, f32[16,128]{1,0:T(8,128)S(1)} %get-tuple-element.44.rhs_ref, f32[16,16,128]{2,1,0:T(8,128)S(1)} %all_to_all.15.parts_ref, ...), custom_call_target="tpu_custom_call" | custom-call | flops 2000000 | bytes 3000000 | tf_op jit(solution)/shard_map/second/pallas_call | solution.py:551
  66.9 11.2 %all_to_all.16.parts_ref = f32[16,16,128]{2,1,0:T(8,128)S(1)} all-to-all(f32[16,16,128]{2,1,0:T(8,128)S(1)} %get-tuple-element.47), channel_id=1, replica_groups=mesh['narrow'=4,'y'=4,'z'=8,'core'=2] {'narrow','y'}, dimensions={0} | all-to-all | bytes 262144 | tf_op jit(solution)/shard_map/all_to_all | solution.py:532
  78.1 1.4 %last.1 = (f32[3,4,8,256]{3,2,1,0:T(8,128)}, f32[16,128]{1,0:T(8,128)}) custom-call(s32[9]{0:T(128)S(1)} %bitcast.33, bf16[8,3,4,8,256]{4,3,2,1,0:T(8,128)(2,1)S(1)} %copy-done, f32[3,4,8,256]{3,2,1,0:T(8,128)S(1)} %get-tuple-element.40.local_ref, f32[16,128]{1,0:T(8,128)S(1)} %get-tuple-element.46.first_ref, f32[16,16,128]{2,1,0:T(8,128)S(1)} %all_to_all.16.parts_ref), custom_call_target="tpu_custom_call" | custom-call | flops 1000000 | bytes 1000000 | tf_op jit(solution)/shard_map/last/pallas_call | solution.py:559
  (27 shorter events, 0.2 us)
Async XLA Ops:
  0.6 8.6 %copy-start.6 = (f32[8,2048]{1,0:T(8,128)S(1)}, f32[8,2048]{1,0:T(8,128)}, u32[]{:S(2)}) copy-start(f32[8,2048]{1,0:T(8,128)} %param.15) | copy-start | bytes 196612
  0.6 9.0 %copy-start = (bf16[8,3,4,8,256]{4,3,2,1,0:T(8,128)(2,1)S(1)}, bf16[8,3,4,8,256]{4,3,2,1,0:T(8,128)(2,1)}, u32[]{:S(2)}) copy-start(bf16[8,3,4,8,256]{4,3,2,1,0:T(8,128)(2,1)} %z_ref.3) | copy-start | bytes 1179652
  0.7 8.6 %copy-start.7 = (f32[3,4,8,256]{3,2,1,0:T(8,128)S(1)}, f32[3,4,8,256]{3,2,1,0:T(8,128)}, u32[]{:S(2)}) copy-start(f32[3,4,8,256]{3,2,1,0:T(8,128)} %param.10) | copy-start | bytes 294916
  0.7 9.0 %copy-start.2 = (f32[4,8,256]{2,1,0:T(8,128)S(1)}, f32[4,8,256]{2,1,0:T(8,128)}, u32[]{:S(2)}) copy-start(f32[4,8,256]{2,1,0:T(8,128)} %stiff_ref.3) | copy-start | bytes 98308
  0.7 9.0 %copy-start.5 = (s32[1,1,9]{2,1,0:T(1,128)S(1)}, s32[1,1,9]{2,1,0:T(1,128)}, u32[]{:S(2)}) copy-start(s32[1,1,9]{2,1,0:T(1,128)} %param.17) | copy-start | bytes 112
  0.7 9.0 %copy-start.4 = (f32[27,3,3]{0,2,1:T(4,128)S(1)}, f32[27,3,3]{0,2,1:T(4,128)}, u32[]{:S(2)}) copy-start(f32[27,3,3]{0,2,1:T(4,128)} %param.13) | copy-start | bytes 2920
  0.7 10.4 %collective-permute-start.8 = (f32[8,2048]{1,0:T(8,128)}, f32[8,2048]{1,0:T(8,128)S(1)}, u32[]{:S(2)}, u32[]{:S(2)}) collective-permute-start(f32[8,2048]{1,0:T(8,128)} %param.15), channel_id=1, source_target_pairs={{0,2},{2,0},{4,6},{6,4},{8,10},{10,8},{12,14},{14,12},{1,3},{3,1},... | collective-permute-start | bytes 196616 | tf_op jit(solution)/shard_map/ppermute | solution.py:479
  4.5 9.9 %collective-permute-start = (bf16[27,8,256]{2,1,0:T(8,128)(2,1)S(1)}, bf16[27,8,256]{2,1,0:T(8,128)(2,1)S(1)}, u32[]{:S(2)}, u32[]{:S(2)}) collective-permute-start(bf16[27,8,256]{2,1,0:T(8,128)(2,1)S(1)} %pad_maximum_fusion.3), channel_id=1, source_target_pairs={{0,64},{64,0},{128,192},{192,128},{1,65},{65,1},{129,193},{193,129... | collective-permute-start | bytes 331784 | tf_op jit(solution)/shard_map/ppermute | solution.py:450
  5.2 9.3 %collective-permute-start.1 = (bf16[27,8,256]{2,1,0:T(8,128)(2,1)S(1)}, bf16[27,8,256]{2,1,0:T(8,128)(2,1)S(1)}, u32[]{:S(2)}, u32[]{:S(2)}) collective-permute-start(bf16[27,8,256]{2,1,0:T(8,128)(2,1)S(1)} %pad_maximum_fusion.4), channel_id=1, source_target_pairs={{64,128},{128,64},{65,129},{129,65},{66,130},{130,66},{67,131},{13... | collective-permute-start | bytes 331784 | tf_op jit(solution)/shard_map/ppermute | solution.py:451
  9.3 6.3 %copy-start.3 = (f32[4,8,256]{2,1,0:T(8,128)S(1)}, f32[4,8,256]{2,1,0:T(8,128)}, u32[]{:S(2)}) copy-start(f32[4,8,256]{2,1,0:T(8,128)} %mass_ref.1) | copy-start | bytes 98308
  11.1 8.6 %collective-permute-start.9 = (f32[16,2048]{1,0:T(8,128)S(1)}, f32[16,2048]{1,0:T(8,128)S(1)}, u32[]{:S(2)}, u32[]{:S(2)}) collective-permute-start(f32[16,2048]{1,0:T(8,128)S(1)} %pad_maximum_fusion.2), channel_id=1, source_target_pairs={{0,4},{2,6},{4,0},{6,2},{8,12},{10,14},{12,8},{14,10},{1,5},{3,7},... | collective-permute-start | bytes 393224 | tf_op jit(solution)/shard_map/ppermute | solution.py:479
  14.8 8.7 %collective-permute-start.3 = (bf16[27,6,256]{2,1,0:T(8,128)(2,1)S(1)}, bf16[27,6,256]{2,1,0:T(8,128)(2,1)S(1)}, u32[]{:S(2)}, u32[]{:S(2)}) collective-permute-start(bf16[27,6,256]{2,1,0:T(8,128)(2,1)S(1)} %get-tuple-element.57), channel_id=1, source_target_pairs={{0,1},{1,0},{2,3},{3,2},{4,5},{5,4},{6,7},{7,6},{8,9},{9,8},{10,11... | collective-permute-start | bytes 248840 | tf_op jit(solution)/shard_map/ppermute | solution.py:450
  14.9 8.6 %collective-permute-start.2 = (bf16[27,6,256]{2,1,0:T(8,128)(2,1)S(1)}, bf16[27,6,256]{2,1,0:T(8,128)(2,1)S(1)}, u32[]{:S(2)}, u32[]{:S(2)}) collective-permute-start(bf16[27,6,256]{2,1,0:T(8,128)(2,1)S(1)} %get-tuple-element.58), channel_id=1, source_target_pairs={{1,2},{2,1},{3,4},{4,3},{5,6},{6,5},{7,8},{8,7},{9,10},{10,9},{11,... | collective-permute-start | bytes 248840 | tf_op jit(solution)/shard_map/ppermute | solution.py:451
  15.6 17.4 %copy-start.8 = (s32[1,1,2,2]{3,2,1,0:T(2,128)S(1)}, s32[1,1,2,2]{3,2,1,0:T(2,128)}, u32[]{:S(2)}) copy-start(s32[1,1,2,2]{3,2,1,0:T(2,128)} %param.16) | copy-start | bytes 52
  15.6 17.5 %copy-start.1 = (bf16[12,12,3,5,256]{4,2,3,1,0:T(4,128)(2,1)S(1)}, bf16[12,12,3,5,256]{4,2,3,1,0:T(4,128)(2,1)}, u32[]{:S(2)}) copy-start(bf16[12,12,3,5,256]{4,2,3,1,0:T(4,128)(2,1)} %param.14) | copy-start | bytes 3317764
  19.7 26.2 %collective-permute-start.10 = (f32[32,2048]{1,0:T(8,128)S(1)}, f32[32,2048]{1,0:T(8,128)S(1)}, u32[]{:S(2)}, u32[]{:S(2)}) collective-permute-start(f32[32,2048]{1,0:T(8,128)S(1)} %constant_dynamic-update-slice_fusion.held0_ref), channel_id=1, source_target_pairs={{0,12},{2,14},{4,8},{6,10},{8,4},{10,6},{12,0},{14,2},{1,13},{3,15... | collective-permute-start | bytes 786440 | tf_op jit(solution)/shard_map/ppermute | solution.py:502
  25.6 16.3 %all-to-all-start = ((f32[32,1,640]{2,1,0:T(1,128)}), f32[32,1,640]{2,1,0:T(1,128)S(1)}, u32[]{:S(2)}, u32[]{:S(2)}) async-start(f32[32,1,640]{2,1,0:T(1,128)} %get-tuple-element.37), calls=%async_computation | async-start | bytes 163840 | tf_op jit(solution)/shard_map/all_to_all | solution.py:513
  41.9 6.5 %collective-permute-start.6 = (f32[32,1,640]{2,1,0:T(1,128)S(1)}, f32[32,1,640]{2,1,0:T(1,128)S(1)}, u32[]{:S(2)}, u32[]{:S(2)}) collective-permute-start(f32[32,1,640]{2,1,0:T(1,128)S(1)} %all-to-all-done), channel_id=1, source_target_pairs={{0,48},{16,32},{32,16},{48,0},{1,49},{17,33},{33,17},{49,1},{2,50}... | collective-permute-start | bytes 245768 | tf_op jit(solution)/shard_map/ppermute | solution.py:524
  44.9 5.9 %collective-permute-start.5 = (f32[32,1,640]{2,1,0:T(1,128)S(1)}, f32[32,1,640]{2,1,0:T(1,128)S(1)}, u32[]{:S(2)}, u32[]{:S(2)}) collective-permute-start(f32[32,1,640]{2,1,0:T(1,128)S(1)} %all-to-all-done), channel_id=1, source_target_pairs={{0,32},{16,48},{32,0},{48,16},{1,33},{17,49},{33,1},{49,17},{2,34}... | collective-permute-start | bytes 245768 | tf_op jit(solution)/shard_map/ppermute | solution.py:524
  45.5 5.3 %collective-permute-start.4 = (f32[32,1,640]{2,1,0:T(1,128)S(1)}, f32[32,1,640]{2,1,0:T(1,128)S(1)}, u32[]{:S(2)}, u32[]{:S(2)}) collective-permute-start(f32[32,1,640]{2,1,0:T(1,128)S(1)} %all-to-all-done), channel_id=1, source_target_pairs={{0,16},{16,0},{32,48},{48,32},{1,17},{17,1},{33,49},{49,33},{2,18}... | collective-permute-start | bytes 245768 | tf_op jit(solution)/shard_map/ppermute | solution.py:524
  46.0 6.8 %collective-permute-start.11 = (f32[64,2048]{1,0:T(8,128)S(1)}, f32[64,2048]{1,0:T(8,128)S(1)}, u32[]{:S(2)}, u32[]{:S(2)}) collective-permute-start(f32[64,2048]{1,0:T(8,128)S(1)} %pad_maximum_fusion), channel_id=1, source_target_pairs={{0,1},{1,0},{2,3},{3,2},{4,5},{5,4},{6,7},{7,6},{8,9},{9,8},{10,11... | collective-permute-start | bytes 1572872 | tf_op jit(solution)/shard_map/ppermute | solution.py:527
  51.1 1.7 %collective-permute-start.7 = (f32[4,32,1,640]{3,2,1,0:T(1,128)S(1)}, f32[4,32,1,640]{3,2,1,0:T(1,128)S(1)}, u32[]{:S(2)}, u32[]{:S(2)}) collective-permute-start(f32[4,32,1,640]{3,2,1,0:T(1,128)S(1)} %pad_maximum_fusion.1.own_ref), channel_id=1, source_target_pairs={{0,1},{1,0},{2,3},{3,2},{4,5},{5,4},{6,7},{7,6},{8,9},{9,8},{10,11... | collective-permute-start | bytes 983048 | tf_op jit(solution)/shard_map/ppermute | solution.py:526
